TPU v7x, 512 devices: a whole 4x4x16 slice. The times are simulated.
512 devices in a mesh: expert: 32 (over z, core), dp: 16 (over x, y).
Axes of the slice: x: 4, y: 4, z: 16, core: 2. Of those that a mesh axis runs over, the one named last changes fastest.
Arguments:
- tokens: bfloat16 [8192, 7168], P('expert', 'dp'), may hold values from -6 to 6
- cotangent: bfloat16 [8192, 7168], P('expert', 'dp'), may hold values from -6 to 6
- gate_weight: bfloat16 [32, 7168, 1024], P('expert', 'dp'), may hold values from -0.0625 to 0.0625
- up_weight: bfloat16 [32, 7168, 1024], P('expert', 'dp'), may hold values from -0.0625 to 0.0625
- down_weight: bfloat16 [32, 1024, 7168], P('expert', None, 'dp'), may hold values from -0.1875 to 0.1875
- expert_ids: int32 [8192, 8], P('expert'), may hold values from 0 to 255, all different within a row; in each aligned block of 256 rows (0 to 255, 256 to 511, ...) at most 16 rows name the same one
- gate_values: float32 [8192, 8], P('expert'), may hold values from 0.05 to 0.5
Outputs:
- token_grad: bfloat16 [8192, 7168], P('expert', 'dp')
- gate_grad: bfloat16 [32, 7168, 1024], P('expert', 'dp')
- up_grad: bfloat16 [32, 7168, 1024], P('expert', 'dp')
Inputs may be any that keep to these rules, and one draw needn't show every extreme that they name: `expert_ids`: each row names 8 different experts. Among the 256 rows of one index of expert no expert is named more than 16 times, and in every draw some expert is named exactly 16 times there; loads are skewed.
All inputs are finite; a program needn't handle non-finite values.
Results may differ from a plain program's by a relative error of at most 0.0058.
Values may be sent and summed in bfloat16 or wider, within the bound.
No kernel may reach another device: no remote copies, remote signals or barrier semaphores. Data moves between devices by JAX's collectives and lax.ppermute only.
A program may use at most 64 MiB of HBM per device.

v0:
```python
import jax
import jax.numpy as jnp
from jax import lax
from jax.sharding import PartitionSpec as P

CAP = 16


def route_tables(expert_ids, gate_values, held, capacity):
    tok_rows, top_count = expert_ids.shape
    flat_ids = expert_ids.reshape(-1)
    onehot = (flat_ids[:, None] == jnp.arange(held, dtype=jnp.int32)[None, :]).astype(jnp.int32)
    before = jnp.cumsum(onehot, axis=0) - onehot
    rank = jnp.sum(before * onehot, axis=1)
    inside = flat_ids < held
    target = jnp.where(inside, flat_ids * capacity + rank, -1)
    placed = jnp.arange(held * capacity, dtype=jnp.int32)[:, None] == target[None, :]
    placed = placed.reshape(held * capacity, tok_rows, top_count)
    member = jnp.sum(placed.astype(jnp.float32), axis=2)
    weighted = jnp.sum(jnp.where(placed, gate_values[None, :, :], 0.0), axis=2)
    return (member, weighted)


def local_grads(gate_act, up_act, back_act):
    sig = jax.nn.sigmoid(gate_act)
    grad_gate = (back_act * up_act * sig * (1.0 + gate_act * (1.0 - sig))).astype(jnp.bfloat16)
    grad_up = (back_act * gate_act * sig).astype(jnp.bfloat16)
    return (grad_gate, grad_up)


def body(tokens, cotangent, gate_weight, up_weight, down_weight, expert_ids, gate_values):
    held = lax.axis_size("expert")
    capacity = CAP
    width = tokens.shape[1]
    member, weighted = route_tables(expert_ids, gate_values, held, capacity)
    member_bf = member.astype(jnp.bfloat16)
    send_rows = jnp.dot(member_bf, tokens, preferred_element_type=jnp.float32).astype(jnp.bfloat16)
    slot_gate = jnp.sum(weighted, axis=1)
    picked = jnp.dot(member_bf, cotangent, preferred_element_type=jnp.float32)
    send_grads = (slot_gate[:, None] * picked).astype(jnp.bfloat16)
    recv_rows, recv_grads = (
        lax.all_to_all(
            send_rows.reshape(held, capacity, width),
            "expert",
            split_axis=0,
            concat_axis=0,
            tiled=True,
        ),
        lax.all_to_all(
            send_grads.reshape(held, capacity, width),
            "expert",
            split_axis=0,
            concat_axis=0,
            tiled=True,
        ),
    )
    recv_rows = recv_rows.reshape(held * capacity, width)
    recv_grads = recv_grads.reshape(held * capacity, width)
    gate_w = gate_weight[0]
    up_w = up_weight[0]
    down_w = down_weight[0]
    part_gate = jnp.dot(recv_rows, gate_w, preferred_element_type=jnp.float32)
    part_up = jnp.dot(recv_rows, up_w, preferred_element_type=jnp.float32)
    part_back = lax.dot_general(
        recv_grads, down_w, (((1,), (1,)), ((), ())), preferred_element_type=jnp.float32
    )
    gate_act, up_act, back_act = lax.psum((part_gate, part_up, part_back), "dp")
    grad_gate, grad_up = local_grads(gate_act, up_act, back_act)
    gate_grad = lax.dot_general(
        recv_rows, grad_gate, (((0,), (0,)), ((), ())), preferred_element_type=jnp.float32
    ).astype(jnp.bfloat16)
    up_grad = lax.dot_general(
        recv_rows, grad_up, (((0,), (0,)), ((), ())), preferred_element_type=jnp.float32
    ).astype(jnp.bfloat16)
    row_grads = (
        lax.dot_general(
            grad_gate, gate_w, (((1,), (1,)), ((), ())), preferred_element_type=jnp.float32
        )
        + lax.dot_general(
            grad_up, up_w, (((1,), (1,)), ((), ())), preferred_element_type=jnp.float32
        )
    ).astype(jnp.bfloat16)
    returned = lax.all_to_all(
        row_grads.reshape(held, capacity, width), "expert", split_axis=0, concat_axis=0, tiled=True
    )
    returned = returned.reshape(held * capacity, width)
    token_grad = lax.dot_general(
        member_bf, returned, (((0,), (0,)), ((), ())), preferred_element_type=jnp.float32
    ).astype(jnp.bfloat16)
    return (token_grad, gate_grad[None], up_grad[None])


def solution(mesh):
    placed = (
        P("expert", "dp"),
        P("expert", "dp"),
        P("expert", "dp", None),
        P("expert", "dp", None),
        P("expert", None, "dp"),
        P("expert", None),
        P("expert", None),
    )
    return jax.shard_map(
        body,
        mesh=mesh,
        in_specs=placed,
        out_specs=(P("expert", "dp"), P("expert", "dp", None), P("expert", "dp", None)),
        check_vma=False,
    )
```

profile of v0, /device:TPU:1, one launch (start us, length us, event | category | flops | bytes accessed | tf_op | source)
XLA Modules:
  0.0 318.5 jit_solution(8350088931126968813)
XLA Ops:
  7.2 0.0 copy-start
  7.2 0.0 copy-start.6
  7.2 0.0 copy-start.7
  7.2 0.0 copy-start.4
  7.2 0.9 copy.36
  8.1 0.1 eq.44
  8.2 0.1 eq.40
  8.4 9.1 %reduce-window.6 = s32[32,16,128]{2,1,0:T(8,128)S(1)} reduce-window(s32[32,16,128]{2,1,0:T(8,128)S(1)} %fusion.16, s32[]{:T(128)} %constant.4.clone.1), window={size=1x1x128 pad=0_0x0_0x127_0}, to_apply=%region_0.0 | reduce-window | flops 8323072 | bytes 524292 | tf_op jit(solution)/shard_map/reduce-window
  17.5 0.1 slice.8
  17.6 0.2 copy.44
  17.8 0.2 reduce-window.9
  18.0 0.0 copy-start.5
  18.0 0.1 broadcast_add_fusion
  18.2 0.1 fusion.15
  18.3 0.1 reduce_sum.34
  18.4 0.1 copy.40
  18.5 0.0 copy-done.6
  18.5 0.0 copy-done.7
  18.5 2.1 select_reduce_fusion
  20.6 0.0 copy-done.4
  20.6 0.3 convolution_convert_fusion.2
  20.9 1.0 copy.42
  21.9 16.8 %all-to-all-start.1 = ((bf16[32,16,448]{2,1,0:T(8,128)(2,1)}), bf16[32,16,448]{2,1,0:T(8,128)(2,1)S(1)}, u32[]{:S(2)}, u32[]{:S(2)}) async-start(bf16[32,16,448]{2,1,0:T(8,128)(2,1)} %bitcast.6), calls=%async_computation.1 | async-start | bytes 1048576 | tf_op jit(solution)/shard_map/all_to_all | solution.py:42
  38.6 0.0 copy-done.5
  38.7 0.3 fusion.3
  39.0 1.0 copy.41
  40.0 32.2 %all-to-all-done.1 = bf16[32,16,448]{2,1,0:T(8,128)(2,1)S(1)} async-done(((bf16[32,16,448]{2,1,0:T(8,128)(2,1)}), bf16[32,16,448]{2,1,0:T(8,128)(2,1)S(1)}, u32[]{:S(2)}, u32[]{:S(2)}) %all-to-all-start.1) | async-done | bytes 458784 | tf_op jit(solution)/shard_map/all_to_all | solution.py:42
  72.2 4.0 %all-to-all-start = ((bf16[32,16,448]{2,1,0:T(8,128)(2,1)}), bf16[32,16,448]{2,1,0:T(8,128)(2,1)S(1)}, u32[]{:S(2)}, u32[]{:S(2)}) async-start(bf16[32,16,448]{2,1,0:T(8,128)(2,1)} %bitcast.3), calls=%async_computation | async-start | bytes 1048576 | tf_op jit(solution)/shard_map/all_to_all | solution.py:49
  76.2 0.0 all-reduce.3.cloned.1.call-start
  76.2 0.0 copy-done
  76.3 2.1 fusion.6
  78.3 0.0 copy-start.2
  78.3 3.3 %fusion.9 = f32[512,1024]{1,0:T(8,128)} fusion(bf16[512,448]{1,0:T(8,128)(2,1)S(1)} %bitcast.59, bf16[1,448,1024]{2,1,0:T(8,128)(2,1)} %param.10), kind=kOutput, calls=%fused_computation.21 | convolution fusion | flops 469762048 | bytes 3473408 | tf_op jit(solution)/shard_map/dot_general | solution.py:63
  81.6 28.1 %all-to-all-done = bf16[32,16,448]{2,1,0:T(8,128)(2,1)S(1)} async-done(((bf16[32,16,448]{2,1,0:T(8,128)(2,1)}), bf16[32,16,448]{2,1,0:T(8,128)(2,1)S(1)}, u32[]{:S(2)}, u32[]{:S(2)}) %all-to-all-start) | async-done | bytes 458784 | tf_op jit(solution)/shard_map/all_to_all | solution.py:49
  109.7 0.0 copy-done.2
  109.7 2.1 fusion.11
  111.8 0.0 all-reduce.3.cloned.1.call-update
  111.8 144.9 %all-reduce.3.cloned.1.call-done = (f32[512,1024]{1,0:T(8,128)}, f32[512,1024]{1,0:T(8,128)}, f32[512,1024]{1,0:T(8,128)}) async-done(((f32[512,1024]{1,0:T(8,128)}, f32[512,1024]{1,0:T(8,128)}, f32[512,1024]{1,0:T(8,128)}), (f32[512,1024]{1,0:T(8,128)}, f32[512,1024]{1,0:T(8,128)}, f32[512,1024]{1,0:T(8,128)})) %all-reduce.3.cloned.1.call-update) | async-done | bytes 6291472 | tf_op jit(solution)/shard_map/psum | solution.py:67
  256.8 4.1 %multiply_convert_fusion = (bf16[512,1024]{1,0:T(8,128)(2,1)S(1)}, bf16[512,1024]{1,0:T(8,128)(2,1)S(1)}) fusion(f32[512,1024]{1,0:T(8,128)} %get-tuple-element.6, f32[512,1024]{1,0:T(8,128)} %get-tuple-element.5, f32[512,1024]{1,0:T(8,128)} %get-tuple-element.7), kind=kLoop, calls=%fused_computation.3 | loop fusion | flops 6815744 | bytes 8388608 | tf_op jit(solution)/shard_map/convert_element_type | solution.py:27
  260.9 0.0 copy-start.1
  260.9 0.0 copy-start.3
  260.9 0.7 fusion.4
  261.6 0.3 copy-done.1
  261.8 0.6 copy-done.3
  262.4 0.7 fusion.2
  263.1 1.0 copy.43
  264.1 13.0 %all-to-all-start.2 = ((bf16[32,16,448]{2,1,0:T(8,128)(2,1)}), bf16[32,16,448]{2,1,0:T(8,128)(2,1)S(1)}, u32[]{:S(2)}, u32[]{:S(2)}) async-start(bf16[32,16,448]{2,1,0:T(8,128)(2,1)} %bitcast.10), calls=%async_computation.2 | async-start | bytes 1048576 | tf_op jit(solution)/shard_map/all_to_all | solution.py:83
  277.1 2.8 fusion.1
  280.0 1.6 fusion
  281.5 29.1 %all-to-all-done.2 = bf16[32,16,448]{2,1,0:T(8,128)(2,1)S(1)} async-done(((bf16[32,16,448]{2,1,0:T(8,128)(2,1)}), bf16[32,16,448]{2,1,0:T(8,128)(2,1)S(1)}, u32[]{:S(2)}, u32[]{:S(2)}) %all-to-all-start.2) | async-done | bytes 458784 | tf_op jit(solution)/shard_map/all_to_all | solution.py:83
  310.7 1.0 convolution_convert_fusion.3
  (2 shorter events, 0.0 us)
Async XLA Ops:
  7.2 69.1 %copy-start = (bf16[1,448,1024]{2,1,0:T(8,128)(2,1)S(1)}, bf16[1,448,1024]{2,1,0:T(8,128)(2,1)}, u32[]{:S(2)}) copy-start(bf16[1,448,1024]{2,1,0:T(8,128)(2,1)} %param.9) | copy-start | bytes 2752516
  7.2 11.3 %copy-start.6 = (s32[256,8]{0,1:T(8,128)S(1)}, s32[256,8]{0,1:T(8,128)}, u32[]{:S(2)}) copy-start(s32[256,8]{0,1:T(8,128)} %param.12) | copy-start | bytes 24580
  7.2 11.3 %copy-start.7 = (f32[256,8]{0,1:T(8,128)S(1)}, f32[256,8]{0,1:T(8,128)}, u32[]{:S(2)}) copy-start(f32[256,8]{0,1:T(8,128)} %param.13) | copy-start | bytes 24580
  7.2 13.4 %copy-start.4 = (bf16[256,448]{0,1:T(8,128)(2,1)S(1)}, bf16[256,448]{0,1:T(8,128)(2,1)}, u32[]{:S(2)}) copy-start(bf16[256,448]{0,1:T(8,128)(2,1)} %param.7) | copy-start | bytes 688132
  18.0 20.6 %copy-start.5 = (bf16[256,448]{0,1:T(8,128)(2,1)S(1)}, bf16[256,448]{0,1:T(8,128)(2,1)}, u32[]{:S(2)}) copy-start(bf16[256,448]{0,1:T(8,128)(2,1)} %param.8) | copy-start | bytes 688132
  21.9 50.3 %all-to-all-start.1 = ((bf16[32,16,448]{2,1,0:T(8,128)(2,1)}), bf16[32,16,448]{2,1,0:T(8,128)(2,1)S(1)}, u32[]{:S(2)}, u32[]{:S(2)}) async-start(bf16[32,16,448]{2,1,0:T(8,128)(2,1)} %bitcast.6), calls=%async_computation.1 | async-start | bytes 1048576 | tf_op jit(solution)/shard_map/all_to_all | solution.py:42
  72.2 37.6 %all-to-all-start = ((bf16[32,16,448]{2,1,0:T(8,128)(2,1)}), bf16[32,16,448]{2,1,0:T(8,128)(2,1)S(1)}, u32[]{:S(2)}, u32[]{:S(2)}) async-start(bf16[32,16,448]{2,1,0:T(8,128)(2,1)} %bitcast.3), calls=%async_computation | async-start | bytes 1048576 | tf_op jit(solution)/shard_map/all_to_all | solution.py:49
  76.2 180.6 %all-reduce.3.cloned.1.call-start = ((), (), s32[]{:S(2)}) async-start(), calls=%async_computation.3 | async-start | bytes 12582912 | tf_op jit(solution)/shard_map/psum | solution.py:67
  78.3 31.4 %copy-start.2 = (bf16[1,1024,448]{1,2,0:T(8,128)(2,1)S(1)}, bf16[1,1024,448]{1,2,0:T(8,128)(2,1)}, u32[]{:S(2)}) copy-start(bf16[1,1024,448]{1,2,0:T(8,128)(2,1)} %param.11) | copy-start | bytes 2752516
  260.9 1.0 copy-start.1
  260.9 1.6 copy-start.3
  264.1 46.5 %all-to-all-start.2 = ((bf16[32,16,448]{2,1,0:T(8,128)(2,1)}), bf16[32,16,448]{2,1,0:T(8,128)(2,1)S(1)}, u32[]{:S(2)}, u32[]{:S(2)}) async-start(bf16[32,16,448]{2,1,0:T(8,128)(2,1)} %bitcast.10), calls=%async_computation.2 | async-start | bytes 1048576 | tf_op jit(solution)/shard_map/all_to_all | solution.py:83
Sparse Core Ops, SparseCore 0:
  112.0 144.7 all-reduce.2
where the time goes:
time: 319 us
  waiting for transfers between devices  234 us (73%)
  starting transfers between devices  33.8 us (11%)
  other arithmetic  15.7 us (5%)
  matrix products  14.8 us (5%)
  between operations  14.2 us (4%)
  local copies, waits for them, and re-layouts  5.58 us (2%)
    psum x1, waiting for transfers between devices, body(): gate_act, up_act, back_act = lax.psum((part_gate, part_up, part_back), 'dp')  145 us
    all_to_all x1, waiting for transfers between devices, body(): lax.all_to_all(send_rows.reshape(held, capacity, width), 'expert', split_...  32.2 us
    all_to_all x1, waiting for transfers between devices, body(): lax.all_to_all(row_grads.reshape(held, capacity, width), 'expert', split_...  29.1 us
    all_to_all x1, waiting for transfers between devices, body(): lax.all_to_all(send_grads.reshape(held, capacity, width), 'expert', split...  28.1 us
    all_to_all x1, starting transfers between devices, body(): lax.all_to_all(send_rows.reshape(held, capacity, width), 'expert', split_...  16.8 us
    all_to_all x1, starting transfers between devices, body(): lax.all_to_all(row_grads.reshape(held, capacity, width), 'expert', split_...  13 us
    another operation x3, other arithmetic  9.41 us
  transfers between devices with their start and end apart: 4, of which 4 were waited for; matrix products, arithmetic and copies ran while one was open for 3% of the time, Pallas kernels for 0%

commit v1 on v0

v1 whole, which is shorter than its diff:
```python
import jax
import jax.numpy as jnp
from jax import lax
from jax.experimental import pallas as pl
from jax.experimental.pallas import tpu as pltpu
from jax.sharding import PartitionSpec as P

CAP = 16
MIB = 1 << 20


def dispatch_kernel(ids_ref, gates_ref, tokens_ref, cotangent_ref, send_ref, member_ref, both):
    tok_rows, top_count = ids_ref.shape
    width = tokens_ref.shape[1]
    slots = send_ref.shape[0]
    held = slots // CAP
    ids = ids_ref[...]
    gates = gates_ref[...]
    lane = lax.broadcasted_iota(jnp.int32, (tok_rows, 128), 1)
    onehot = jnp.zeros((tok_rows, 128), jnp.float32)
    gate = jnp.zeros((tok_rows, 128), jnp.float32)
    for k in range(top_count):
        hit = ids[:, k : k + 1] == lane
        onehot = jnp.where(hit, 1.0, onehot)
        gate = jnp.where(hit, gates[:, k : k + 1], gate)
    named = onehot.T[:held]
    gate = gate.T[:held]
    earlier = lax.broadcasted_iota(jnp.int32, (tok_rows, tok_rows), 0) < lax.broadcasted_iota(
        jnp.int32, (tok_rows, tok_rows), 1
    )
    rank = jnp.dot(
        named.astype(jnp.bfloat16),
        jnp.where(earlier, 1.0, 0.0).astype(jnp.bfloat16),
        preferred_element_type=jnp.float32,
    )
    code = jnp.where(named > 0.0, rank, -1.0)

    def by_slot(table):
        return jnp.broadcast_to(table[:, None, :], (held, CAP, tok_rows)).reshape(slots, tok_rows)

    slot = (lax.broadcasted_iota(jnp.int32, (slots, tok_rows), 0) % CAP).astype(jnp.float32)
    placed = by_slot(code) == slot
    slot_gate = jnp.sum(jnp.where(placed, by_slot(gate), 0.0), axis=1, keepdims=True)
    member = jnp.where(placed, 1.0, 0.0).astype(jnp.bfloat16)
    member_ref[...] = member
    both[:, :width] = tokens_ref[...]
    both[:, width:] = cotangent_ref[...]
    picked = jnp.dot(member, both[...], preferred_element_type=jnp.float32)
    column = lax.broadcasted_iota(jnp.int32, picked.shape, 1)
    send_ref[...] = jnp.where(column < width, picked, picked * slot_gate).astype(jnp.bfloat16)


def partial_kernel(scale, recv_ref, gate_ref, up_ref, down_ref, out_ref):
    width = gate_ref.shape[0]
    parts, _, rows, cols = out_ref.shape
    x = recv_ref[:, :width]
    g = recv_ref[:, width:]

    def put(i, value):
        out_ref[:, i] = (value * scale).astype(out_ref.dtype).reshape(parts, rows, cols)

    put(0, jnp.dot(x, gate_ref[...], preferred_element_type=jnp.float32))
    put(1, jnp.dot(x, up_ref[...], preferred_element_type=jnp.float32))
    put(
        2,
        lax.dot_general(
            g, down_ref[...], (((1,), (1,)), ((), ())), preferred_element_type=jnp.float32
        ),
    )


def local_kernel(scale, parts_ref, out_ref):
    parts, _, rows, cols = parts_ref.shape

    def total(i):
        value = parts_ref[0, i].astype(jnp.float32)
        for p in range(1, parts):
            value = value + parts_ref[p, i].astype(jnp.float32)
        return value * scale

    gate_act, up_act, back_act = total(0), total(1), total(2)
    sig = 1.0 / (1.0 + jnp.exp(-gate_act))
    back_sig = back_act * sig
    grad_gate = (back_act * up_act * sig * (1.0 + gate_act * (1.0 - sig))).astype(jnp.bfloat16)
    grad_up = (back_act * gate_act * sig).astype(jnp.bfloat16)
    for p in range(out_ref.shape[0]):
        out_ref[p, 0] = grad_gate
        out_ref[p, 1] = grad_up


def body(tokens, cotangent, gate_weight, up_weight, down_weight, expert_ids, gate_values):
    held = lax.axis_size("expert")
    parts = lax.axis_size("dp")
    tok_rows, width = tokens.shape
    slots = held * CAP
    hidden = gate_weight.shape[2]
    gate_w = gate_weight[0]
    up_w = up_weight[0]
    down_w = down_weight[0]
    send, member = pl.pallas_call(
        dispatch_kernel,
        out_shape=(
            jax.ShapeDtypeStruct((slots, 2 * width), jnp.bfloat16),
            jax.ShapeDtypeStruct((slots, tok_rows), jnp.bfloat16),
        ),
        scratch_shapes=[pltpu.VMEM((tok_rows, 2 * width), jnp.bfloat16)],
        compiler_params=pltpu.CompilerParams(vmem_limit_bytes=32 * MIB),
        name="dispatch",
    )(expert_ids, gate_values, tokens, cotangent)
    recv = lax.all_to_all(
        send.reshape(held, CAP, 2 * width), "expert", split_axis=0, concat_axis=0, tiled=True
    ).reshape(slots, 2 * width)
    rows = slots // parts
    tile = 256
    sums = pl.pallas_call(
        lambda *refs: partial_kernel(1.0, *refs),
        grid=(hidden // tile,),
        in_specs=[
            pl.BlockSpec((slots, 2 * width), lambda i: (0, 0)),
            pl.BlockSpec((width, tile), lambda i: (0, i)),
            pl.BlockSpec((width, tile), lambda i: (0, i)),
            pl.BlockSpec((tile, width), lambda i: (i, 0)),
        ],
        out_specs=pl.BlockSpec((parts, 3, rows, tile), lambda i: (0, 0, 0, i)),
        out_shape=jax.ShapeDtypeStruct((parts, 3, rows, hidden), SENT),
        compiler_params=pltpu.CompilerParams(vmem_limit_bytes=32 * MIB),
        name="partials",
    )(recv, gate_w, up_w, down_w)
    sums = lax.all_to_all(sums, "dp", split_axis=0, concat_axis=0, tiled=True)
    grads = pl.pallas_call(
        lambda *refs: local_kernel(1.0, *refs),
        grid=(hidden // tile,),
        in_specs=[pl.BlockSpec((parts, 3, rows, tile), lambda i: (0, 0, 0, i))],
        out_specs=pl.BlockSpec((parts, 2, rows, tile), lambda i: (0, 0, 0, i)),
        out_shape=jax.ShapeDtypeStruct((parts, 2, rows, hidden), jnp.bfloat16),
        compiler_params=pltpu.CompilerParams(vmem_limit_bytes=32 * MIB),
        name="local_grads",
    )(sums)
    grads = lax.all_to_all(grads, "dp", split_axis=0, concat_axis=0, tiled=True)
    grad_gate = grads[:, 0].reshape(slots, hidden)
    grad_up = grads[:, 1].reshape(slots, hidden)
    row_grads = (
        lax.dot_general(
            grad_gate, gate_w, (((1,), (1,)), ((), ())), preferred_element_type=jnp.float32
        )
        + lax.dot_general(
            grad_up, up_w, (((1,), (1,)), ((), ())), preferred_element_type=jnp.float32
        )
    ).astype(jnp.bfloat16)
    returned = lax.all_to_all(
        row_grads.reshape(held, CAP, width), "expert", split_axis=0, concat_axis=0, tiled=True
    ).reshape(slots, width)
    recv_rows = recv[:, :width]
    gate_grad = lax.dot_general(
        recv_rows, grad_gate, (((0,), (0,)), ((), ())), preferred_element_type=jnp.float32
    ).astype(jnp.bfloat16)
    up_grad = lax.dot_general(
        recv_rows, grad_up, (((0,), (0,)), ((), ())), preferred_element_type=jnp.float32
    ).astype(jnp.bfloat16)
    token_grad = lax.dot_general(
        member, returned, (((0,), (0,)), ((), ())), preferred_element_type=jnp.float32
    ).astype(jnp.bfloat16)
    return (token_grad, gate_grad[None], up_grad[None])


SENT = jnp.bfloat16


def solution(mesh):
    placed = (
        P("expert", "dp"),
        P("expert", "dp"),
        P("expert", "dp", None),
        P("expert", "dp", None),
        P("expert", None, "dp"),
        P("expert", None),
        P("expert", None),
    )
    return jax.shard_map(
        body,
        mesh=mesh,
        in_specs=placed,
        out_specs=(P("expert", "dp"), P("expert", "dp", None), P("expert", "dp", None)),
        check_vma=False,
    )
```

time: 319 us -> 200 us (0.63)
  waiting for transfers between devices: 234 us -> 77.9 us
  blocking collectives: 0 us -> 75 us
  other arithmetic: 15.7 us -> 0 us
  between operations: 14.2 us -> 0.74 us
  starting transfers between devices: 33.8 us -> 23.6 us
  matrix products: 14.8 us -> 6.79 us
  Pallas kernels: 0 us -> 6.48 us
    psum x1 -> x0, waiting for transfers between devices: 145 us -> none  [body(): gate_act, up_act, back_act = lax.psum((part_gate, part_up, part_back), 'dp')]
    all_to_all x0 -> x2, blocking collectives: none -> 75 us  [the longest x1 44.7 us: body(): sums = lax.all_to_all(sums, 'dp', split_axis=0, concat_axis=0, tiled=True)]
    all_to_all x3 -> x2, waiting for transfers between devices: 89.4 us -> 77.9 us  [the longest x1 48.7 us: body(): lax.all_to_all(send.reshape(held, CAP, 2 * width), 'expert', split_axis=0...]
    all_to_all x3 -> x2, starting transfers between devices: 33.8 us -> 23.6 us  [the longest x1 16.9 us: body(): lax.all_to_all(send.reshape(held, CAP, 2 * width), 'expert', split_axis=0...]
    another operation x3 -> x0, other arithmetic: 9.41 us -> none
    dot_general x6 -> x1, matrix products: 9.05 us -> 1.03 us  [body(): lax.dot_general(member, returned, (((0,), (0,)), ((), ())), preferred_ele...]
    pallas_call x0 -> x3, Pallas kernels: none -> 6.48 us  [the longest x1 2.97 us: body(): pl.pallas_call(lambda *refs: partial_kernel(1.0, *refs), grid=(hidden //...]
    unnamed x17 -> x13, local copies, waits for them, and re-layouts: 1.82 us -> 7.31 us
  transfers between devices with their start and end apart: 4 -> 2, of which waited for: 4 -> 2; matrix products, arithmetic and copies ran while one was open for 3% -> 3% of each run, Pallas kernels for 0% -> 0%
where the time goes in v1:
time: 200 us; the launch traced here: 199 us
  waiting for transfers between devices  77.9 us (39%)
  blocking collectives  75 us (38%)
  starting transfers between devices  23.6 us (12%)
  local copies, waits for them, and re-layouts  8.53 us (4%)
  matrix products  6.79 us (3%)
  Pallas kernels  6.48 us (3%)
    all_to_all x1, waiting for transfers between devices, body(): lax.all_to_all(send.reshape(held, CAP, 2 * width), 'expert', split_axis=0...  48.7 us
    all_to_all x1, blocking collectives, body(): sums = lax.all_to_all(sums, 'dp', split_axis=0, concat_axis=0, tiled=True)  44.7 us
    all_to_all x1, blocking collectives, body(): grads = lax.all_to_all(grads, 'dp', split_axis=0, concat_axis=0, tiled=True)  30.3 us
    all_to_all x1, waiting for transfers between devices, body(): lax.all_to_all(row_grads.reshape(held, CAP, width), 'expert', split_axis=...  29.1 us
    all_to_all x1, starting transfers between devices, body(): lax.all_to_all(send.reshape(held, CAP, 2 * width), 'expert', split_axis=0...  16.9 us
    unnamed x13, local copies, waits for them, and re-layouts  7.31 us
    all_to_all x1, starting transfers between devices, body(): lax.all_to_all(row_grads.reshape(held, CAP, width), 'expert', split_axis=...  6.67 us
  transfers between devices with their start and end apart: 2, of which 2 were waited for; matrix products, arithmetic and copies ran while one was open for 3% of the time, Pallas kernels for 0%

profile of v1, /device:TPU:1, one launch (start us, length us, event | category | flops | bytes accessed | tf_op | source)
XLA Modules:
  0.0 199.0 jit_solution(9236686854042991017)
XLA Ops:
  0.6 0.8 copy.15.ids_ref
  1.5 0.8 copy.16.gates_ref
  2.3 1.1 copy.17.tokens_ref
  3.4 1.1 copy.18.cotangent_ref
  4.5 2.1 %dispatch.1 = (bf16[512,896]{1,0:T(8,128)(2,1)}, bf16[512,256]{1,0:T(8,128)(2,1)S(1)}) custom-call(s32[256,8]{1,0:T(8,128)S(1)} %copy.15.ids_ref, f32[256,8]{1,0:T(8,128)S(1)} %copy.16.gates_ref, bf16[256,448]{1,0:T(8,128)(2,1)S(1)} %copy.17.tokens_ref, bf16[256,448]{1,0:T(8,128)(2,1)S(1)} %copy.18.cotangent_ref), custom_call_target="tpu_custom_call" | custom-call | tf_op jit(solution)/shard_map/dispatch/pallas_call | solution.py:100
  6.6 0.0 copy-start
  6.6 16.9 %all-to-all-start = ((bf16[32,16,896]{2,1,0:T(8,128)(2,1)}), bf16[32,16,896]{2,1,0:T(8,128)(2,1)S(1)}, u32[]{:S(2)}, u32[]{:S(2)}) async-start(bf16[32,16,896]{2,1,0:T(8,128)(2,1)} %bitcast), calls=%async_computation | async-start | bytes 1835008 | tf_op jit(solution)/shard_map/all_to_all | solution.py:110
  23.5 1.5 copy.19
  25.0 48.7 %all-to-all-done = bf16[32,16,896]{2,1,0:T(8,128)(2,1)S(1)} async-done(((bf16[32,16,896]{2,1,0:T(8,128)(2,1)}), bf16[32,16,896]{2,1,0:T(8,128)(2,1)S(1)}, u32[]{:S(2)}, u32[]{:S(2)}) %all-to-all-start) | async-done | bytes 917536 | tf_op jit(solution)/shard_map/all_to_all | solution.py:110
  73.7 0.0 copy-done
  73.7 0.0 copy-start.1
  73.7 1.2 copy-done.1
  74.9 3.0 %partials.1 = bf16[16,3,32,1024]{3,2,1,0:T(8,128)(2,1)S(1)} custom-call(bf16[512,896]{1,0:T(8,128)(2,1)S(1)} %bitcast.24, bf16[448,1024]{1,0:T(8,128)(2,1)S(1)} %bitcast.27, bf16[448,1024]{1,0:T(8,128)(2,1)S(1)} %bitcast.28, bf16[1024,448]{1,0:T(8,128)(2,1)S(1)} %bitcast.23), custom_call_target="tpu_custom_call" | custom-call | tf_op jit(solution)/shard_map/partials/pallas_call | solution.py:115
  77.8 44.7 %all_to_all.20.refs_0_ = bf16[16,3,32,1024]{3,2,1,0:T(8,128)(2,1)S(1)} all-to-all(bf16[16,3,32,1024]{3,2,1,0:T(8,128)(2,1)S(1)} %partials.1), channel_id=1, replica_groups=mesh['expert'=32,'dp'=16] {'dp'}, dimensions={0} | all-to-all | bytes 6291456 | tf_op jit(solution)/shard_map/all_to_all | solution.py:129
  122.6 1.4 local_grads.1
  124.0 30.3 %all_to_all.21 = bf16[16,2,32,1024]{3,2,1,0:T(8,128)(2,1)S(1)} all-to-all(bf16[16,2,32,1024]{3,2,1,0:T(8,128)(2,1)S(1)} %local_grads.1), channel_id=1, replica_groups=mesh['expert'=32,'dp'=16] {'dp'}, dimensions={0} | all-to-all | bytes 4194304 | tf_op jit(solution)/shard_map/all_to_all | solution.py:139
  154.2 0.2 fusion.8
  154.5 0.0 copy-start.3
  154.5 0.0 copy-start.2
  154.5 0.7 fusion.6
  155.2 0.3 copy-done.3
  155.4 0.6 copy-done.2
  156.0 0.7 fusion.2
  156.7 1.0 copy.20
  157.7 6.7 %all-to-all-start.3 = ((bf16[32,16,448]{2,1,0:T(8,128)(2,1)}), bf16[32,16,448]{2,1,0:T(8,128)(2,1)S(1)}, u32[]{:S(2)}, u32[]{:S(2)}) async-start(bf16[32,16,448]{2,1,0:T(8,128)(2,1)} %bitcast.7), calls=%async_computation.3 | async-start | bytes 1048576 | tf_op jit(solution)/shard_map/all_to_all | solution.py:150
  164.4 2.8 %fusion = bf16[1,448,1024]{2,1,0:T(8,128)(2,1)} fusion(bf16[512,1024]{1,0:T(8,128)(2,1)} %bitcast.33, bf16[512,896]{1,0:T(8,128)(2,1)S(1)} %bitcast.25), kind=kOutput, calls=%fused_computation.3 | convolution fusion | flops 470220800 | bytes 2490368 | tf_op jit(solution)/shard_map/dot_general | solution.py:154
  167.2 1.6 fusion.1
  168.8 29.1 %all-to-all-done.3 = bf16[32,16,448]{2,1,0:T(8,128)(2,1)S(1)} async-done(((bf16[32,16,448]{2,1,0:T(8,128)(2,1)}), bf16[32,16,448]{2,1,0:T(8,128)(2,1)S(1)}, u32[]{:S(2)}, u32[]{:S(2)}) %all-to-all-start.3) | async-done | bytes 458784 | tf_op jit(solution)/shard_map/all_to_all | solution.py:150
  198.0 1.0 convolution_convert_fusion.2
Async XLA Ops:
  6.6 67.1 %copy-start = (bf16[1,448,1024]{2,1,0:T(8,128)(2,1)S(1)}, bf16[1,448,1024]{2,1,0:T(8,128)(2,1)}, u32[]{:S(2)}) copy-start(bf16[1,448,1024]{2,1,0:T(8,128)(2,1)} %param.9) | copy-start | bytes 2752516
  6.6 67.1 %all-to-all-start = ((bf16[32,16,896]{2,1,0:T(8,128)(2,1)}), bf16[32,16,896]{2,1,0:T(8,128)(2,1)S(1)}, u32[]{:S(2)}, u32[]{:S(2)}) async-start(bf16[32,16,896]{2,1,0:T(8,128)(2,1)} %bitcast), calls=%async_computation | async-start | bytes 1835008 | tf_op jit(solution)/shard_map/all_to_all | solution.py:110
  73.7 1.2 copy-start.1
  154.5 1.0 copy-start.3
  154.5 1.6 copy-start.2
  157.7 40.2 %all-to-all-start.3 = ((bf16[32,16,448]{2,1,0:T(8,128)(2,1)}), bf16[32,16,448]{2,1,0:T(8,128)(2,1)S(1)}, u32[]{:S(2)}, u32[]{:S(2)}) async-start(bf16[32,16,448]{2,1,0:T(8,128)(2,1)} %bitcast.7), calls=%async_computation.3 | async-start | bytes 1048576 | tf_op jit(solution)/shard_map/all_to_all | solution.py:150

commit v2 on v1

v2 whole, which is shorter than its diff:
```python
import jax
import jax.numpy as jnp
from jax import lax
from jax.experimental import pallas as pl
from jax.experimental.pallas import tpu as pltpu
from jax.sharding import PartitionSpec as P

CAP = 16
MIB = 1 << 20


def dispatch_kernel(
    ids_hbm, gates_hbm, tokens_hbm, cotangent_hbm, send_ref, member_ref,
    ids_ref, gates_ref, tokens_ref, cotangent_ref, both, sems,
):
    copies = [
        pltpu.make_async_copy(source, target, sems.at[i])
        for i, (source, target) in enumerate(
            (
                (ids_hbm, ids_ref),
                (gates_hbm, gates_ref),
                (tokens_hbm, tokens_ref),
                (cotangent_hbm, cotangent_ref),
            )
        )
    ]
    for copy in copies:
        copy.start()
    tok_rows, top_count = ids_ref.shape
    width = tokens_ref.shape[1]
    slots = send_ref.shape[0]
    held = slots // CAP
    copies[0].wait()
    copies[1].wait()
    ids = ids_ref[...]
    gates = gates_ref[...]
    lane = lax.broadcasted_iota(jnp.int32, (tok_rows, 128), 1)
    onehot = jnp.zeros((tok_rows, 128), jnp.float32)
    gate = jnp.zeros((tok_rows, 128), jnp.float32)
    for k in range(top_count):
        hit = ids[:, k : k + 1] == lane
        onehot = jnp.where(hit, 1.0, onehot)
        gate = jnp.where(hit, gates[:, k : k + 1], gate)
    named = onehot.T[:held]
    gate = gate.T[:held]
    earlier = lax.broadcasted_iota(jnp.int32, (tok_rows, tok_rows), 0) < lax.broadcasted_iota(
        jnp.int32, (tok_rows, tok_rows), 1
    )
    rank = jnp.dot(
        named.astype(jnp.bfloat16),
        jnp.where(earlier, 1.0, 0.0).astype(jnp.bfloat16),
        preferred_element_type=jnp.float32,
    )
    code = jnp.where(named > 0.0, rank, -1.0)

    def by_slot(table):
        return jnp.broadcast_to(table[:, None, :], (held, CAP, tok_rows)).reshape(slots, tok_rows)

    slot = (lax.broadcasted_iota(jnp.int32, (slots, tok_rows), 0) % CAP).astype(jnp.float32)
    placed = by_slot(code) == slot
    slot_gate = jnp.sum(jnp.where(placed, by_slot(gate), 0.0), axis=1, keepdims=True)
    member = jnp.where(placed, 1.0, 0.0).astype(jnp.bfloat16)
    member_ref[...] = member
    copies[2].wait()
    copies[3].wait()
    both[:, :width] = tokens_ref[...]
    both[:, width:] = cotangent_ref[...]
    picked = jnp.dot(member, both[...], preferred_element_type=jnp.float32)
    column = lax.broadcasted_iota(jnp.int32, picked.shape, 1)
    send_ref[...] = jnp.where(column < width, picked, picked * slot_gate).astype(jnp.bfloat16)


def scale_power(value):
    most = jnp.max(jnp.abs(value), axis=1, keepdims=True)
    return jnp.floor(jnp.log2(jnp.maximum(most, 1e-30)))


def put_coded(out_ref, at, values):
    rows, cols = values[0].shape
    lane = lax.broadcasted_iota(jnp.int32, (rows, 128), 1)
    powers = jnp.zeros((rows, 128), jnp.float32)
    for i, value in enumerate(values):
        power = scale_power(value)
        coded = jnp.round(value * jnp.exp2(13.0 - power)).astype(jnp.int32).astype(jnp.int16)
        out_ref[at, i * cols : (i + 1) * cols] = coded
        powers = jnp.where(lane == i, power, powers)
    out_ref[at, 3 * cols :] = powers.astype(jnp.int32).astype(jnp.int16)


def sum_coded(parts_ref, cols):
    totals = [None] * 3
    for p in range(parts_ref.shape[0]):
        powers = parts_ref[p, :, 3 * cols :].astype(jnp.int32).astype(jnp.float32)
        for i in range(3):
            unit = jnp.exp2(powers[:, i : i + 1] - 13.0)
            coded = parts_ref[p, :, i * cols : (i + 1) * cols].astype(jnp.int32)
            value = coded.astype(jnp.float32) * unit
            totals[i] = value if p == 0 else totals[i] + value
    return totals


def partial_kernel(recv_ref, gate_ref, up_ref, down_ref, out_ref):
    width = gate_ref.shape[0]
    x = recv_ref[:, :width]
    g = recv_ref[:, width:]
    values = (
        jnp.dot(x, gate_ref[...], preferred_element_type=jnp.float32),
        jnp.dot(x, up_ref[...], preferred_element_type=jnp.float32),
        lax.dot_general(
            g, down_ref[...], (((1,), (1,)), ((), ())), preferred_element_type=jnp.float32
        ),
    )
    put_coded(out_ref, slice(None), values)


def middle_kernel(cols, parts_ref, out_ref):
    put_coded(out_ref, slice(None), sum_coded(parts_ref, cols))


def local_kernel(cols, parts_ref, out_ref):
    gate_act, up_act, back_act = sum_coded(parts_ref, cols)
    sig = 1.0 / (1.0 + jnp.exp(-gate_act))
    grad_gate = (back_act * up_act * sig * (1.0 + gate_act * (1.0 - sig))).astype(jnp.bfloat16)
    grad_up = (back_act * gate_act * sig).astype(jnp.bfloat16)
    for p in range(out_ref.shape[0]):
        out_ref[p, :, :cols] = grad_gate
        out_ref[p, :, cols:] = grad_up


def row_kernel(grads_ref, gate_ref, up_ref, out_ref):
    hidden = gate_ref.shape[1]
    across = (((1,), (1,)), ((), ()))
    out_ref[...] = (
        lax.dot_general(
            grads_ref[:, :hidden], gate_ref[...], across, preferred_element_type=jnp.float32
        )
        + lax.dot_general(
            grads_ref[:, hidden:], up_ref[...], across, preferred_element_type=jnp.float32
        )
    ).astype(jnp.bfloat16)


def plane_groups(held, side, swap):
    groups = []
    for e in range(held):
        for other in range(side):
            if (e % 2 == 1) == swap:
                group = [(e * side + a) * side + other for a in range(side)]
            else:
                group = [(e * side + other) * side + a for a in range(side)]
            groups.append(group)
    return groups


def exchange(blocks, axes, groups):
    return lax.all_to_all(
        blocks, axes, split_axis=0, concat_axis=0, tiled=True, axis_index_groups=groups
    )


def body(tokens, cotangent, gate_weight, up_weight, down_weight, expert_ids, gate_values):
    held = lax.axis_size("expert")
    parts = lax.axis_size("dp")
    tok_rows, width = tokens.shape
    slots = held * CAP
    hidden = gate_weight.shape[2]
    gate_w = gate_weight[0]
    up_w = up_weight[0]
    down_w = down_weight[0]
    send, member = pl.pallas_call(
        dispatch_kernel,
        out_shape=(
            jax.ShapeDtypeStruct((slots, 2 * width), jnp.bfloat16),
            jax.ShapeDtypeStruct((slots, tok_rows), jnp.bfloat16),
        ),
        in_specs=[pl.BlockSpec(memory_space=pltpu.HBM)] * 4,
        scratch_shapes=[
            pltpu.VMEM(expert_ids.shape, expert_ids.dtype),
            pltpu.VMEM(gate_values.shape, gate_values.dtype),
            pltpu.VMEM(tokens.shape, tokens.dtype),
            pltpu.VMEM(cotangent.shape, cotangent.dtype),
            pltpu.VMEM((tok_rows, 2 * width), jnp.bfloat16),
            pltpu.SemaphoreType.DMA((4,)),
        ],
        compiler_params=pltpu.CompilerParams(vmem_limit_bytes=32 * MIB),
        name="dispatch",
    )(expert_ids, gate_values, tokens, cotangent)
    recv = lax.all_to_all(
        send.reshape(held, CAP, 2 * width), "expert", split_axis=0, concat_axis=0, tiled=True
    ).reshape(slots, 2 * width)
    side = 4
    axes = ("expert", "dp")
    first, second = plane_groups(held, side, False), plane_groups(held, side, True)
    rows = slots // parts
    wide = side * rows
    coded = 3 * hidden + 128
    compiler_params = pltpu.CompilerParams(vmem_limit_bytes=32 * MIB)
    sums = pl.pallas_call(
        partial_kernel,
        grid=(side,),
        in_specs=[
            pl.BlockSpec((wide, 2 * width), lambda i: (i, 0)),
            pl.BlockSpec((width, hidden), lambda i: (0, 0)),
            pl.BlockSpec((width, hidden), lambda i: (0, 0)),
            pl.BlockSpec((hidden, width), lambda i: (0, 0)),
        ],
        out_specs=pl.BlockSpec((wide, coded), lambda i: (i, 0)),
        out_shape=jax.ShapeDtypeStruct((slots, coded), jnp.int16),
        compiler_params=compiler_params,
        name="partials",
    )(recv, gate_w, up_w, down_w)
    sums = exchange(sums.reshape(side, wide, coded), axes, first)
    sums = pl.pallas_call(
        lambda *refs: middle_kernel(hidden, *refs),
        grid=(side,),
        in_specs=[pl.BlockSpec((side, rows, coded), lambda i: (0, i, 0))],
        out_specs=pl.BlockSpec((rows, coded), lambda i: (i, 0)),
        out_shape=jax.ShapeDtypeStruct((wide, coded), jnp.int16),
        compiler_params=compiler_params,
        name="middle_sums",
    )(sums)
    sums = exchange(sums.reshape(side, rows, coded), axes, second)
    grads = pl.pallas_call(
        lambda *refs: local_kernel(hidden, *refs),
        out_shape=jax.ShapeDtypeStruct((side, rows, 2 * hidden), jnp.bfloat16),
        compiler_params=compiler_params,
        name="local_grads",
    )(sums)
    grads = exchange(grads, axes, second).reshape(1, wide, 2 * hidden)
    grads = exchange(jnp.broadcast_to(grads, (side, wide, 2 * hidden)), axes, first)
    grads = grads.reshape(slots, 2 * hidden)
    grad_gate = grads[:, :hidden]
    grad_up = grads[:, hidden:]
    half = slots // 2
    row_grads = pl.pallas_call(
        row_kernel,
        grid=(2,),
        in_specs=[
            pl.BlockSpec((half, 2 * hidden), lambda i: (i, 0)),
            pl.BlockSpec((width, hidden), lambda i: (0, 0)),
            pl.BlockSpec((width, hidden), lambda i: (0, 0)),
        ],
        out_specs=pl.BlockSpec((half, width), lambda i: (i, 0)),
        out_shape=jax.ShapeDtypeStruct((slots, width), jnp.bfloat16),
        compiler_params=compiler_params,
        name="row_grads",
    )(grads, gate_w, up_w)
    returned = lax.all_to_all(
        row_grads.reshape(held, CAP, width), "expert", split_axis=0, concat_axis=0, tiled=True
    ).reshape(slots, width)
    recv_rows = recv[:, :width]
    gate_grad = lax.dot_general(
        recv_rows, grad_gate, (((0,), (0,)), ((), ())), preferred_element_type=jnp.float32
    ).astype(jnp.bfloat16)
    up_grad = lax.dot_general(
        recv_rows, grad_up, (((0,), (0,)), ((), ())), preferred_element_type=jnp.float32
    ).astype(jnp.bfloat16)
    token_grad = lax.dot_general(
        member, returned, (((0,), (0,)), ((), ())), preferred_element_type=jnp.float32
    ).astype(jnp.bfloat16)
    return (token_grad, gate_grad[None], up_grad[None])


def solution(mesh):
    placed = (
        P("expert", "dp"),
        P("expert", "dp"),
        P("expert", "dp", None),
        P("expert", "dp", None),
        P("expert", None, "dp"),
        P("expert", None),
        P("expert", None),
    )
    return jax.shard_map(
        body,
        mesh=mesh,
        in_specs=placed,
        out_specs=(P("expert", "dp"), P("expert", "dp", None), P("expert", "dp", None)),
        check_vma=False,
    )
```

time: 200 us -> 195 us (0.975)
  blocking collectives: 75 us -> 65.6 us
  Pallas kernels: 6.48 us -> 10.5 us
  starting transfers between devices: 23.6 us -> 26.4 us
    all_to_all x2 -> x4, blocking collectives: 75 us -> 65.6 us  [exchange(): lax.all_to_all(blocks, axes, split_axis=0, concat_axis=0, tiled=True, axi...]
    pallas_call x2 -> x4, Pallas kernels: 4.33 us -> 7.67 us  [the longest x1 3.71 us: body(): pl.pallas_call(partial_kernel, grid=(side,), in_specs=[pl.BlockSpec((wide...]
    all_to_all x1, starting transfers between devices: 6.67 us -> 9.5 us  [body(): lax.all_to_all(row_grads.reshape(held, CAP, width), 'expert', split_axis=...]
  transfers between devices with their start and end apart: 2 -> 2, of which waited for: 2 -> 2; matrix products, arithmetic and copies ran while one was open for 3% -> 2% of each run, Pallas kernels for 0% -> 0%
where the time goes in v2:
time: 195 us; the launch traced here: 194 us
  waiting for transfers between devices  79.1 us (41%)
  blocking collectives  65.6 us (34%)
  starting transfers between devices  26.4 us (14%)
  Pallas kernels  10.5 us (5%)
  local copies, waits for them, and re-layouts  6.7 us (3%)
  matrix products  5.25 us (3%)
    all_to_all x4, blocking collectives, exchange(): lax.all_to_all(blocks, axes, split_axis=0, concat_axis=0, tiled=True, axi...  65.6 us
    all_to_all x1, waiting for transfers between devices, body(): lax.all_to_all(send.reshape(held, CAP, 2 * width), 'expert', split_axis=0...  48.7 us
    all_to_all x1, waiting for transfers between devices, body(): lax.all_to_all(row_grads.reshape(held, CAP, width), 'expert', split_axis=...  30.4 us
    all_to_all x1, starting transfers between devices, body(): lax.all_to_all(send.reshape(held, CAP, 2 * width), 'expert', split_axis=0...  16.9 us
    all_to_all x1, starting transfers between devices, body(): lax.all_to_all(row_grads.reshape(held, CAP, width), 'expert', split_axis=...  9.5 us
    unnamed x13, local copies, waits for them, and re-layouts  6.46 us
  transfers between devices with their start and end apart: 2, of which 2 were waited for; matrix products, arithmetic and copies ran while one was open for 2% of the time, Pallas kernels for 0%

profile of v2, /device:TPU:1, one launch (start us, length us, event | category | flops | bytes accessed | tf_op | source)
XLA Modules:
  0.0 194.4 jit_solution(16155299867763179322)
XLA Ops:
  0.6 0.8 copy.10.ids_hbm
  1.5 0.8 copy.11.gates_hbm
  2.3 1.1 copy.12.tokens_hbm
  3.4 1.1 copy.13.cotangent_hbm
  4.5 2.9 %dispatch.1 = (bf16[512,896]{1,0:T(8,128)(2,1)}, bf16[512,256]{1,0:T(8,128)(2,1)S(1)}) custom-call(s32[256,8]{1,0:T(8,128)S(1)} %copy.10.ids_hbm, f32[256,8]{1,0:T(8,128)S(1)} %copy.11.gates_hbm, bf16[256,448]{1,0:T(8,128)(2,1)S(1)} %copy.12.tokens_hbm, bf16[256,448]{1,0:T(8,128)(2,1)S(1)} %copy.13.cotangent_hbm), custom_call_target="tpu_custom_call" | custom-call | tf_op jit(solution)/shard_map/dispatch/pallas_call | solution.py:170
  7.3 0.0 copy-start
  7.3 16.9 %all-to-all-start = ((bf16[32,16,896]{2,1,0:T(8,128)(2,1)}), bf16[32,16,896]{2,1,0:T(8,128)(2,1)S(1)}, u32[]{:S(2)}, u32[]{:S(2)}) async-start(bf16[32,16,896]{2,1,0:T(8,128)(2,1)} %bitcast), calls=%async_computation | async-start | bytes 1835008 | tf_op jit(solution)/shard_map/all_to_all | solution.py:188
  24.2 1.5 copy.14
  25.7 48.7 %all-to-all-done = bf16[32,16,896]{2,1,0:T(8,128)(2,1)S(1)} async-done(((bf16[32,16,896]{2,1,0:T(8,128)(2,1)}), bf16[32,16,896]{2,1,0:T(8,128)(2,1)S(1)}, u32[]{:S(2)}, u32[]{:S(2)}) %all-to-all-start) | async-done | bytes 917536 | tf_op jit(solution)/shard_map/all_to_all | solution.py:188
  74.4 0.0 copy-done
  74.4 0.0 copy-start.2
  74.4 1.2 copy-done.2
  75.6 3.7 %partials.1 = s16[512,3200]{1,0:T(8,128)(2,1)S(1)} custom-call(bf16[512,896]{1,0:T(8,128)(2,1)S(1)} %bitcast.22, bf16[448,1024]{1,0:T(8,128)(2,1)S(1)} %bitcast.25, bf16[448,1024]{1,0:T(8,128)(2,1)S(1)} %bitcast.27, bf16[1024,448]{1,0:T(8,128)(2,1)S(1)} %bitcast.21), custom_call_target="tpu_custom_call" | custom-call | tf_op jit(solution)/shard_map/partials/pallas_call | solution.py:198
  79.3 25.6 %all_to_all.30.refs_0_ = s16[4,128,3200]{2,1,0:T(8,128)(2,1)S(1)} all-to-all(s16[4,128,3200]{2,1,0:T(8,128)(2,1)S(1)} %bitcast.17), channel_id=1, replica_groups={{0,4,8,12},{1,5,9,13},{2,6,10,14},{3,7,11,15},{16,17,18,19},{20,21,22,2..., dimensions={0} | all-to-all | bytes 6553600 | tf_op jit(solution)/shard_map/all_to_all | solution.py:156
  105.0 1.5 middle_sums.1
  106.5 12.7 %all_to_all.31.refs_0_ = s16[4,32,3200]{2,1,0:T(8,128)(2,1)S(1)} all-to-all(s16[4,32,3200]{2,1,0:T(8,128)(2,1)S(1)} %bitcast.29), channel_id=1, replica_groups={{0,1,2,3},{4,5,6,7},{8,9,10,11},{12,13,14,15},{16,20,24,28},{17,21,25,2..., dimensions={0} | all-to-all | bytes 1638400 | tf_op jit(solution)/shard_map/all_to_all | solution.py:156
  119.1 0.3 local_grads.1
  119.4 9.3 %all_to_all.32 = bf16[4,32,2048]{2,1,0:T(8,128)(2,1)S(1)} all-to-all(bf16[4,32,2048]{2,1,0:T(8,128)(2,1)S(1)} %local_grads.1), channel_id=1, replica_groups={{0,1,2,3},{4,5,6,7},{8,9,10,11},{12,13,14,15},{16,20,24,28},{17,21,25,2..., dimensions={0} | all-to-all | bytes 1048576 | tf_op jit(solution)/shard_map/all_to_all | solution.py:156
  128.8 0.2 broadcast_in_dim.14
  129.0 0.0 copy-start.1
  129.0 0.0 copy-start.3
  129.0 18.0 %all_to_all.33 = bf16[4,128,2048]{2,1,0:T(8,128)(2,1)S(1)} all-to-all(bf16[4,128,2048]{2,1,0:T(8,128)(2,1)S(1)} %broadcast_in_dim.14), channel_id=1, replica_groups={{0,4,8,12},{1,5,9,13},{2,6,10,14},{3,7,11,15},{16,17,18,19},{20,21,22,2..., dimensions={0} | all-to-all | bytes 4194304 | tf_op jit(solution)/shard_map/all_to_all | solution.py:156
  147.0 0.0 copy-done.1
  147.0 0.0 copy-done.3
  147.0 2.2 %row_grads.1 = bf16[512,448]{1,0:T(8,128)(2,1)} custom-call(bf16[512,2048]{1,0:T(8,128)(2,1)S(1)} %bitcast.18, bf16[448,1024]{1,0:T(8,128)(2,1)S(1)} %bitcast.26, bf16[448,1024]{1,0:T(8,128)(2,1)S(1)} %bitcast.28), custom_call_target="tpu_custom_call" | custom-call | tf_op jit(solution)/shard_map/row_grads/pallas_call | solution.py:235
  149.2 9.5 %all-to-all-start.5 = ((bf16[32,16,448]{2,1,0:T(8,128)(2,1)}), bf16[32,16,448]{2,1,0:T(8,128)(2,1)}, u32[]{:S(2)}, u32[]{:S(2)}) async-start(bf16[32,16,448]{2,1,0:T(8,128)(2,1)} %bitcast.9), calls=%async_computation.5 | async-start | bytes 1048576 | tf_op jit(solution)/shard_map/all_to_all | solution.py:248
  158.7 1.6 fusion.1
  160.3 1.6 fusion
  161.9 30.4 %all-to-all-done.5 = bf16[32,16,448]{2,1,0:T(8,128)(2,1)} async-done(((bf16[32,16,448]{2,1,0:T(8,128)(2,1)}), bf16[32,16,448]{2,1,0:T(8,128)(2,1)}, u32[]{:S(2)}, u32[]{:S(2)}) %all-to-all-start.5) | async-done | bytes 458784 | tf_op jit(solution)/shard_map/all_to_all | solution.py:248
  192.3 2.1 %convolution_convert_fusion.2 = bf16[256,448]{0,1:T(8,128)(2,1)} fusion(bf16[512,256]{1,0:T(8,128)(2,1)S(1)} %get-tuple-element.5, bf16[512,448]{1,0:T(8,128)(2,1)} %bitcast.10), kind=kOutput, calls=%fused_computation.4 | convolution fusion | flops 117555200 | bytes 950272 | tf_op jit(solution)/shard_map/dot_general | solution.py:258
Async XLA Ops:
  7.3 67.1 %copy-start = (bf16[1,448,1024]{2,1,0:T(8,128)(2,1)S(1)}, bf16[1,448,1024]{2,1,0:T(8,128)(2,1)}, u32[]{:S(2)}) copy-start(bf16[1,448,1024]{2,1,0:T(8,128)(2,1)} %param.9) | copy-start | bytes 2752516
  7.3 67.1 %all-to-all-start = ((bf16[32,16,896]{2,1,0:T(8,128)(2,1)}), bf16[32,16,896]{2,1,0:T(8,128)(2,1)S(1)}, u32[]{:S(2)}, u32[]{:S(2)}) async-start(bf16[32,16,896]{2,1,0:T(8,128)(2,1)} %bitcast), calls=%async_computation | async-start | bytes 1835008 | tf_op jit(solution)/shard_map/all_to_all | solution.py:188
  74.4 1.2 copy-start.2
  129.0 18.0 %copy-start.1 = (bf16[1,448,1024]{2,1,0:T(8,128)(2,1)S(1)}, bf16[1,448,1024]{2,1,0:T(8,128)(2,1)}, u32[]{:S(2)}) copy-start(bf16[1,448,1024]{2,1,0:T(8,128)(2,1)} %param.9) | copy-start | bytes 2752516
  129.0 18.0 %copy-start.3 = (bf16[1,448,1024]{2,1,0:T(8,128)(2,1)S(1)}, bf16[1,448,1024]{2,1,0:T(8,128)(2,1)}, u32[]{:S(2)}) copy-start(bf16[1,448,1024]{2,1,0:T(8,128)(2,1)} %param.10) | copy-start | bytes 2752516
  149.2 43.1 %all-to-all-start.5 = ((bf16[32,16,448]{2,1,0:T(8,128)(2,1)}), bf16[32,16,448]{2,1,0:T(8,128)(2,1)}, u32[]{:S(2)}, u32[]{:S(2)}) async-start(bf16[32,16,448]{2,1,0:T(8,128)(2,1)} %bitcast.9), calls=%async_computation.5 | async-start | bytes 1048576 | tf_op jit(solution)/shard_map/all_to_all | solution.py:248

commit v3 on v1

v3 whole, which is shorter than its diff:
```python
import jax
import jax.numpy as jnp
from jax import lax
from jax.experimental import pallas as pl
from jax.experimental.pallas import tpu as pltpu
from jax.sharding import PartitionSpec as P

CAP = 16
SIDE = 4
TILE = 256
MIB = 1 << 20
AXES = ("expert", "dp")
ACROSS = (((1,), (1,)), ((), ()))
DOWN = (((0,), (0,)), ((), ()))


def dispatch_kernel(ids_ref, gates_ref, tokens_ref, cotangent_ref, send_ref, member_ref, both):
    top_count, tok_rows = ids_ref.shape
    width = tokens_ref.shape[0]
    slots = send_ref.shape[0]
    held = slots // CAP
    ids = ids_ref[...]
    gates = gates_ref[...]
    expert = lax.broadcasted_iota(jnp.int32, (held, tok_rows), 0)
    named = jnp.zeros((held, tok_rows), jnp.float32)
    gate = jnp.zeros((held, tok_rows), jnp.float32)
    for k in range(top_count):
        hit = ids[k : k + 1, :] == expert
        named = jnp.where(hit, 1.0, named)
        gate = jnp.where(hit, gates[k : k + 1, :], gate)
    earlier = lax.broadcasted_iota(jnp.int32, (tok_rows, tok_rows), 0) < lax.broadcasted_iota(
        jnp.int32, (tok_rows, tok_rows), 1
    )
    rank = jnp.dot(
        named.astype(jnp.bfloat16),
        jnp.where(earlier, 1.0, 0.0).astype(jnp.bfloat16),
        preferred_element_type=jnp.float32,
    )
    code = jnp.where(named > 0.0, rank, -1.0)

    def by_slot(table):
        return jnp.broadcast_to(table[:, None, :], (held, CAP, tok_rows)).reshape(slots, tok_rows)

    slot = (lax.broadcasted_iota(jnp.int32, (slots, tok_rows), 0) % CAP).astype(jnp.float32)
    placed = by_slot(code) == slot
    slot_gate = jnp.sum(jnp.where(placed, by_slot(gate), 0.0), axis=1, keepdims=True)
    member = jnp.where(placed, 1.0, 0.0)
    halves = member.reshape(held, 2, CAP // 2, tok_rows)
    for i in (0, 1):
        member_ref[i] = halves[:, i].reshape(slots // 2, tok_rows).astype(jnp.bfloat16)
    member = member.astype(jnp.bfloat16)
    both[:width, :] = tokens_ref[...]
    both[width:, :] = cotangent_ref[...]
    picked = lax.dot_general(member, both[...], ACROSS, preferred_element_type=jnp.float32)
    column = lax.broadcasted_iota(jnp.int32, picked.shape, 1)
    send_ref[...] = jnp.where(column < width, picked, picked * slot_gate).astype(jnp.bfloat16)


def put_coded(out_ref, values):
    rows, cols = values[0].shape
    lane = lax.broadcasted_iota(jnp.int32, (rows, 128), 1)
    powers = jnp.zeros((rows, 128), jnp.float32)
    for i, value in enumerate(values):
        most = jnp.max(jnp.abs(value), axis=1, keepdims=True)
        power = jnp.floor(jnp.log2(jnp.maximum(most, 1e-30)))
        coded = jnp.round(value * jnp.exp2(13.0 - power)).astype(jnp.int32).astype(jnp.int16)
        out_ref[:, i * cols : (i + 1) * cols] = coded
        powers = jnp.where(lane == i, power, powers)
    out_ref[:, 3 * cols :] = powers.astype(jnp.int32).astype(jnp.int16)


def sum_coded(parts_ref, start, cols):
    totals = [None] * 3
    for p in range(parts_ref.shape[0]):
        stop = start + 3 * cols
        powers = parts_ref[p, :, stop : stop + 128].astype(jnp.int32).astype(jnp.float32)
        for i in range(3):
            at = start + i * cols
            unit = jnp.exp2(powers[:, i : i + 1] - 13.0)
            coded = parts_ref[p, :, at : at + cols].astype(jnp.int32)
            value = coded.astype(jnp.float32) * unit
            totals[i] = value if p == 0 else totals[i] + value
    return totals


def partial_kernel(rows_ref, weights_ref, out_ref, x_ref, g_ref):
    parts = rows_ref.shape[0]
    width = rows_ref.shape[2] // 2

    @pl.when(pl.program_id(0) == 0)
    def _():
        for p in range(parts):
            x_ref[:, p * width : (p + 1) * width] = rows_ref[p, :, :width]
            g_ref[:, p * width : (p + 1) * width] = rows_ref[p, :, width:]

    def product(rows, which):
        weight = weights_ref[:, which].reshape(parts * width, TILE)
        return jnp.dot(rows, weight, preferred_element_type=jnp.float32)

    x = x_ref[...]
    put_coded(out_ref, (product(x, 0), product(x, 1), product(g_ref[...], 2)))


def local_kernel(hidden, parts_ref, out_ref):
    for tile in range(hidden // TILE):
        gate_act, up_act, back_act = sum_coded(parts_ref, tile * (3 * TILE + 128), TILE)
        sig = 1.0 / (1.0 + jnp.exp(-gate_act))
        grad_gate = (back_act * up_act * sig * (1.0 + gate_act * (1.0 - sig))).astype(jnp.bfloat16)
        grad_up = (back_act * gate_act * sig).astype(jnp.bfloat16)
        at = tile * TILE
        for p in range(out_ref.shape[0]):
            out_ref[p, :, at : at + TILE] = grad_gate
            out_ref[p, :, hidden + at : hidden + at + TILE] = grad_up


def row_kernel(grads_ref, weights_ref, out_ref):
    width, hidden = weights_ref.shape[2:]

    def product(which):
        grad = grads_ref[:, which * hidden : (which + 1) * hidden]
        return lax.dot_general(
            grad, weights_ref[0, which], ACROSS, preferred_element_type=jnp.float32
        )

    both = (product(0) + product(1)).reshape(-1, 2, CAP // 2, width)
    pair = [both[:, i].reshape(-1, width) for i in (0, 1)]
    out_ref[0] = jnp.concatenate(pair, axis=1).astype(jnp.bfloat16)


def combine_kernel(returned_ref, member_ref, out_ref):
    width = out_ref.shape[0]
    out_ref[...] = (
        lax.dot_general(
            returned_ref[:, :width], member_ref[0], DOWN, preferred_element_type=jnp.float32
        )
        + lax.dot_general(
            returned_ref[:, width:], member_ref[1], DOWN, preferred_element_type=jnp.float32
        )
    ).astype(jnp.bfloat16)


def plane_groups(held, swap):
    groups = []
    for e in range(held):
        for other in range(SIDE):
            if (e % 2 == 1) == swap:
                group = [(e * SIDE + a) * SIDE + other for a in range(SIDE)]
            else:
                group = [(e * SIDE + other) * SIDE + a for a in range(SIDE)]
            groups.append(group)
    return groups


def exchange(blocks, groups):
    return lax.all_to_all(
        blocks, AXES, split_axis=0, concat_axis=0, tiled=True, axis_index_groups=groups
    )


def gather(block, groups):
    return lax.all_gather(block, AXES, axis=0, tiled=True, axis_index_groups=groups)


def body(tokens, cotangent, gate_weight, up_weight, down_weight, expert_ids, gate_values):
    held = lax.axis_size("expert")
    tok_rows, width = tokens.shape
    slots = held * CAP
    hidden = gate_weight.shape[2]
    first, second = plane_groups(held, False), plane_groups(held, True)
    wide = slots // SIDE
    rows = wide // SIDE
    spread = SIDE * width
    coded = hidden // TILE * (3 * TILE + 128)
    params = pltpu.CompilerParams(vmem_limit_bytes=32 * MIB)
    streaming = pltpu.CompilerParams(vmem_limit_bytes=56 * MIB)

    weights = jnp.stack([gate_weight[0], up_weight[0], down_weight[0].T])[None]
    weights = gather(weights, first)

    send, member = pl.pallas_call(
        dispatch_kernel,
        out_shape=(
            jax.ShapeDtypeStruct((slots, 2 * width), jnp.bfloat16),
            jax.ShapeDtypeStruct((2, slots // 2, tok_rows), jnp.bfloat16),
        ),
        scratch_shapes=[pltpu.VMEM((2 * width, tok_rows), jnp.bfloat16)],
        compiler_params=params,
        name="dispatch",
    )(expert_ids.T, gate_values.T, tokens.T, cotangent.T)
    recv = lax.all_to_all(
        send.reshape(held, CAP, 2 * width), "expert", split_axis=0, concat_axis=0, tiled=True
    ).reshape(slots, 2 * width)

    mine = exchange(recv.reshape(SIDE, wide, 2 * width), first)
    sums = pl.pallas_call(
        partial_kernel,
        grid=(hidden // TILE,),
        in_specs=[
            pl.BlockSpec((SIDE, wide, 2 * width), lambda i: (0, 0, 0)),
            pl.BlockSpec((SIDE, 3, width, TILE), lambda i: (0, 0, 0, i)),
        ],
        out_specs=pl.BlockSpec((wide, 3 * TILE + 128), lambda i: (0, i)),
        out_shape=jax.ShapeDtypeStruct((wide, coded), jnp.int16),
        scratch_shapes=[
            pltpu.VMEM((wide, spread), jnp.bfloat16),
            pltpu.VMEM((wide, spread), jnp.bfloat16),
        ],
        compiler_params=streaming,
        name="partials",
    )(mine, weights)
    sums = exchange(sums.reshape(SIDE, rows, coded), second)
    grads = pl.pallas_call(
        lambda *refs: local_kernel(hidden, *refs),
        out_shape=jax.ShapeDtypeStruct((SIDE, rows, 2 * hidden), jnp.bfloat16),
        compiler_params=params,
        name="local_grads",
    )(sums)
    grads = exchange(grads, second).reshape(wide, 2 * hidden)
    row_grads = pl.pallas_call(
        row_kernel,
        grid=(SIDE,),
        in_specs=[
            pl.BlockSpec((wide, 2 * hidden), lambda i: (0, 0)),
            pl.BlockSpec((1, 2, width, hidden), lambda i: (i, 0, 0, 0)),
        ],
        out_specs=pl.BlockSpec((1, wide // 2, 2 * width), lambda i: (i, 0, 0)),
        out_shape=jax.ShapeDtypeStruct((SIDE, wide // 2, 2 * width), jnp.bfloat16),
        compiler_params=streaming,
        name="row_grads",
    )(grads, weights)
    row_grads = exchange(row_grads, first)
    returned = lax.all_to_all(
        row_grads.reshape(held, CAP // 2, 2 * width),
        "expert",
        split_axis=0,
        concat_axis=0,
        tiled=True,
    ).reshape(slots // 2, 2 * width)

    grads_all = gather(grads, first)
    recv_rows = recv[:, :width]
    gate_grad = lax.dot_general(
        recv_rows, grads_all[:, :hidden], DOWN, preferred_element_type=jnp.float32
    ).astype(jnp.bfloat16)
    up_grad = lax.dot_general(
        recv_rows, grads_all[:, hidden:], DOWN, preferred_element_type=jnp.float32
    ).astype(jnp.bfloat16)
    returned, gate_grad, up_grad = lax.optimization_barrier((returned, gate_grad, up_grad))
    token_grad = pl.pallas_call(
        combine_kernel,
        out_shape=jax.ShapeDtypeStruct((width, tok_rows), jnp.bfloat16),
        compiler_params=params,
        name="combine",
    )(returned, member).T
    return (token_grad, gate_grad[None], up_grad[None])


def solution(mesh):
    placed = (
        P("expert", "dp"),
        P("expert", "dp"),
        P("expert", "dp", None),
        P("expert", "dp", None),
        P("expert", None, "dp"),
        P("expert", None),
        P("expert", None),
    )
    return jax.shard_map(
        body,
        mesh=mesh,
        in_specs=placed,
        out_specs=(P("expert", "dp"), P("expert", "dp", None), P("expert", "dp", None)),
        check_vma=False,
    )
```

time: 200 us -> 194 us (0.970)
  waiting for transfers between devices: 77.9 us -> 26.2 us
  blocking collectives: 75 us -> 114 us
  between operations: 0.74 us -> 14.1 us
  Pallas kernels: 6.48 us -> 15.5 us
  starting transfers between devices: 23.6 us -> 14.6 us
  local copies, waits for them, and re-layouts: 8.53 us -> 0.97 us
  other arithmetic: 0 us -> 3.7 us
  matrix products: 6.79 us -> 4.55 us
    all_to_all x2 -> x1, waiting for transfers between devices: 77.9 us -> 26.2 us  [body(): lax.all_to_all(row_grads.reshape(held, CAP // 2, 2 * width), 'expert', sp...]
    all_to_all x2 -> x5, blocking collectives: 75 us -> 114 us  [the longest x1 66.7 us: body(): lax.all_to_all(send.reshape(held, CAP, 2 * width), 'expert', split_axis=0...]
    pallas_call x2 -> x4, Pallas kernels: 4.33 us -> 14.8 us  [the longest x1 7.1 us: body(): pl.pallas_call(partial_kernel, grid=(hidden // TILE,), in_specs=[pl.Block...]
    all_to_all x2 -> x1, starting transfers between devices: 23.6 us -> 14.6 us  [body(): lax.all_to_all(row_grads.reshape(held, CAP // 2, 2 * width), 'expert', sp...]
    unnamed x13 -> x10, local copies, waits for them, and re-layouts: 7.31 us -> 0.97 us
    another operation x0 -> x1, other arithmetic: none -> 3.7 us  [body(): weights = jnp.stack([gate_weight[0], up_weight[0], down_weight[0].T])[None]]
    dot_general x5 -> x2, matrix products: 6.79 us -> 4.55 us  [the longest x1 2.96 us: body(): lax.dot_general(recv_rows, grads_all[:, hidden:], DOWN, preferred_element...]
  transfers between devices with their start and end apart: 2 -> 3, of which waited for: 2 -> 1; matrix products, arithmetic and copies ran while one was open for 3% -> 2% of each run, Pallas kernels for 0% -> 4%
where the time goes in v3:
time: 194 us; the launch traced here: 193 us
  blocking collectives  114 us (59%)
  waiting for transfers between devices  26.2 us (14%)
  Pallas kernels  15.5 us (8%)
  starting transfers between devices  14.6 us (8%)
  between operations  14.1 us (7%)
  matrix products  4.55 us (2%)
  other arithmetic  3.7 us (2%)
    all_to_all x1, blocking collectives, body(): lax.all_to_all(send.reshape(held, CAP, 2 * width), 'expert', split_axis=0...  66.7 us
    all_to_all x4, blocking collectives, exchange(): lax.all_to_all(blocks, AXES, split_axis=0, concat_axis=0, tiled=True, axi...  47.1 us
    all_to_all x1, waiting for transfers between devices, body(): lax.all_to_all(row_grads.reshape(held, CAP // 2, 2 * width), 'expert', sp...  26.2 us
    all_to_all x1, starting transfers between devices, body(): lax.all_to_all(row_grads.reshape(held, CAP // 2, 2 * width), 'expert', sp...  14.6 us
    pallas_call x1, Pallas kernels, body(): pl.pallas_call(partial_kernel, grid=(hidden // TILE,), in_specs=[pl.Block...  7.1 us
    pallas_call x1, Pallas kernels, body(): pl.pallas_call(row_kernel, grid=(SIDE,), in_specs=[pl.BlockSpec((wide, 2...  6.21 us
  transfers between devices with their start and end apart: 3, of which 1 were waited for; matrix products, arithmetic and copies ran while one was open for 2% of the time, Pallas kernels for 4%

profile of v3, /device:TPU:1, one launch (start us, length us, event | category | flops | bytes accessed | tf_op | source)
XLA Modules:
  0.0 193.5 jit_solution(10696698921045641056)
XLA Ops:
  7.2 0.0 all-gather.6.cloned.1.call-start
  7.2 3.7 %pad_maximum_fusion = bf16[3,448,1024]{2,1,0:T(8,128)(2,1)} fusion(bf16[1,448,1024]{2,1,0:T(8,128)(2,1)} %bitcast.34, bf16[1,448,1024]{2,1,0:T(8,128)(2,1)} %param.10, bf16[1,448,1024]{2,1,0:T(8,128)(2,1)} %param.9), kind=kLoop, calls=%fused_computation | loop fusion | flops 2752512 | bytes 5505024 | tf_op jit(solution)/shard_map/stack | solution.py:177
  10.9 0.0 copy-start
  10.9 0.0 copy-start.1
  10.9 0.0 copy-start.2
  10.9 0.0 copy-start.3
  10.9 0.0 all-gather.6.cloned.1.call-update
  10.9 0.0 all-gather.4.cloned.1.call-start
  11.0 0.8 copy-done
  11.8 0.1 copy-done.1
  12.0 0.0 copy-done.2
  12.0 0.0 copy-done.3
  12.0 0.6 dispatch.1
  12.6 66.7 %all_to_all.30 = bf16[32,16,896]{2,1,0:T(8,128)(2,1)S(1)} all-to-all(bf16[32,16,896]{2,1,0:T(8,128)(2,1)S(1)} %bitcast.21), channel_id=1, replica_groups=mesh['expert'=32,'dp'=16] {'expert'}, dimensions={0} | all-to-all | bytes 1835008 | tf_op jit(solution)/shard_map/all_to_all | solution.py:190
  79.3 13.1 %all_to_all.31.rows_ref = bf16[4,128,896]{2,1,0:T(8,128)(2,1)} all-to-all(bf16[4,128,896]{2,1,0:T(8,128)(2,1)S(1)} %bitcast.31), channel_id=1, replica_groups={{0,4,8,12},{1,5,9,13},{2,6,10,14},{3,7,11,15},{16,17,18,19},{20,21,22,2..., dimensions={0} | all-to-all | bytes 1835008 | tf_op jit(solution)/shard_map/all_to_all | solution.py:155
  92.5 0.0 all-gather.6.cloned.1.call-done
  92.5 7.1 %partials.1 = s16[128,3584]{1,0:T(8,128)(2,1)} custom-call(bf16[4,128,896]{2,1,0:T(8,128)(2,1)} %all_to_all.31.rows_ref, bf16[4,3,448,1024]{3,2,1,0:T(8,128)(2,1)} %bitcast.26), custom_call_target="tpu_custom_call" | custom-call | tf_op jit(solution)/shard_map/partials/pallas_call | solution.py:195
  99.6 13.2 %all_to_all.32.refs_0_ = s16[4,32,3584]{2,1,0:T(8,128)(2,1)S(1)} all-to-all(s16[4,32,3584]{2,1,0:T(8,128)(2,1)} %bitcast.30), channel_id=1, replica_groups={{0,1,2,3},{4,5,6,7},{8,9,10,11},{12,13,14,15},{16,20,24,28},{17,21,25,2..., dimensions={0} | all-to-all | bytes 1835008 | tf_op jit(solution)/shard_map/all_to_all | solution.py:155
  112.8 0.4 local_grads.1
  113.2 10.0 %all_to_all.33 = bf16[4,32,2048]{2,1,0:T(8,128)(2,1)} all-to-all(bf16[4,32,2048]{2,1,0:T(8,128)(2,1)S(1)} %local_grads.1), channel_id=1, replica_groups={{0,1,2,3},{4,5,6,7},{8,9,10,11},{12,13,14,15},{16,20,24,28},{17,21,25,2..., dimensions={0} | all-to-all | bytes 1048576 | tf_op jit(solution)/shard_map/all_to_all | solution.py:155
  123.2 0.0 all-gather.4.cloned.1.call-update
  123.2 6.2 %row_grads.1 = bf16[4,64,896]{2,1,0:T(8,128)(2,1)} custom-call(bf16[128,2048]{1,0:T(8,128)(2,1)} %bitcast.29, bf16[4,3,448,1024]{3,2,1,0:T(8,128)(2,1)} %bitcast.27), custom_call_target="tpu_custom_call" | custom-call | tf_op jit(solution)/shard_map/row_grads/pallas_call | solution.py:219
  129.4 10.8 %all_to_all.34 = bf16[4,64,896]{2,1,0:T(8,128)(2,1)} all-to-all(bf16[4,64,896]{2,1,0:T(8,128)(2,1)} %row_grads.1), channel_id=1, replica_groups={{0,4,8,12},{1,5,9,13},{2,6,10,14},{3,7,11,15},{16,17,18,19},{20,21,22,2..., dimensions={0} | all-to-all | bytes 917504 | tf_op jit(solution)/shard_map/all_to_all | solution.py:155
  140.2 14.6 %all-to-all-start.5 = ((bf16[32,8,896]{2,1,0:T(8,128)(2,1)}), bf16[32,8,896]{2,1,0:T(8,128)(2,1)S(1)}, u32[]{:S(2)}, u32[]{:S(2)}) async-start(bf16[32,8,896]{2,1,0:T(8,128)(2,1)} %bitcast.12), calls=%async_computation.5 | async-start | bytes 917504 | tf_op jit(solution)/shard_map/all_to_all | solution.py:232
  154.8 0.0 all-gather.4.cloned.1.call-done
  154.8 0.0 copy-start.4
  154.8 3.0 %convolution_convert_fusion = bf16[448,1024]{1,0:T(8,128)(2,1)} fusion(bf16[512,2048]{1,0:T(8,128)(2,1)} %all-gather.4.cloned.1.call-done, bf16[512,896]{1,0:T(8,128)(2,1)S(1)} %bitcast.32), kind=kOutput, calls=%fused_computation.1 | convolution fusion | flops 470220800 | bytes 2490368 | tf_op jit(solution)/shard_map/dot_general | solution.py:245
  157.8 0.0 copy-done.4
  157.8 1.6 convolution_convert_fusion.1
  159.3 26.2 %all-to-all-done.5 = bf16[32,8,896]{2,1,0:T(8,128)(2,1)S(1)} async-done(((bf16[32,8,896]{2,1,0:T(8,128)(2,1)}), bf16[32,8,896]{2,1,0:T(8,128)(2,1)S(1)}, u32[]{:S(2)}, u32[]{:S(2)}) %all-to-all-start.5) | async-done | bytes 458784 | tf_op jit(solution)/shard_map/all_to_all | solution.py:232
  185.5 1.1 combine.1
Async XLA Ops:
  7.2 85.3 %all-gather.6.cloned.1.call-start = ((), (), s32[]{:S(2)}) async-start(), calls=%async_computation.7 | async-start | bytes 13762560 | tf_op jit(solution)/shard_map/all_gather | solution.py:161
  10.9 0.9 copy-start
  10.9 1.0 copy-start.1
  10.9 1.0 copy-start.2
  10.9 1.0 copy-start.3
  10.9 143.8 %all-gather.4.cloned.1.call-start = ((), (), s32[]{:S(2)}) async-start(), calls=%async_computation.6 | async-start | bytes 2621440 | tf_op jit(solution)/shard_map/all_gather | solution.py:161
  140.2 45.3 %all-to-all-start.5 = ((bf16[32,8,896]{2,1,0:T(8,128)(2,1)}), bf16[32,8,896]{2,1,0:T(8,128)(2,1)S(1)}, u32[]{:S(2)}, u32[]{:S(2)}) async-start(bf16[32,8,896]{2,1,0:T(8,128)(2,1)} %bitcast.12), calls=%async_computation.5 | async-start | bytes 917504 | tf_op jit(solution)/shard_map/all_to_all | solution.py:232
  154.8 3.0 %copy-start.4 = (bf16[512,2048]{1,0:T(8,128)(2,1)S(1)}, bf16[512,2048]{1,0:T(8,128)(2,1)}, u32[]{:S(2)}) copy-start(bf16[512,2048]{1,0:T(8,128)(2,1)} %all-gather.4.cloned.1.call-done) | copy-start | bytes 6291460
Sparse Core Ops, SparseCore 0:
  11.1 74.2 all-gather.5
  123.3 30.9 all-gather.3

commit v4 on v3

--- a/solution.py
+++ b/solution.py
@@ -12,6 +12,23 @@
 AXES = ("expert", "dp")
 ACROSS = (((1,), (1,)), ((), ()))
 DOWN = (((0,), (0,)), ((), ()))
+SHIFTS = (0, 3, 1, 2)
+
+
+def block_at(ref, at):
+    block = ref[0]
+    for p in range(1, SIDE):
+        block = jnp.where(at == p, ref[p], block)
+    return block
+
+
+def pack_kernel(gate_ref, up_ref, down_ref, low_ref, high_ref):
+    width = gate_ref.shape[0]
+    half = width // 2
+    low_ref[:width] = gate_ref[...]
+    low_ref[width:] = down_ref[:half]
+    high_ref[:width] = up_ref[...]
+    high_ref[width:] = down_ref[half:]
 
 
 def dispatch_kernel(ids_ref, gates_ref, tokens_ref, cotangent_ref, send_ref, member_ref, both):
@@ -69,62 +86,80 @@
     out_ref[:, 3 * cols :] = powers.astype(jnp.int32).astype(jnp.int16)
 
 
-def sum_coded(parts_ref, start, cols):
+def sum_coded(parts_ref, cols):
     totals = [None] * 3
     for p in range(parts_ref.shape[0]):
-        stop = start + 3 * cols
-        powers = parts_ref[p, :, stop : stop + 128].astype(jnp.int32).astype(jnp.float32)
+        powers = parts_ref[p, :, 3 * cols :].astype(jnp.int32).astype(jnp.float32)
         for i in range(3):
-            at = start + i * cols
             unit = jnp.exp2(powers[:, i : i + 1] - 13.0)
-            coded = parts_ref[p, :, at : at + cols].astype(jnp.int32)
+            coded = parts_ref[p, :, i * cols : (i + 1) * cols].astype(jnp.int32)
             value = coded.astype(jnp.float32) * unit
             totals[i] = value if p == 0 else totals[i] + value
     return totals
 
 
-def partial_kernel(rows_ref, weights_ref, out_ref, x_ref, g_ref):
-    parts = rows_ref.shape[0]
+def partial_kernel(place_ref, rows_ref, *refs):
+    lows, highs = refs[:SIDE], refs[SIDE : 2 * SIDE]
+    out_ref = refs[2 * SIDE]
     width = rows_ref.shape[2] // 2
-
-    @pl.when(pl.program_id(0) == 0)
-    def _():
-        for p in range(parts):
-            x_ref[:, p * width : (p + 1) * width] = rows_ref[p, :, :width]
-            g_ref[:, p * width : (p + 1) * width] = rows_ref[p, :, width:]
-
-    def product(rows, which):
-        weight = weights_ref[:, which].reshape(parts * width, TILE)
-        return jnp.dot(rows, weight, preferred_element_type=jnp.float32)
-
-    x = x_ref[...]
-    put_coded(out_ref, (product(x, 0), product(x, 1), product(g_ref[...], 2)))
+    half = width // 2
+    totals = [None] * 3
+
+    def add(which, rows, weight):
+        value = jnp.dot(rows, weight, preferred_element_type=jnp.float32)
+        totals[which] = value if totals[which] is None else totals[which] + value
+
+    for shift, low, high in zip(SHIFTS, lows, highs):
+        both = block_at(rows_ref, lax.rem(place_ref[0] + shift, SIDE))
+        x = both[:, :width]
+        add(0, x, low[:width])
+        add(1, x, high[:width])
+        add(2, both[:, width : width + half], low[width:])
+        add(2, both[:, width + half :], high[width:])
+    put_coded(out_ref, totals)
 
 
 def local_kernel(hidden, parts_ref, out_ref):
-    for tile in range(hidden // TILE):
-        gate_act, up_act, back_act = sum_coded(parts_ref, tile * (3 * TILE + 128), TILE)
-        sig = 1.0 / (1.0 + jnp.exp(-gate_act))
-        grad_gate = (back_act * up_act * sig * (1.0 + gate_act * (1.0 - sig))).astype(jnp.bfloat16)
-        grad_up = (back_act * gate_act * sig).astype(jnp.bfloat16)
-        at = tile * TILE
-        for p in range(out_ref.shape[0]):
-            out_ref[p, :, at : at + TILE] = grad_gate
-            out_ref[p, :, hidden + at : hidden + at + TILE] = grad_up
-
-
-def row_kernel(grads_ref, weights_ref, out_ref):
-    width, hidden = weights_ref.shape[2:]
-
-    def product(which):
-        grad = grads_ref[:, which * hidden : (which + 1) * hidden]
-        return lax.dot_general(
-            grad, weights_ref[0, which], ACROSS, preferred_element_type=jnp.float32
+    gate_act, up_act, back_act = sum_coded(parts_ref, hidden)
+    sig = 1.0 / (1.0 + jnp.exp(-gate_act))
+    grad_gate = (back_act * up_act * sig * (1.0 + gate_act * (1.0 - sig))).astype(jnp.bfloat16)
+    grad_up = (back_act * gate_act * sig).astype(jnp.bfloat16)
+    for p in range(out_ref.shape[0]):
+        out_ref[p, :, :hidden] = grad_gate
+        out_ref[p, :, hidden:] = grad_up
+
+
+def row_kernel(place_ref, grads_ref, *refs):
+    lows, highs = refs[:SIDE], refs[SIDE : 2 * SIDE]
+    out_ref = refs[2 * SIDE]
+    wide, hidden = grads_ref.shape[0], grads_ref.shape[1] // 2
+    width = out_ref.shape[2] // 2
+    for shift, low, high in zip(SHIFTS, lows, highs):
+        total = lax.dot_general(
+            grads_ref[:, :hidden], low[:width], ACROSS, preferred_element_type=jnp.float32
+        ) + lax.dot_general(
+            grads_ref[:, hidden:], high[:width], ACROSS, preferred_element_type=jnp.float32
         )
-
-    both = (product(0) + product(1)).reshape(-1, 2, CAP // 2, width)
-    pair = [both[:, i].reshape(-1, width) for i in (0, 1)]
-    out_ref[0] = jnp.concatenate(pair, axis=1).astype(jnp.bfloat16)
+        both = total.reshape(-1, 2, CAP // 2, width)
+        pair = [both[:, j].reshape(wide // 2, width) for j in (0, 1)]
+        value = jnp.concatenate(pair, axis=1).astype(jnp.bfloat16)
+        at = lax.rem(place_ref[0] + shift, SIDE)
+        for p in range(SIDE):
+
+            @pl.when(at == p)
+            def _():
+                out_ref[p] = value
+
+
+def weight_kernel(place_ref, rows_ref, *refs):
+    grads, out_ref = refs[:SIDE], refs[SIDE]
+    width = out_ref.shape[1]
+    value = None
+    for shift, grad in zip(SHIFTS, grads):
+        rows = block_at(rows_ref, lax.rem(place_ref[0] + shift, SIDE))[:, :width]
+        term = lax.dot_general(rows, grad[...], DOWN, preferred_element_type=jnp.float32)
+        value = term if value is None else value + term
+    out_ref[0] = value.astype(jnp.bfloat16)
 
 
 def combine_kernel(returned_ref, member_ref, out_ref):
@@ -151,14 +186,17 @@
     return groups
 
 
+def plane_ring(held, step):
+    pairs = []
+    for group in plane_groups(held, False):
+        pairs += [(group[i], group[(i + step) % SIDE]) for i in range(SIDE)]
+    return pairs
+
+
 def exchange(blocks, groups):
     return lax.all_to_all(
         blocks, AXES, split_axis=0, concat_axis=0, tiled=True, axis_index_groups=groups
     )
-
-
-def gather(block, groups):
-    return lax.all_gather(block, AXES, axis=0, tiled=True, axis_index_groups=groups)
 
 
 def body(tokens, cotangent, gate_weight, up_weight, down_weight, expert_ids, gate_values):
@@ -169,13 +207,14 @@
     first, second = plane_groups(held, False), plane_groups(held, True)
     wide = slots // SIDE
     rows = wide // SIDE
-    spread = SIDE * width
-    coded = hidden // TILE * (3 * TILE + 128)
-    params = pltpu.CompilerParams(vmem_limit_bytes=32 * MIB)
-    streaming = pltpu.CompilerParams(vmem_limit_bytes=56 * MIB)
-
-    weights = jnp.stack([gate_weight[0], up_weight[0], down_weight[0].T])[None]
-    weights = gather(weights, first)
+    coded = 3 * hidden + 128
+    params = pltpu.CompilerParams(vmem_limit_bytes=24 * MIB)
+    alone = pltpu.CompilerParams(vmem_limit_bytes=48 * MIB)
+
+    onward, back = plane_ring(held, 1), plane_ring(held, -1)
+    dp = lax.axis_index("dp")
+    place = jnp.where(lax.axis_index("expert") % 2 == 0, dp // SIDE, dp % SIDE)
+    place = place.astype(jnp.int32).reshape(1)
 
     send, member = pl.pallas_call(
         dispatch_kernel,
@@ -184,30 +223,41 @@
             jax.ShapeDtypeStruct((2, slots // 2, tok_rows), jnp.bfloat16),
         ),
         scratch_shapes=[pltpu.VMEM((2 * width, tok_rows), jnp.bfloat16)],
-        compiler_params=params,
+        compiler_params=alone,
         name="dispatch",
     )(expert_ids.T, gate_values.T, tokens.T, cotangent.T)
+    send, gate_w, up_w, down_w = lax.optimization_barrier(
+        (send, gate_weight[0], up_weight[0], down_weight[0].T)
+    )
+    half = jax.ShapeDtypeStruct((width + width // 2, hidden), jnp.bfloat16)
+    low, high = pl.pallas_call(
+        pack_kernel,
+        out_shape=(half, half),
+        compiler_params=params,
+        name="pack",
+    )(gate_w, up_w, down_w)
+    low_1 = lax.ppermute(low, AXES, onward)
+    high_3 = lax.ppermute(high, AXES, back)
+    high_1 = lax.ppermute(high, AXES, onward)
+    low_3 = lax.ppermute(low, AXES, back)
+    low_2 = lax.ppermute(low_1, AXES, onward)
+    high_2 = lax.ppermute(high_3, AXES, back)
+    lows, highs = (low, low_1, low_3, low_2), (high, high_1, high_3, high_2)
     recv = lax.all_to_all(
         send.reshape(held, CAP, 2 * width), "expert", split_axis=0, concat_axis=0, tiled=True
     ).reshape(slots, 2 * width)
 
     mine = exchange(recv.reshape(SIDE, wide, 2 * width), first)
+    vmem = pl.BlockSpec(memory_space=pltpu.VMEM)
+    smem = pl.BlockSpec(memory_space=pltpu.SMEM)
     sums = pl.pallas_call(
         partial_kernel,
-        grid=(hidden // TILE,),
-        in_specs=[
-            pl.BlockSpec((SIDE, wide, 2 * width), lambda i: (0, 0, 0)),
-            pl.BlockSpec((SIDE, 3, width, TILE), lambda i: (0, 0, 0, i)),
-        ],
-        out_specs=pl.BlockSpec((wide, 3 * TILE + 128), lambda i: (0, i)),
+        in_specs=[smem] + [vmem] * (1 + 2 * SIDE),
+        out_specs=vmem,
         out_shape=jax.ShapeDtypeStruct((wide, coded), jnp.int16),
-        scratch_shapes=[
-            pltpu.VMEM((wide, spread), jnp.bfloat16),
-            pltpu.VMEM((wide, spread), jnp.bfloat16),
-        ],
-        compiler_params=streaming,
+        compiler_params=params,
         name="partials",
-    )(mine, weights)
+    )(place, mine, *lows, *highs)
     sums = exchange(sums.reshape(SIDE, rows, coded), second)
     grads = pl.pallas_call(
         lambda *refs: local_kernel(hidden, *refs),
@@ -218,16 +268,12 @@
     grads = exchange(grads, second).reshape(wide, 2 * hidden)
     row_grads = pl.pallas_call(
         row_kernel,
-        grid=(SIDE,),
-        in_specs=[
-            pl.BlockSpec((wide, 2 * hidden), lambda i: (0, 0)),
-            pl.BlockSpec((1, 2, width, hidden), lambda i: (i, 0, 0, 0)),
-        ],
-        out_specs=pl.BlockSpec((1, wide // 2, 2 * width), lambda i: (i, 0, 0)),
+        in_specs=[smem] + [vmem] * (1 + 2 * SIDE),
+        out_specs=vmem,
         out_shape=jax.ShapeDtypeStruct((SIDE, wide // 2, 2 * width), jnp.bfloat16),
-        compiler_params=streaming,
+        compiler_params=params,
         name="row_grads",
-    )(grads, weights)
+    )(place, grads, *lows, *highs)
     row_grads = exchange(row_grads, first)
     returned = lax.all_to_all(
         row_grads.reshape(held, CAP // 2, 2 * width),
@@ -237,14 +283,26 @@
         tiled=True,
     ).reshape(slots // 2, 2 * width)
 
-    grads_all = gather(grads, first)
-    recv_rows = recv[:, :width]
-    gate_grad = lax.dot_general(
-        recv_rows, grads_all[:, :hidden], DOWN, preferred_element_type=jnp.float32
-    ).astype(jnp.bfloat16)
-    up_grad = lax.dot_general(
-        recv_rows, grads_all[:, hidden:], DOWN, preferred_element_type=jnp.float32
-    ).astype(jnp.bfloat16)
+    blocks = [grads] + [lax.ppermute(grads, AXES, plane_ring(held, k)) for k in (1, 3, 2)]
+    column = 2 * TILE
+    per = hidden // column
+
+    def weight_grad(first_column):
+        return pl.pallas_call(
+            weight_kernel,
+            grid=(per,),
+            in_specs=[
+                pl.BlockSpec(memory_space=pltpu.SMEM),
+                pl.BlockSpec((SIDE, wide, 2 * width), lambda i: (0, 0, 0)),
+            ]
+            + [pl.BlockSpec((wide, column), lambda i: (0, i + first_column))] * SIDE,
+            out_specs=pl.BlockSpec((1, width, column), lambda i: (0, 0, i)),
+            out_shape=jax.ShapeDtypeStruct((1, width, hidden), jnp.bfloat16),
+            compiler_params=params,
+            name="weight_grad",
+        )(place, recv.reshape(SIDE, wide, 2 * width), *blocks)
+
+    gate_grad, up_grad = weight_grad(0), weight_grad(per)
     returned, gate_grad, up_grad = lax.optimization_barrier((returned, gate_grad, up_grad))
     token_grad = pl.pallas_call(
         combine_kernel,
@@ -252,7 +310,7 @@
         compiler_params=params,
         name="combine",
     )(returned, member).T
-    return (token_grad, gate_grad[None], up_grad[None])
+    return (token_grad, gate_grad, up_grad)
 
 
 def solution(mesh):

time: 194 us -> 178 us (0.918)
  blocking collectives: 114 us -> 31 us
  starting transfers between devices: 14.6 us -> 63.1 us
  waiting for transfers between devices: 26.2 us -> 53.1 us
  between operations: 14.1 us -> 0.83 us
  Pallas kernels: 15.5 us -> 22.1 us
  local copies, waits for them, and re-layouts: 0.97 us -> 6.79 us
  matrix products: 4.55 us -> 0 us
  other arithmetic: 3.7 us -> 0 us
    all_to_all x1 -> x0, blocking collectives: 66.7 us -> none  [body(): lax.all_to_all(send.reshape(held, CAP, 2 * width), 'expert', split_axis=0...]
    all_to_all x0 -> x2, waiting for transfers between devices: none -> 27.3 us  [the longest x1 19.3 us: body(): lax.all_to_all(send.reshape(held, CAP, 2 * width), 'expert', split_axis=0...]
    ppermute x0 -> x9, starting transfers between devices: none -> 26.8 us  [the longest x3 8.42 us: body(): lax.ppermute(grads, AXES, plane_ring(held, k))]
    all_to_all x0 -> x2, starting transfers between devices: none -> 21 us  [the longest x1 16.8 us: body(): lax.all_to_all(send.reshape(held, CAP, 2 * width), 'expert', split_axis=0...]
    all_to_all x1, waiting for transfers between devices: 26.2 us -> 6.11 us  [body(): lax.all_to_all(row_grads.reshape(held, CAP // 2, 2 * width), 'expert', sp...]
    ppermute x0 -> x9, waiting for transfers between devices: none -> 19.7 us  [the longest x3 9.5 us: body(): lax.ppermute(grads, AXES, plane_ring(held, k))]
    all_to_all x4 -> x3, blocking collectives: 47.1 us -> 31 us  [exchange(): lax.all_to_all(blocks, AXES, split_axis=0, concat_axis=0, tiled=True, axi...]
    pallas_call x2 -> x5, Pallas kernels: 13.3 us -> 19.2 us  [the longest x2 6.7 us: weight_grad(): pl.pallas_call(weight_kernel, grid=(per,), in_specs=[pl.BlockSpec(memory_...]
  transfers between devices with their start and end apart: 3 -> 12, of which waited for: 1 -> 8; matrix products, arithmetic and copies ran while one was open for 2% -> 0% of each run, Pallas kernels for 4% -> 4%
where the time goes in v4:
time: 178 us; the launch traced here: 177 us
  starting transfers between devices  63.1 us (35%)
  waiting for transfers between devices  53.1 us (30%)
  blocking collectives  31 us (17%)
  Pallas kernels  22.1 us (12%)
  local copies, waits for them, and re-layouts  6.79 us (4%)
    all_to_all x3, blocking collectives, exchange(): lax.all_to_all(blocks, AXES, split_axis=0, concat_axis=0, tiled=True, axi...  31 us
    all_to_all x1, waiting for transfers between devices, body(): lax.all_to_all(send.reshape(held, CAP, 2 * width), 'expert', split_axis=0...  19.3 us
    all_to_all x1, starting transfers between devices, body(): lax.all_to_all(send.reshape(held, CAP, 2 * width), 'expert', split_axis=0...  16.8 us
    all_to_all x1, starting transfers between devices, body(): lax.all_to_all(row_grads.reshape(held, CAP // 2, 2 * width), 'expert', sp...  15.4 us
    ppermute x3, waiting for transfers between devices, body(): lax.ppermute(grads, AXES, plane_ring(held, k))  9.5 us
    ppermute x1, waiting for transfers between devices, body(): low_1 = lax.ppermute(low, AXES, onward)  8.85 us
    ppermute x3, starting transfers between devices, body(): lax.ppermute(grads, AXES, plane_ring(held, k))  8.42 us
    all_to_all x1, waiting for transfers between devices, exchange(): lax.all_to_all(blocks, AXES, split_axis=0, concat_axis=0, tiled=True, axi...  7.99 us
  transfers between devices with their start and end apart: 12, of which 8 were waited for; matrix products, arithmetic and copies ran while one was open for 0% of the time, Pallas kernels for 4%

profile of v4, /device:TPU:1, one launch (start us, length us, event | category | flops | bytes accessed | tf_op | source)
XLA Modules:
  0.0 177.0 jit_solution(11303384100155155601)
XLA Ops:
  0.6 0.0 copy-start.3
  0.6 0.9 copy-done.3
  1.6 0.0 copy-start.4
  1.6 0.9 copy-done.4
  2.5 0.0 copy-start.5
  2.5 0.7 copy-done.5
  3.2 0.0 copy-start.6
  3.2 0.7 copy-done.6
  3.9 1.6 dispatch.1
  5.5 16.8 %all-to-all-start = ((bf16[32,16,896]{2,1,0:T(8,128)(2,1)}), bf16[32,16,896]{2,1,0:T(8,128)(2,1)}, u32[]{:S(2)}, u32[]{:S(2)}) async-start(bf16[32,16,896]{2,1,0:T(8,128)(2,1)} %bitcast.9), calls=%async_computation | async-start | bytes 1835008 | tf_op jit(solution)/shard_map/all_to_all | solution.py:246
  22.3 0.0 copy-start
  22.3 1.2 copy-done
  23.5 0.0 copy-start.1
  23.5 1.2 copy-done.1
  24.6 0.0 copy-start.2
  24.6 1.2 copy-done.2
  25.8 0.2 pack.1
  26.0 3.2 %collective-permute-start = (bf16[672,1024]{1,0:T(8,128)(2,1)S(1)}, bf16[672,1024]{1,0:T(8,128)(2,1)}, u32[]{:S(2)}, u32[]{:S(2)}) collective-permute-start(bf16[672,1024]{1,0:T(8,128)(2,1)S(1)} %get-tuple-element.19.refs_0_), channel_id=1, source_target_pairs={{0,4},{4,8},{8,12},{12,0},{1,5},{5,9},{9,13},{13,1},{2,6},{6,10},{... | collective-permute-start | bytes 4128776 | tf_op jit(solution)/shard_map/ppermute | solution.py:239
  29.2 3.4 %collective-permute-start.4 = (bf16[672,1024]{1,0:T(8,128)(2,1)S(1)}, bf16[672,1024]{1,0:T(8,128)(2,1)}, u32[]{:S(2)}, u32[]{:S(2)}) collective-permute-start(bf16[672,1024]{1,0:T(8,128)(2,1)S(1)} %get-tuple-element.20.refs_4_), channel_id=1, source_target_pairs={{0,12},{4,0},{8,4},{12,8},{1,13},{5,1},{9,5},{13,9},{2,14},{6,2},{... | collective-permute-start | bytes 4128776 | tf_op jit(solution)/shard_map/ppermute | solution.py:240
  32.6 3.4 %collective-permute-start.1 = (bf16[672,1024]{1,0:T(8,128)(2,1)S(1)}, bf16[672,1024]{1,0:T(8,128)(2,1)}, u32[]{:S(2)}, u32[]{:S(2)}) collective-permute-start(bf16[672,1024]{1,0:T(8,128)(2,1)S(1)} %get-tuple-element.19.refs_0_), channel_id=1, source_target_pairs={{0,12},{4,0},{8,4},{12,8},{1,13},{5,1},{9,5},{13,9},{2,14},{6,2},{... | collective-permute-start | bytes 4128776 | tf_op jit(solution)/shard_map/ppermute | solution.py:242
  35.9 1.9 %collective-permute-start.3 = (bf16[672,1024]{1,0:T(8,128)(2,1)S(1)}, bf16[672,1024]{1,0:T(8,128)(2,1)}, u32[]{:S(2)}, u32[]{:S(2)}) collective-permute-start(bf16[672,1024]{1,0:T(8,128)(2,1)S(1)} %get-tuple-element.20.refs_4_), channel_id=1, source_target_pairs={{0,4},{4,8},{8,12},{12,0},{1,5},{5,9},{9,13},{13,1},{2,6},{6,10},{... | collective-permute-start | bytes 4128776 | tf_op jit(solution)/shard_map/ppermute | solution.py:241
  37.9 8.9 %collective-permute-done.refs_1_ = bf16[672,1024]{1,0:T(8,128)(2,1)} collective-permute-done((bf16[672,1024]{1,0:T(8,128)(2,1)S(1)}, bf16[672,1024]{1,0:T(8,128)(2,1)}, u32[]{:S(2)}, u32[]{:S(2)}) %collective-permute-start) | collective-permute-done | bytes 1376288 | tf_op jit(solution)/shard_map/ppermute | solution.py:239
  46.7 1.9 %collective-permute-start.2 = (bf16[672,1024]{1,0:T(8,128)(2,1)}, bf16[672,1024]{1,0:T(8,128)(2,1)}, u32[]{:S(2)}, u32[]{:S(2)}) collective-permute-start(bf16[672,1024]{1,0:T(8,128)(2,1)} %collective-permute-done.refs_1_), channel_id=1, source_target_pairs={{0,4},{4,8},{8,12},{12,0},{1,5},{5,9},{9,13},{13,1},{2,6},{6,10},{... | collective-permute-start | bytes 4128776 | tf_op jit(solution)/shard_map/ppermute | solution.py:243
  48.7 0.0 collective-permute-done.4.refs_6_
  48.7 4.6 %collective-permute-start.5 = (bf16[672,1024]{1,0:T(8,128)(2,1)}, bf16[672,1024]{1,0:T(8,128)(2,1)}, u32[]{:S(2)}, u32[]{:S(2)}) collective-permute-start(bf16[672,1024]{1,0:T(8,128)(2,1)} %collective-permute-done.4.refs_6_), channel_id=1, source_target_pairs={{0,12},{4,0},{8,4},{12,8},{1,13},{5,1},{9,5},{13,9},{2,14},{6,2},{... | collective-permute-start | bytes 4128776 | tf_op jit(solution)/shard_map/ppermute | solution.py:244
  53.2 19.3 %all-to-all-done = bf16[32,16,896]{2,1,0:T(8,128)(2,1)} async-done(((bf16[32,16,896]{2,1,0:T(8,128)(2,1)}), bf16[32,16,896]{2,1,0:T(8,128)(2,1)}, u32[]{:S(2)}, u32[]{:S(2)}) %all-to-all-start) | async-done | bytes 917536 | tf_op jit(solution)/shard_map/all_to_all | solution.py:246
  72.5 4.2 %all-to-all-start.1 = ((bf16[4,128,896]{2,1,0:T(8,128)(2,1)}), bf16[4,128,896]{2,1,0:T(8,128)(2,1)}, u32[]{:S(2)}, u32[]{:S(2)}) async-start(bf16[4,128,896]{2,1,0:T(8,128)(2,1)} %bitcast.10.rows_ref), calls=%async_computation.1 | async-start | bytes 1835008 | tf_op jit(solution)/shard_map/all_to_all | solution.py:197
  76.8 0.0 collective-permute-done.1.refs_2_
  76.8 0.0 collective-permute-done.3.refs_5_
  76.8 0.0 collective-permute-done.2.refs_3_
  76.8 1.4 collective-permute-done.5.refs_7_
  78.2 8.0 %all-to-all-done.1.rows_ref = bf16[4,128,896]{2,1,0:T(8,128)(2,1)} async-done(((bf16[4,128,896]{2,1,0:T(8,128)(2,1)}), bf16[4,128,896]{2,1,0:T(8,128)(2,1)}, u32[]{:S(2)}, u32[]{:S(2)}) %all-to-all-start.1) | async-done | bytes 917536 | tf_op jit(solution)/shard_map/all_to_all | solution.py:197
  86.1 5.6 %partials.1 = s16[128,3200]{1,0:T(8,128)(2,1)S(1)} custom-call(s32[1]{0:T(128)} %bitcast.place_ref, bf16[4,128,896]{2,1,0:T(8,128)(2,1)} %all-to-all-done.1.rows_ref, bf16[672,1024]{1,0:T(8,128)(2,1)S(1)} %get-tuple-element.19.refs_0_, bf16[672,1024]{1,0:T(8,128)(2,1)} %collective-permute-done.refs_1_, bf16[672,1024]{1,0:T(8,128)(2,1)} %collective-permute-done.1.refs_2_, ...), custom_call_target="tpu_custom_call" | custom-call | tf_op jit(solution)/shard_map/partials/pallas_call | solution.py:253
  91.8 12.0 %all_to_all.30.refs_0_ = s16[4,32,3200]{2,1,0:T(8,128)(2,1)S(1)} all-to-all(s16[4,32,3200]{2,1,0:T(8,128)(2,1)S(1)} %bitcast.23), channel_id=1, replica_groups={{0,1,2,3},{4,5,6,7},{8,9,10,11},{12,13,14,15},{16,20,24,28},{17,21,25,2..., dimensions={0} | all-to-all | bytes 1638400 | tf_op jit(solution)/shard_map/all_to_all | solution.py:197
  103.8 0.3 local_grads.1
  104.1 9.3 %all_to_all.31 = bf16[4,32,2048]{2,1,0:T(8,128)(2,1)S(1)} all-to-all(bf16[4,32,2048]{2,1,0:T(8,128)(2,1)S(1)} %local_grads.1), channel_id=1, replica_groups={{0,1,2,3},{4,5,6,7},{8,9,10,11},{12,13,14,15},{16,20,24,28},{17,21,25,2..., dimensions={0} | all-to-all | bytes 1048576 | tf_op jit(solution)/shard_map/all_to_all | solution.py:197
  113.4 6.6 %row_grads.1 = bf16[4,64,896]{2,1,0:T(8,128)(2,1)S(1)} custom-call(s32[1]{0:T(128)} %bitcast.place_ref, bf16[128,2048]{1,0:T(8,128)(2,1)S(1)} %bitcast.17, bf16[672,1024]{1,0:T(8,128)(2,1)S(1)} %get-tuple-element.19.refs_0_, bf16[672,1024]{1,0:T(8,128)(2,1)} %collective-permute-done.refs_1_, bf16[672,1024]{1,0:T(8,128)(2,1)} %collective-permute-done.1.refs_2_, ...), custom_call_target="tpu_custom_call" | custom-call | tf_op jit(solution)/shard_map/row_grads/pallas_call | solution.py:269
  120.1 9.7 %all_to_all.32 = bf16[4,64,896]{2,1,0:T(8,128)(2,1)} all-to-all(bf16[4,64,896]{2,1,0:T(8,128)(2,1)S(1)} %row_grads.1), channel_id=1, replica_groups={{0,4,8,12},{1,5,9,13},{2,6,10,14},{3,7,11,15},{16,17,18,19},{20,21,22,2..., dimensions={0} | all-to-all | bytes 917504 | tf_op jit(solution)/shard_map/all_to_all | solution.py:197
  129.8 15.4 %all-to-all-start.5 = ((bf16[32,8,896]{2,1,0:T(8,128)(2,1)}), bf16[32,8,896]{2,1,0:T(8,128)(2,1)S(1)}, u32[]{:S(2)}, u32[]{:S(2)}) async-start(bf16[32,8,896]{2,1,0:T(8,128)(2,1)} %bitcast.13), calls=%async_computation.5 | async-start | bytes 917504 | tf_op jit(solution)/shard_map/all_to_all | solution.py:278
  145.2 2.5 %collective-permute-start.8 = (bf16[128,2048]{1,0:T(8,128)(2,1)S(1)}, bf16[128,2048]{1,0:T(8,128)(2,1)S(1)}, u32[]{:S(2)}, u32[]{:S(2)}) collective-permute-start(bf16[128,2048]{1,0:T(8,128)(2,1)S(1)} %bitcast.18), channel_id=1, source_target_pairs={{0,8},{4,12},{8,0},{12,4},{1,9},{5,13},{9,1},{13,5},{2,10},{6,14},... | collective-permute-start | bytes 1572872 | tf_op jit(solution)/shard_map/ppermute | solution.py:286
  147.6 4.0 %collective-permute-start.7 = (bf16[128,2048]{1,0:T(8,128)(2,1)S(1)}, bf16[128,2048]{1,0:T(8,128)(2,1)S(1)}, u32[]{:S(2)}, u32[]{:S(2)}) collective-permute-start(bf16[128,2048]{1,0:T(8,128)(2,1)S(1)} %bitcast.19), channel_id=1, source_target_pairs={{0,12},{4,0},{8,4},{12,8},{1,13},{5,1},{9,5},{13,9},{2,14},{6,2},{... | collective-permute-start | bytes 1572872 | tf_op jit(solution)/shard_map/ppermute | solution.py:286
  151.7 1.9 %collective-permute-start.6 = (bf16[128,2048]{1,0:T(8,128)(2,1)S(1)}, bf16[128,2048]{1,0:T(8,128)(2,1)S(1)}, u32[]{:S(2)}, u32[]{:S(2)}) collective-permute-start(bf16[128,2048]{1,0:T(8,128)(2,1)S(1)} %bitcast.20), channel_id=1, source_target_pairs={{0,4},{4,8},{8,12},{12,0},{1,5},{5,9},{9,13},{13,1},{2,6},{6,10},{... | collective-permute-start | bytes 1572872 | tf_op jit(solution)/shard_map/ppermute | solution.py:286
  153.6 3.3 %collective-permute-done.8.refs_3_ = bf16[128,2048]{1,0:T(8,128)(2,1)S(1)} collective-permute-done((bf16[128,2048]{1,0:T(8,128)(2,1)S(1)}, bf16[128,2048]{1,0:T(8,128)(2,1)S(1)}, u32[]{:S(2)}, u32[]{:S(2)}) %collective-permute-start.8) | collective-permute-done | bytes 524320 | tf_op jit(solution)/shard_map/ppermute | solution.py:286
  156.9 4.2 %collective-permute-done.7.refs_2_ = bf16[128,2048]{1,0:T(8,128)(2,1)S(1)} collective-permute-done((bf16[128,2048]{1,0:T(8,128)(2,1)S(1)}, bf16[128,2048]{1,0:T(8,128)(2,1)S(1)}, u32[]{:S(2)}, u32[]{:S(2)}) %collective-permute-start.7) | collective-permute-done | bytes 524320 | tf_op jit(solution)/shard_map/ppermute | solution.py:286
  161.0 2.1 %collective-permute-done.6.refs_1_ = bf16[128,2048]{1,0:T(8,128)(2,1)S(1)} collective-permute-done((bf16[128,2048]{1,0:T(8,128)(2,1)S(1)}, bf16[128,2048]{1,0:T(8,128)(2,1)S(1)}, u32[]{:S(2)}, u32[]{:S(2)}) %collective-permute-start.6) | collective-permute-done | bytes 524320 | tf_op jit(solution)/shard_map/ppermute | solution.py:286
  163.1 3.4 %weight_grad.3 = bf16[1,448,1024]{2,1,0:T(8,128)(2,1)} custom-call(s32[1]{0:T(128)} %bitcast.place_ref, bf16[4,128,896]{2,1,0:T(8,128)(2,1)} %bitcast.10.rows_ref, bf16[128,2048]{1,0:T(8,128)(2,1)S(1)} %bitcast.21, bf16[128,2048]{1,0:T(8,128)(2,1)S(1)} %collective-permute-done.6.refs_1_, bf16[128,2048]{1,0:T(8,128)(2,1)S(1)} %collective-permute-done.7.refs_2_, ...), custom_call_target="tpu_custom_call" | custom-call | tf_op jit(solution)/shard_map/weight_grad/pallas_call | solution.py:291
  166.5 3.3 %weight_grad.2 = bf16[1,448,1024]{2,1,0:T(8,128)(2,1)} custom-call(s32[1]{0:T(128)} %bitcast.place_ref, bf16[4,128,896]{2,1,0:T(8,128)(2,1)} %bitcast.10.rows_ref, bf16[128,2048]{1,0:T(8,128)(2,1)S(1)} %bitcast.22, bf16[128,2048]{1,0:T(8,128)(2,1)S(1)} %collective-permute-done.6.refs_1_, bf16[128,2048]{1,0:T(8,128)(2,1)S(1)} %collective-permute-done.7.refs_2_, ...), custom_call_target="tpu_custom_call" | custom-call | tf_op jit(solution)/shard_map/weight_grad/pallas_call | solution.py:291
  169.8 6.1 %all-to-all-done.5 = bf16[32,8,896]{2,1,0:T(8,128)(2,1)S(1)} async-done(((bf16[32,8,896]{2,1,0:T(8,128)(2,1)}), bf16[32,8,896]{2,1,0:T(8,128)(2,1)S(1)}, u32[]{:S(2)}, u32[]{:S(2)}) %all-to-all-start.5) | async-done | bytes 458784 | tf_op jit(solution)/shard_map/all_to_all | solution.py:278
  175.9 1.1 combine.1
Async XLA Ops:
  0.6 0.9 copy-start.3
  1.6 0.9 copy-start.4
  2.5 0.7 copy-start.5
  3.2 0.7 copy-start.6
  5.5 67.0 %all-to-all-start = ((bf16[32,16,896]{2,1,0:T(8,128)(2,1)}), bf16[32,16,896]{2,1,0:T(8,128)(2,1)}, u32[]{:S(2)}, u32[]{:S(2)}) async-start(bf16[32,16,896]{2,1,0:T(8,128)(2,1)} %bitcast.9), calls=%async_computation | async-start | bytes 1835008 | tf_op jit(solution)/shard_map/all_to_all | solution.py:246
  22.3 1.2 copy-start
  23.5 1.2 copy-start.1
  24.6 1.2 copy-start.2
  26.0 20.7 %collective-permute-start = (bf16[672,1024]{1,0:T(8,128)(2,1)S(1)}, bf16[672,1024]{1,0:T(8,128)(2,1)}, u32[]{:S(2)}, u32[]{:S(2)}) collective-permute-start(bf16[672,1024]{1,0:T(8,128)(2,1)S(1)} %get-tuple-element.19.refs_0_), channel_id=1, source_target_pairs={{0,4},{4,8},{8,12},{12,0},{1,5},{5,9},{9,13},{13,1},{2,6},{6,10},{... | collective-permute-start | bytes 4128776 | tf_op jit(solution)/shard_map/ppermute | solution.py:239
  29.2 19.5 %collective-permute-start.4 = (bf16[672,1024]{1,0:T(8,128)(2,1)S(1)}, bf16[672,1024]{1,0:T(8,128)(2,1)}, u32[]{:S(2)}, u32[]{:S(2)}) collective-permute-start(bf16[672,1024]{1,0:T(8,128)(2,1)S(1)} %get-tuple-element.20.refs_4_), channel_id=1, source_target_pairs={{0,12},{4,0},{8,4},{12,8},{1,13},{5,1},{9,5},{13,9},{2,14},{6,2},{... | collective-permute-start | bytes 4128776 | tf_op jit(solution)/shard_map/ppermute | solution.py:240
  32.6 44.2 %collective-permute-start.1 = (bf16[672,1024]{1,0:T(8,128)(2,1)S(1)}, bf16[672,1024]{1,0:T(8,128)(2,1)}, u32[]{:S(2)}, u32[]{:S(2)}) collective-permute-start(bf16[672,1024]{1,0:T(8,128)(2,1)S(1)} %get-tuple-element.19.refs_0_), channel_id=1, source_target_pairs={{0,12},{4,0},{8,4},{12,8},{1,13},{5,1},{9,5},{13,9},{2,14},{6,2},{... | collective-permute-start | bytes 4128776 | tf_op jit(solution)/shard_map/ppermute | solution.py:242
  35.9 40.8 %collective-permute-start.3 = (bf16[672,1024]{1,0:T(8,128)(2,1)S(1)}, bf16[672,1024]{1,0:T(8,128)(2,1)}, u32[]{:S(2)}, u32[]{:S(2)}) collective-permute-start(bf16[672,1024]{1,0:T(8,128)(2,1)S(1)} %get-tuple-element.20.refs_4_), channel_id=1, source_target_pairs={{0,4},{4,8},{8,12},{12,0},{1,5},{5,9},{9,13},{13,1},{2,6},{6,10},{... | collective-permute-start | bytes 4128776 | tf_op jit(solution)/shard_map/ppermute | solution.py:241
  46.7 30.1 %collective-permute-start.2 = (bf16[672,1024]{1,0:T(8,128)(2,1)}, bf16[672,1024]{1,0:T(8,128)(2,1)}, u32[]{:S(2)}, u32[]{:S(2)}) collective-permute-start(bf16[672,1024]{1,0:T(8,128)(2,1)} %collective-permute-done.refs_1_), channel_id=1, source_target_pairs={{0,4},{4,8},{8,12},{12,0},{1,5},{5,9},{9,13},{13,1},{2,6},{6,10},{... | collective-permute-start | bytes 4128776 | tf_op jit(solution)/shard_map/ppermute | solution.py:243
  48.7 29.5 %collective-permute-start.5 = (bf16[672,1024]{1,0:T(8,128)(2,1)}, bf16[672,1024]{1,0:T(8,128)(2,1)}, u32[]{:S(2)}, u32[]{:S(2)}) collective-permute-start(bf16[672,1024]{1,0:T(8,128)(2,1)} %collective-permute-done.4.refs_6_), channel_id=1, source_target_pairs={{0,12},{4,0},{8,4},{12,8},{1,13},{5,1},{9,5},{13,9},{2,14},{6,2},{... | collective-permute-start | bytes 4128776 | tf_op jit(solution)/shard_map/ppermute | solution.py:244
  72.5 13.6 %all-to-all-start.1 = ((bf16[4,128,896]{2,1,0:T(8,128)(2,1)}), bf16[4,128,896]{2,1,0:T(8,128)(2,1)}, u32[]{:S(2)}, u32[]{:S(2)}) async-start(bf16[4,128,896]{2,1,0:T(8,128)(2,1)} %bitcast.10.rows_ref), calls=%async_computation.1 | async-start | bytes 1835008 | tf_op jit(solution)/shard_map/all_to_all | solution.py:197
  129.8 46.1 %all-to-all-start.5 = ((bf16[32,8,896]{2,1,0:T(8,128)(2,1)}), bf16[32,8,896]{2,1,0:T(8,128)(2,1)S(1)}, u32[]{:S(2)}, u32[]{:S(2)}) async-start(bf16[32,8,896]{2,1,0:T(8,128)(2,1)} %bitcast.13), calls=%async_computation.5 | async-start | bytes 917504 | tf_op jit(solution)/shard_map/all_to_all | solution.py:278
  145.2 11.7 %collective-permute-start.8 = (bf16[128,2048]{1,0:T(8,128)(2,1)S(1)}, bf16[128,2048]{1,0:T(8,128)(2,1)S(1)}, u32[]{:S(2)}, u32[]{:S(2)}) collective-permute-start(bf16[128,2048]{1,0:T(8,128)(2,1)S(1)} %bitcast.18), channel_id=1, source_target_pairs={{0,8},{4,12},{8,0},{12,4},{1,9},{5,13},{9,1},{13,5},{2,10},{6,14},... | collective-permute-start | bytes 1572872 | tf_op jit(solution)/shard_map/ppermute | solution.py:286
  147.6 13.4 %collective-permute-start.7 = (bf16[128,2048]{1,0:T(8,128)(2,1)S(1)}, bf16[128,2048]{1,0:T(8,128)(2,1)S(1)}, u32[]{:S(2)}, u32[]{:S(2)}) collective-permute-start(bf16[128,2048]{1,0:T(8,128)(2,1)S(1)} %bitcast.19), channel_id=1, source_target_pairs={{0,12},{4,0},{8,4},{12,8},{1,13},{5,1},{9,5},{13,9},{2,14},{6,2},{... | collective-permute-start | bytes 1572872 | tf_op jit(solution)/shard_map/ppermute | solution.py:286
  151.7 11.4 %collective-permute-start.6 = (bf16[128,2048]{1,0:T(8,128)(2,1)S(1)}, bf16[128,2048]{1,0:T(8,128)(2,1)S(1)}, u32[]{:S(2)}, u32[]{:S(2)}) collective-permute-start(bf16[128,2048]{1,0:T(8,128)(2,1)S(1)} %bitcast.20), channel_id=1, source_target_pairs={{0,4},{4,8},{8,12},{12,0},{1,5},{5,9},{9,13},{13,1},{2,6},{6,10},{... | collective-permute-start | bytes 1572872 | tf_op jit(solution)/shard_map/ppermute | solution.py:286

commit v5 on v4

--- a/solution.py
+++ b/solution.py
@@ -98,9 +98,24 @@
     return totals
 
 
-def partial_kernel(place_ref, rows_ref, *refs):
-    lows, highs = refs[:SIDE], refs[SIDE : 2 * SIDE]
-    out_ref = refs[2 * SIDE]
+def fetch(arrays, buffers, sems):
+    copies = []
+    for i, (array, buffer) in enumerate(zip(arrays, buffers)):
+        source = array.at[: buffer.shape[0]]
+        copies.append(pltpu.make_async_copy(source, buffer, sems.at[i]))
+        copies[-1].start()
+
+    def ready(i):
+        copies[i].wait()
+        return buffers[i]
+
+    return ready
+
+
+def partial_kernel(place_ref, rows_ref, own_low, own_high, *refs):
+    others = 2 * (SIDE - 1)
+    out_ref = refs[others]
+    ready = fetch(refs[:others], refs[others + 1 : -1], refs[-1])
     width = rows_ref.shape[2] // 2
     half = width // 2
     totals = [None] * 3
@@ -109,12 +124,14 @@
         value = jnp.dot(rows, weight, preferred_element_type=jnp.float32)
         totals[which] = value if totals[which] is None else totals[which] + value
 
-    for shift, low, high in zip(SHIFTS, lows, highs):
+    for i, shift in enumerate(SHIFTS):
         both = block_at(rows_ref, lax.rem(place_ref[0] + shift, SIDE))
         x = both[:, :width]
+        low = own_low if i == 0 else ready(2 * i - 2)
         add(0, x, low[:width])
+        add(2, both[:, width : width + half], low[width:])
+        high = own_high if i == 0 else ready(2 * i - 1)
         add(1, x, high[:width])
-        add(2, both[:, width : width + half], low[width:])
         add(2, both[:, width + half :], high[width:])
     put_coded(out_ref, totals)
 
@@ -129,26 +146,30 @@
         out_ref[p, :, hidden:] = grad_up
 
 
-def row_kernel(place_ref, grads_ref, *refs):
-    lows, highs = refs[:SIDE], refs[SIDE : 2 * SIDE]
-    out_ref = refs[2 * SIDE]
+def row_kernel(place_ref, grads_ref, own_low, own_high, *refs):
+    others = 2 * (SIDE - 1)
+    out_ref = refs[others]
+    ready = fetch(refs[:others], refs[others + 1 : -1], refs[-1])
     wide, hidden = grads_ref.shape[0], grads_ref.shape[1] // 2
     width = out_ref.shape[2] // 2
-    for shift, low, high in zip(SHIFTS, lows, highs):
+    values = []
+    for i in range(SIDE):
+        low = own_low if i == 0 else ready(2 * i - 2)
         total = lax.dot_general(
             grads_ref[:, :hidden], low[:width], ACROSS, preferred_element_type=jnp.float32
-        ) + lax.dot_general(
+        )
+        high = own_high if i == 0 else ready(2 * i - 1)
+        total = total + lax.dot_general(
             grads_ref[:, hidden:], high[:width], ACROSS, preferred_element_type=jnp.float32
         )
         both = total.reshape(-1, 2, CAP // 2, width)
         pair = [both[:, j].reshape(wide // 2, width) for j in (0, 1)]
-        value = jnp.concatenate(pair, axis=1).astype(jnp.bfloat16)
-        at = lax.rem(place_ref[0] + shift, SIDE)
-        for p in range(SIDE):
-
-            @pl.when(at == p)
-            def _():
-                out_ref[p] = value
+        values.append(jnp.concatenate(pair, axis=1).astype(jnp.bfloat16))
+    for p in range(SIDE):
+        block = values[0]
+        for shift, value in zip(SHIFTS[1:], values[1:]):
+            block = jnp.where(lax.rem(place_ref[0] + shift, SIDE) == p, value, block)
+        out_ref[p] = block
 
 
 def weight_kernel(place_ref, rows_ref, *refs):
@@ -209,7 +230,7 @@
     rows = wide // SIDE
     coded = 3 * hidden + 128
     params = pltpu.CompilerParams(vmem_limit_bytes=24 * MIB)
-    alone = pltpu.CompilerParams(vmem_limit_bytes=48 * MIB)
+    alone = pltpu.CompilerParams(vmem_limit_bytes=56 * MIB)
 
     onward, back = plane_ring(held, 1), plane_ring(held, -1)
     dp = lax.axis_index("dp")
@@ -242,7 +263,7 @@
     low_3 = lax.ppermute(low, AXES, back)
     low_2 = lax.ppermute(low_1, AXES, onward)
     high_2 = lax.ppermute(high_3, AXES, back)
-    lows, highs = (low, low_1, low_3, low_2), (high, high_1, high_3, high_2)
+    weights = (low, high, low_1, high_1, low_3, high_3, low_2, high_2)
     recv = lax.all_to_all(
         send.reshape(held, CAP, 2 * width), "expert", split_axis=0, concat_axis=0, tiled=True
     ).reshape(slots, 2 * width)
@@ -250,14 +271,18 @@
     mine = exchange(recv.reshape(SIDE, wide, 2 * width), first)
     vmem = pl.BlockSpec(memory_space=pltpu.VMEM)
     smem = pl.BlockSpec(memory_space=pltpu.SMEM)
+    anywhere = pl.BlockSpec(memory_space=pl.ANY)
+    others = 2 * (SIDE - 1)
     sums = pl.pallas_call(
         partial_kernel,
-        in_specs=[smem] + [vmem] * (1 + 2 * SIDE),
+        in_specs=[smem] + [vmem] * 3 + [anywhere] * others,
         out_specs=vmem,
         out_shape=jax.ShapeDtypeStruct((wide, coded), jnp.int16),
+        scratch_shapes=[pltpu.VMEM((width + width // 2, hidden), jnp.bfloat16)] * others
+        + [pltpu.SemaphoreType.DMA((others,))],
         compiler_params=params,
         name="partials",
-    )(place, mine, *lows, *highs)
+    )(place, mine, *weights)
     sums = exchange(sums.reshape(SIDE, rows, coded), second)
     grads = pl.pallas_call(
         lambda *refs: local_kernel(hidden, *refs),
@@ -268,12 +293,14 @@
     grads = exchange(grads, second).reshape(wide, 2 * hidden)
     row_grads = pl.pallas_call(
         row_kernel,
-        in_specs=[smem] + [vmem] * (1 + 2 * SIDE),
+        in_specs=[smem] + [vmem] * 3 + [anywhere] * others,
         out_specs=vmem,
         out_shape=jax.ShapeDtypeStruct((SIDE, wide // 2, 2 * width), jnp.bfloat16),
+        scratch_shapes=[pltpu.VMEM((width, hidden), jnp.bfloat16)] * others
+        + [pltpu.SemaphoreType.DMA((others,))],
         compiler_params=params,
         name="row_grads",
-    )(place, grads, *lows, *highs)
+    )(place, grads, *weights)
     row_grads = exchange(row_grads, first)
     returned = lax.all_to_all(
         row_grads.reshape(held, CAP // 2, 2 * width),

time: 178 us -> 173 us (0.972)
  local copies, waits for them, and re-layouts: 6.79 us -> 3.53 us
    unnamed x14 -> x8, local copies, waits for them, and re-layouts: 6.79 us -> 3.53 us
    pallas_call x2, Pallas kernels: 12.3 us -> 9.88 us  [the longest x1 5.22 us: body(): pl.pallas_call(partial_kernel, in_specs=[smem] + [vmem] * 3 + [anywhere]...]
where the time goes in v5:
time: 173 us; the launch traced here: 172 us
  starting transfers between devices  63.2 us (37%)
  waiting for transfers between devices  53.1 us (31%)
  blocking collectives  31 us (18%)
  Pallas kernels  20.8 us (12%)
  local copies, waits for them, and re-layouts  3.53 us (2%)
    all_to_all x3, blocking collectives, exchange(): lax.all_to_all(blocks, AXES, split_axis=0, concat_axis=0, tiled=True, axi...  31 us
    all_to_all x1, waiting for transfers between devices, body(): lax.all_to_all(send.reshape(held, CAP, 2 * width), 'expert', split_axis=0...  19.3 us
    all_to_all x1, starting transfers between devices, body(): lax.all_to_all(send.reshape(held, CAP, 2 * width), 'expert', split_axis=0...  16.8 us
    all_to_all x1, starting transfers between devices, body(): lax.all_to_all(row_grads.reshape(held, CAP // 2, 2 * width), 'expert', sp...  15.4 us
    ppermute x3, waiting for transfers between devices, body(): lax.ppermute(grads, AXES, plane_ring(held, k))  9.5 us
    ppermute x1, waiting for transfers between devices, body(): low_1 = lax.ppermute(low, AXES, onward)  8.85 us
    ppermute x3, starting transfers between devices, body(): lax.ppermute(grads, AXES, plane_ring(held, k))  8.42 us
    all_to_all x1, waiting for transfers between devices, exchange(): lax.all_to_all(blocks, AXES, split_axis=0, concat_axis=0, tiled=True, axi...  7.99 us
  transfers between devices with their start and end apart: 12, of which 8 were waited for; matrix products, arithmetic and copies ran while one was open for 0% of the time, Pallas kernels for 4%

profile of v5, /device:TPU:1, one launch (start us, length us, event | category | flops | bytes accessed | tf_op | source)
XLA Modules:
  0.0 172.5 jit_solution(13112784581830423556)
XLA Ops:
  0.6 2.6 %dispatch.1 = (bf16[512,896]{1,0:T(8,128)(2,1)}, bf16[2,256,256]{2,1,0:T(8,128)(2,1)}) custom-call(s32[8,256]{1,0:T(8,128)} %bitcast.32, f32[8,256]{1,0:T(8,128)} %bitcast.33, bf16[448,256]{1,0:T(8,128)(2,1)} %bitcast.29, bf16[448,256]{1,0:T(8,128)(2,1)} %bitcast.30), custom_call_target="tpu_custom_call" | custom-call | tf_op jit(solution)/shard_map/dispatch/pallas_call | solution.py:240
  3.3 16.8 %all-to-all-start = ((bf16[32,16,896]{2,1,0:T(8,128)(2,1)}), bf16[32,16,896]{2,1,0:T(8,128)(2,1)}, u32[]{:S(2)}, u32[]{:S(2)}) async-start(bf16[32,16,896]{2,1,0:T(8,128)(2,1)} %bitcast.28), calls=%async_computation | async-start | bytes 1835008 | tf_op jit(solution)/shard_map/all_to_all | solution.py:267
  20.1 0.0 copy-start
  20.1 1.2 copy-done
  21.3 0.0 copy-start.1
  21.3 1.2 copy-done.1
  22.4 0.0 copy-start.2
  22.4 1.2 copy-done.2
  23.6 0.2 pack.1
  23.8 3.2 %collective-permute-start = (bf16[672,1024]{1,0:T(8,128)(2,1)S(1)}, bf16[672,1024]{1,0:T(8,128)(2,1)}, u32[]{:S(2)}, u32[]{:S(2)}) collective-permute-start(bf16[672,1024]{1,0:T(8,128)(2,1)S(1)} %get-tuple-element.19.own_low), channel_id=1, source_target_pairs={{0,4},{4,8},{8,12},{12,0},{1,5},{5,9},{9,13},{13,1},{2,6},{6,10},{... | collective-permute-start | bytes 4128776 | tf_op jit(solution)/shard_map/ppermute | solution.py:260
  27.0 3.4 %collective-permute-start.3 = (bf16[672,1024]{1,0:T(8,128)(2,1)S(1)}, bf16[672,1024]{1,0:T(8,128)(2,1)}, u32[]{:S(2)}, u32[]{:S(2)}) collective-permute-start(bf16[672,1024]{1,0:T(8,128)(2,1)S(1)} %get-tuple-element.20.own_high), channel_id=1, source_target_pairs={{0,12},{4,0},{8,4},{12,8},{1,13},{5,1},{9,5},{13,9},{2,14},{6,2},{... | collective-permute-start | bytes 4128776 | tf_op jit(solution)/shard_map/ppermute | solution.py:261
  30.4 3.4 %collective-permute-start.2 = (bf16[672,1024]{1,0:T(8,128)(2,1)S(1)}, bf16[672,1024]{1,0:T(8,128)(2,1)}, u32[]{:S(2)}, u32[]{:S(2)}) collective-permute-start(bf16[672,1024]{1,0:T(8,128)(2,1)S(1)} %get-tuple-element.19.own_low), channel_id=1, source_target_pairs={{0,12},{4,0},{8,4},{12,8},{1,13},{5,1},{9,5},{13,9},{2,14},{6,2},{... | collective-permute-start | bytes 4128776 | tf_op jit(solution)/shard_map/ppermute | solution.py:263
  33.8 1.9 %collective-permute-start.1 = (bf16[672,1024]{1,0:T(8,128)(2,1)S(1)}, bf16[672,1024]{1,0:T(8,128)(2,1)}, u32[]{:S(2)}, u32[]{:S(2)}) collective-permute-start(bf16[672,1024]{1,0:T(8,128)(2,1)S(1)} %get-tuple-element.20.own_high), channel_id=1, source_target_pairs={{0,4},{4,8},{8,12},{12,0},{1,5},{5,9},{9,13},{13,1},{2,6},{6,10},{... | collective-permute-start | bytes 4128776 | tf_op jit(solution)/shard_map/ppermute | solution.py:262
  35.7 8.9 %collective-permute-done.refs_0_ = bf16[672,1024]{1,0:T(8,128)(2,1)} collective-permute-done((bf16[672,1024]{1,0:T(8,128)(2,1)S(1)}, bf16[672,1024]{1,0:T(8,128)(2,1)}, u32[]{:S(2)}, u32[]{:S(2)}) %collective-permute-start) | collective-permute-done | bytes 1376288 | tf_op jit(solution)/shard_map/ppermute | solution.py:260
  44.5 1.9 %collective-permute-start.4 = (bf16[672,1024]{1,0:T(8,128)(2,1)}, bf16[672,1024]{1,0:T(8,128)(2,1)}, u32[]{:S(2)}, u32[]{:S(2)}) collective-permute-start(bf16[672,1024]{1,0:T(8,128)(2,1)} %collective-permute-done.refs_0_), channel_id=1, source_target_pairs={{0,4},{4,8},{8,12},{12,0},{1,5},{5,9},{9,13},{13,1},{2,6},{6,10},{... | collective-permute-start | bytes 4128776 | tf_op jit(solution)/shard_map/ppermute | solution.py:264
  46.5 0.0 collective-permute-done.3.refs_3_
  46.5 4.6 %collective-permute-start.5 = (bf16[672,1024]{1,0:T(8,128)(2,1)}, bf16[672,1024]{1,0:T(8,128)(2,1)}, u32[]{:S(2)}, u32[]{:S(2)}) collective-permute-start(bf16[672,1024]{1,0:T(8,128)(2,1)} %collective-permute-done.3.refs_3_), channel_id=1, source_target_pairs={{0,12},{4,0},{8,4},{12,8},{1,13},{5,1},{9,5},{13,9},{2,14},{6,2},{... | collective-permute-start | bytes 4128776 | tf_op jit(solution)/shard_map/ppermute | solution.py:265
  51.0 19.3 %all-to-all-done = bf16[32,16,896]{2,1,0:T(8,128)(2,1)} async-done(((bf16[32,16,896]{2,1,0:T(8,128)(2,1)}), bf16[32,16,896]{2,1,0:T(8,128)(2,1)}, u32[]{:S(2)}, u32[]{:S(2)}) %all-to-all-start) | async-done | bytes 917536 | tf_op jit(solution)/shard_map/all_to_all | solution.py:267
  70.3 4.2 %all-to-all-start.1 = ((bf16[4,128,896]{2,1,0:T(8,128)(2,1)}), bf16[4,128,896]{2,1,0:T(8,128)(2,1)}, u32[]{:S(2)}, u32[]{:S(2)}) async-start(bf16[4,128,896]{2,1,0:T(8,128)(2,1)} %bitcast.10.rows_ref), calls=%async_computation.1 | async-start | bytes 1835008 | tf_op jit(solution)/shard_map/all_to_all | solution.py:218
  74.6 0.0 collective-permute-done.2.refs_2_
  74.6 0.0 collective-permute-done.1.refs_1_
  74.6 0.0 collective-permute-done.4.refs_4_
  74.6 1.4 collective-permute-done.5.refs_5_
  76.0 8.0 %all-to-all-done.1.rows_ref = bf16[4,128,896]{2,1,0:T(8,128)(2,1)} async-done(((bf16[4,128,896]{2,1,0:T(8,128)(2,1)}), bf16[4,128,896]{2,1,0:T(8,128)(2,1)}, u32[]{:S(2)}, u32[]{:S(2)}) %all-to-all-start.1) | async-done | bytes 917536 | tf_op jit(solution)/shard_map/all_to_all | solution.py:218
  84.0 5.2 %partials.1 = s16[128,3200]{1,0:T(8,128)(2,1)S(1)} custom-call(s32[1]{0:T(128)} %bitcast.place_ref, bf16[4,128,896]{2,1,0:T(8,128)(2,1)} %all-to-all-done.1.rows_ref, bf16[672,1024]{1,0:T(8,128)(2,1)S(1)} %get-tuple-element.19.own_low, bf16[672,1024]{1,0:T(8,128)(2,1)S(1)} %get-tuple-element.20.own_high, bf16[672,1024]{1,0:T(8,128)(2,1)} %collective-permute-done.refs_0_, ...), custom_call_target="tpu_custom_call" | custom-call | tf_op jit(solution)/shard_map/partials/pallas_call | solution.py:276
  89.2 12.0 %all_to_all.30.refs_0_ = s16[4,32,3200]{2,1,0:T(8,128)(2,1)S(1)} all-to-all(s16[4,32,3200]{2,1,0:T(8,128)(2,1)S(1)} %bitcast.23), channel_id=1, replica_groups={{0,1,2,3},{4,5,6,7},{8,9,10,11},{12,13,14,15},{16,20,24,28},{17,21,25,2..., dimensions={0} | all-to-all | bytes 1638400 | tf_op jit(solution)/shard_map/all_to_all | solution.py:218
  101.2 0.3 local_grads.1
  101.5 9.3 %all_to_all.31 = bf16[4,32,2048]{2,1,0:T(8,128)(2,1)S(1)} all-to-all(bf16[4,32,2048]{2,1,0:T(8,128)(2,1)S(1)} %local_grads.1), channel_id=1, replica_groups={{0,1,2,3},{4,5,6,7},{8,9,10,11},{12,13,14,15},{16,20,24,28},{17,21,25,2..., dimensions={0} | all-to-all | bytes 1048576 | tf_op jit(solution)/shard_map/all_to_all | solution.py:218
  110.8 4.7 %row_grads.1 = bf16[4,64,896]{2,1,0:T(8,128)(2,1)S(1)} custom-call(s32[1]{0:T(128)} %bitcast.place_ref, bf16[128,2048]{1,0:T(8,128)(2,1)S(1)} %bitcast.17, bf16[672,1024]{1,0:T(8,128)(2,1)S(1)} %get-tuple-element.19.own_low, bf16[672,1024]{1,0:T(8,128)(2,1)S(1)} %get-tuple-element.20.own_high, bf16[672,1024]{1,0:T(8,128)(2,1)} %collective-permute-done.refs_0_, ...), custom_call_target="tpu_custom_call" | custom-call | tf_op jit(solution)/shard_map/row_grads/pallas_call | solution.py:294
  115.5 9.7 %all_to_all.32 = bf16[4,64,896]{2,1,0:T(8,128)(2,1)} all-to-all(bf16[4,64,896]{2,1,0:T(8,128)(2,1)S(1)} %row_grads.1), channel_id=1, replica_groups={{0,4,8,12},{1,5,9,13},{2,6,10,14},{3,7,11,15},{16,17,18,19},{20,21,22,2..., dimensions={0} | all-to-all | bytes 917504 | tf_op jit(solution)/shard_map/all_to_all | solution.py:218
  125.2 15.4 %all-to-all-start.5 = ((bf16[32,8,896]{2,1,0:T(8,128)(2,1)}), bf16[32,8,896]{2,1,0:T(8,128)(2,1)S(1)}, u32[]{:S(2)}, u32[]{:S(2)}) async-start(bf16[32,8,896]{2,1,0:T(8,128)(2,1)} %bitcast.13), calls=%async_computation.5 | async-start | bytes 917504 | tf_op jit(solution)/shard_map/all_to_all | solution.py:305
  140.6 2.4 %collective-permute-start.8 = (bf16[128,2048]{1,0:T(8,128)(2,1)S(1)}, bf16[128,2048]{1,0:T(8,128)(2,1)S(1)}, u32[]{:S(2)}, u32[]{:S(2)}) collective-permute-start(bf16[128,2048]{1,0:T(8,128)(2,1)S(1)} %bitcast.18), channel_id=1, source_target_pairs={{0,8},{4,12},{8,0},{12,4},{1,9},{5,13},{9,1},{13,5},{2,10},{6,14},... | collective-permute-start | bytes 1572872 | tf_op jit(solution)/shard_map/ppermute | solution.py:313
  143.0 4.0 %collective-permute-start.7 = (bf16[128,2048]{1,0:T(8,128)(2,1)S(1)}, bf16[128,2048]{1,0:T(8,128)(2,1)S(1)}, u32[]{:S(2)}, u32[]{:S(2)}) collective-permute-start(bf16[128,2048]{1,0:T(8,128)(2,1)S(1)} %bitcast.19), channel_id=1, source_target_pairs={{0,12},{4,0},{8,4},{12,8},{1,13},{5,1},{9,5},{13,9},{2,14},{6,2},{... | collective-permute-start | bytes 1572872 | tf_op jit(solution)/shard_map/ppermute | solution.py:313
  147.1 1.9 %collective-permute-start.6 = (bf16[128,2048]{1,0:T(8,128)(2,1)S(1)}, bf16[128,2048]{1,0:T(8,128)(2,1)S(1)}, u32[]{:S(2)}, u32[]{:S(2)}) collective-permute-start(bf16[128,2048]{1,0:T(8,128)(2,1)S(1)} %bitcast.20), channel_id=1, source_target_pairs={{0,4},{4,8},{8,12},{12,0},{1,5},{5,9},{9,13},{13,1},{2,6},{6,10},{... | collective-permute-start | bytes 1572872 | tf_op jit(solution)/shard_map/ppermute | solution.py:313
  149.0 3.3 %collective-permute-done.8.refs_3_ = bf16[128,2048]{1,0:T(8,128)(2,1)S(1)} collective-permute-done((bf16[128,2048]{1,0:T(8,128)(2,1)S(1)}, bf16[128,2048]{1,0:T(8,128)(2,1)S(1)}, u32[]{:S(2)}, u32[]{:S(2)}) %collective-permute-start.8) | collective-permute-done | bytes 524320 | tf_op jit(solution)/shard_map/ppermute | solution.py:313
  152.3 4.2 %collective-permute-done.7.refs_2_ = bf16[128,2048]{1,0:T(8,128)(2,1)S(1)} collective-permute-done((bf16[128,2048]{1,0:T(8,128)(2,1)S(1)}, bf16[128,2048]{1,0:T(8,128)(2,1)S(1)}, u32[]{:S(2)}, u32[]{:S(2)}) %collective-permute-start.7) | collective-permute-done | bytes 524320 | tf_op jit(solution)/shard_map/ppermute | solution.py:313
  156.5 2.1 %collective-permute-done.6.refs_1_ = bf16[128,2048]{1,0:T(8,128)(2,1)S(1)} collective-permute-done((bf16[128,2048]{1,0:T(8,128)(2,1)S(1)}, bf16[128,2048]{1,0:T(8,128)(2,1)S(1)}, u32[]{:S(2)}, u32[]{:S(2)}) %collective-permute-start.6) | collective-permute-done | bytes 524320 | tf_op jit(solution)/shard_map/ppermute | solution.py:313
  158.5 3.4 %weight_grad.3 = bf16[1,448,1024]{2,1,0:T(8,128)(2,1)} custom-call(s32[1]{0:T(128)} %bitcast.place_ref, bf16[4,128,896]{2,1,0:T(8,128)(2,1)} %bitcast.10.rows_ref, bf16[128,2048]{1,0:T(8,128)(2,1)S(1)} %bitcast.21, bf16[128,2048]{1,0:T(8,128)(2,1)S(1)} %collective-permute-done.6.refs_1_, bf16[128,2048]{1,0:T(8,128)(2,1)S(1)} %collective-permute-done.7.refs_2_, ...), custom_call_target="tpu_custom_call" | custom-call | tf_op jit(solution)/shard_map/weight_grad/pallas_call | solution.py:318
  161.9 0.0 copy-start.3
  161.9 3.4 %weight_grad.2 = bf16[1,448,1024]{2,1,0:T(8,128)(2,1)} custom-call(s32[1]{0:T(128)} %bitcast.place_ref, bf16[4,128,896]{2,1,0:T(8,128)(2,1)} %bitcast.10.rows_ref, bf16[128,2048]{1,0:T(8,128)(2,1)S(1)} %bitcast.22, bf16[128,2048]{1,0:T(8,128)(2,1)S(1)} %collective-permute-done.6.refs_1_, bf16[128,2048]{1,0:T(8,128)(2,1)S(1)} %collective-permute-done.7.refs_2_, ...), custom_call_target="tpu_custom_call" | custom-call | tf_op jit(solution)/shard_map/weight_grad/pallas_call | solution.py:318
  165.3 6.1 %all-to-all-done.5 = bf16[32,8,896]{2,1,0:T(8,128)(2,1)S(1)} async-done(((bf16[32,8,896]{2,1,0:T(8,128)(2,1)}), bf16[32,8,896]{2,1,0:T(8,128)(2,1)S(1)}, u32[]{:S(2)}, u32[]{:S(2)}) %all-to-all-start.5) | async-done | bytes 458784 | tf_op jit(solution)/shard_map/all_to_all | solution.py:305
  171.3 0.0 copy-done.3
  171.3 1.1 combine.1
Async XLA Ops:
  3.3 67.1 %all-to-all-start = ((bf16[32,16,896]{2,1,0:T(8,128)(2,1)}), bf16[32,16,896]{2,1,0:T(8,128)(2,1)}, u32[]{:S(2)}, u32[]{:S(2)}) async-start(bf16[32,16,896]{2,1,0:T(8,128)(2,1)} %bitcast.28), calls=%async_computation | async-start | bytes 1835008 | tf_op jit(solution)/shard_map/all_to_all | solution.py:267
  20.1 1.2 copy-start
  21.3 1.2 copy-start.1
  22.4 1.2 copy-start.2
  23.8 20.7 %collective-permute-start = (bf16[672,1024]{1,0:T(8,128)(2,1)S(1)}, bf16[672,1024]{1,0:T(8,128)(2,1)}, u32[]{:S(2)}, u32[]{:S(2)}) collective-permute-start(bf16[672,1024]{1,0:T(8,128)(2,1)S(1)} %get-tuple-element.19.own_low), channel_id=1, source_target_pairs={{0,4},{4,8},{8,12},{12,0},{1,5},{5,9},{9,13},{13,1},{2,6},{6,10},{... | collective-permute-start | bytes 4128776 | tf_op jit(solution)/shard_map/ppermute | solution.py:260
  27.0 19.5 %collective-permute-start.3 = (bf16[672,1024]{1,0:T(8,128)(2,1)S(1)}, bf16[672,1024]{1,0:T(8,128)(2,1)}, u32[]{:S(2)}, u32[]{:S(2)}) collective-permute-start(bf16[672,1024]{1,0:T(8,128)(2,1)S(1)} %get-tuple-element.20.own_high), channel_id=1, source_target_pairs={{0,12},{4,0},{8,4},{12,8},{1,13},{5,1},{9,5},{13,9},{2,14},{6,2},{... | collective-permute-start | bytes 4128776 | tf_op jit(solution)/shard_map/ppermute | solution.py:261
  30.4 44.2 %collective-permute-start.2 = (bf16[672,1024]{1,0:T(8,128)(2,1)S(1)}, bf16[672,1024]{1,0:T(8,128)(2,1)}, u32[]{:S(2)}, u32[]{:S(2)}) collective-permute-start(bf16[672,1024]{1,0:T(8,128)(2,1)S(1)} %get-tuple-element.19.own_low), channel_id=1, source_target_pairs={{0,12},{4,0},{8,4},{12,8},{1,13},{5,1},{9,5},{13,9},{2,14},{6,2},{... | collective-permute-start | bytes 4128776 | tf_op jit(solution)/shard_map/ppermute | solution.py:263
  33.8 40.8 %collective-permute-start.1 = (bf16[672,1024]{1,0:T(8,128)(2,1)S(1)}, bf16[672,1024]{1,0:T(8,128)(2,1)}, u32[]{:S(2)}, u32[]{:S(2)}) collective-permute-start(bf16[672,1024]{1,0:T(8,128)(2,1)S(1)} %get-tuple-element.20.own_high), channel_id=1, source_target_pairs={{0,4},{4,8},{8,12},{12,0},{1,5},{5,9},{9,13},{13,1},{2,6},{6,10},{... | collective-permute-start | bytes 4128776 | tf_op jit(solution)/shard_map/ppermute | solution.py:262
  44.5 30.1 %collective-permute-start.4 = (bf16[672,1024]{1,0:T(8,128)(2,1)}, bf16[672,1024]{1,0:T(8,128)(2,1)}, u32[]{:S(2)}, u32[]{:S(2)}) collective-permute-start(bf16[672,1024]{1,0:T(8,128)(2,1)} %collective-permute-done.refs_0_), channel_id=1, source_target_pairs={{0,4},{4,8},{8,12},{12,0},{1,5},{5,9},{9,13},{13,1},{2,6},{6,10},{... | collective-permute-start | bytes 4128776 | tf_op jit(solution)/shard_map/ppermute | solution.py:264
  46.5 29.5 %collective-permute-start.5 = (bf16[672,1024]{1,0:T(8,128)(2,1)}, bf16[672,1024]{1,0:T(8,128)(2,1)}, u32[]{:S(2)}, u32[]{:S(2)}) collective-permute-start(bf16[672,1024]{1,0:T(8,128)(2,1)} %collective-permute-done.3.refs_3_), channel_id=1, source_target_pairs={{0,12},{4,0},{8,4},{12,8},{1,13},{5,1},{9,5},{13,9},{2,14},{6,2},{... | collective-permute-start | bytes 4128776 | tf_op jit(solution)/shard_map/ppermute | solution.py:265
  70.3 13.6 %all-to-all-start.1 = ((bf16[4,128,896]{2,1,0:T(8,128)(2,1)}), bf16[4,128,896]{2,1,0:T(8,128)(2,1)}, u32[]{:S(2)}, u32[]{:S(2)}) async-start(bf16[4,128,896]{2,1,0:T(8,128)(2,1)} %bitcast.10.rows_ref), calls=%async_computation.1 | async-start | bytes 1835008 | tf_op jit(solution)/shard_map/all_to_all | solution.py:218
  125.2 46.2 %all-to-all-start.5 = ((bf16[32,8,896]{2,1,0:T(8,128)(2,1)}), bf16[32,8,896]{2,1,0:T(8,128)(2,1)S(1)}, u32[]{:S(2)}, u32[]{:S(2)}) async-start(bf16[32,8,896]{2,1,0:T(8,128)(2,1)} %bitcast.13), calls=%async_computation.5 | async-start | bytes 917504 | tf_op jit(solution)/shard_map/all_to_all | solution.py:305
  140.6 11.7 %collective-permute-start.8 = (bf16[128,2048]{1,0:T(8,128)(2,1)S(1)}, bf16[128,2048]{1,0:T(8,128)(2,1)S(1)}, u32[]{:S(2)}, u32[]{:S(2)}) collective-permute-start(bf16[128,2048]{1,0:T(8,128)(2,1)S(1)} %bitcast.18), channel_id=1, source_target_pairs={{0,8},{4,12},{8,0},{12,4},{1,9},{5,13},{9,1},{13,5},{2,10},{6,14},... | collective-permute-start | bytes 1572872 | tf_op jit(solution)/shard_map/ppermute | solution.py:313
  143.0 13.4 %collective-permute-start.7 = (bf16[128,2048]{1,0:T(8,128)(2,1)S(1)}, bf16[128,2048]{1,0:T(8,128)(2,1)S(1)}, u32[]{:S(2)}, u32[]{:S(2)}) collective-permute-start(bf16[128,2048]{1,0:T(8,128)(2,1)S(1)} %bitcast.19), channel_id=1, source_target_pairs={{0,12},{4,0},{8,4},{12,8},{1,13},{5,1},{9,5},{13,9},{2,14},{6,2},{... | collective-permute-start | bytes 1572872 | tf_op jit(solution)/shard_map/ppermute | solution.py:313
  147.1 11.4 %collective-permute-start.6 = (bf16[128,2048]{1,0:T(8,128)(2,1)S(1)}, bf16[128,2048]{1,0:T(8,128)(2,1)S(1)}, u32[]{:S(2)}, u32[]{:S(2)}) collective-permute-start(bf16[128,2048]{1,0:T(8,128)(2,1)S(1)} %bitcast.20), channel_id=1, source_target_pairs={{0,4},{4,8},{8,12},{12,0},{1,5},{5,9},{9,13},{13,1},{2,6},{6,10},{... | collective-permute-start | bytes 1572872 | tf_op jit(solution)/shard_map/ppermute | solution.py:313
  161.9 9.4 %copy-start.3 = (bf16[2,256,256]{2,1,0:T(8,128)(2,1)S(1)}, bf16[2,256,256]{2,1,0:T(8,128)(2,1)}, u32[]{:S(2)}) copy-start(bf16[2,256,256]{2,1,0:T(8,128)(2,1)} %get-tuple-element.22.member_ref) | copy-start | bytes 786436

commit v6 on v5

--- a/solution.py
+++ b/solution.py
@@ -20,15 +20,6 @@
     for p in range(1, SIDE):
         block = jnp.where(at == p, ref[p], block)
     return block
-
-
-def pack_kernel(gate_ref, up_ref, down_ref, low_ref, high_ref):
-    width = gate_ref.shape[0]
-    half = width // 2
-    low_ref[:width] = gate_ref[...]
-    low_ref[width:] = down_ref[:half]
-    high_ref[:width] = up_ref[...]
-    high_ref[width:] = down_ref[half:]
 
 
 def dispatch_kernel(ids_ref, gates_ref, tokens_ref, cotangent_ref, send_ref, member_ref, both):
@@ -83,14 +74,15 @@
         coded = jnp.round(value * jnp.exp2(13.0 - power)).astype(jnp.int32).astype(jnp.int16)
         out_ref[:, i * cols : (i + 1) * cols] = coded
         powers = jnp.where(lane == i, power, powers)
-    out_ref[:, 3 * cols :] = powers.astype(jnp.int32).astype(jnp.int16)
+    out_ref[:, len(values) * cols :] = powers.astype(jnp.int32).astype(jnp.int16)
 
 
 def sum_coded(parts_ref, cols):
-    totals = [None] * 3
+    count = parts_ref.shape[2] // cols
+    totals = [None] * count
     for p in range(parts_ref.shape[0]):
-        powers = parts_ref[p, :, 3 * cols :].astype(jnp.int32).astype(jnp.float32)
-        for i in range(3):
+        powers = parts_ref[p, :, count * cols :].astype(jnp.int32).astype(jnp.float32)
+        for i in range(count):
             unit = jnp.exp2(powers[:, i : i + 1] - 13.0)
             coded = parts_ref[p, :, i * cols : (i + 1) * cols].astype(jnp.int32)
             value = coded.astype(jnp.float32) * unit
@@ -112,27 +104,49 @@
     return ready
 
 
-def partial_kernel(place_ref, rows_ref, own_low, own_high, *refs):
-    others = 2 * (SIDE - 1)
-    out_ref = refs[others]
-    ready = fetch(refs[:others], refs[others + 1 : -1], refs[-1])
+def pack_kernel(up_ref, down_ref, ups_ref):
+    width = up_ref.shape[0]
+    ups_ref[:width] = up_ref[...]
+    ups_ref[width:] = down_ref[...]
+
+
+def far_kernel(place_ref, recv_ref, ups_ref, out_ref):
+    width = recv_ref.shape[2] // 2
+    g = block_at(recv_ref, lax.rem(place_ref[0] + 2, SIDE))[:, width:]
+    put_coded(out_ref, [jnp.dot(g, ups_ref[width:], preferred_element_type=jnp.float32)])
+
+
+def partial_kernel(place_ref, rows_ref, far_ref, own_ups, *refs):
+    count = (len(refs) - 2) // 2
+    out_ref = refs[count]
+    ready = fetch(refs[:count], refs[count + 1 : -1], refs[-1])
     width = rows_ref.shape[2] // 2
-    half = width // 2
-    totals = [None] * 3
+    totals = [None, None, sum_coded(far_ref, own_ups.shape[1])[0]]
 
     def add(which, rows, weight):
         value = jnp.dot(rows, weight, preferred_element_type=jnp.float32)
         totals[which] = value if totals[which] is None else totals[which] + value
 
-    for i, shift in enumerate(SHIFTS):
-        both = block_at(rows_ref, lax.rem(place_ref[0] + shift, SIDE))
-        x = both[:, :width]
-        low = own_low if i == 0 else ready(2 * i - 2)
-        add(0, x, low[:width])
-        add(2, both[:, width : width + half], low[width:])
-        high = own_high if i == 0 else ready(2 * i - 1)
-        add(1, x, high[:width])
-        add(2, both[:, width + half :], high[width:])
+    def rows_of(i):
+        both = block_at(rows_ref, lax.rem(place_ref[0] + SHIFTS[i], SIDE))
+        return both[:, :width], both[:, width:]
+
+    x, g = rows_of(0)
+    add(1, x, own_ups[:width])
+    add(2, g, own_ups[width:])
+    add(0, x, ready(0)[...])
+    x, g = rows_of(1)
+    add(0, x, ready(1)[...])
+    ups = ready(2)
+    add(1, x, ups[:width])
+    add(2, g, ups[width:])
+    x, g = rows_of(2)
+    add(1, x, ready(3)[...])
+    add(0, x, ready(4)[...])
+    add(2, g, ready(5)[...])
+    x, _ = rows_of(3)
+    add(0, x, ready(6)[...])
+    add(1, x, ready(7)[...])
     put_coded(out_ref, totals)
 
 
@@ -146,22 +160,24 @@
         out_ref[p, :, hidden:] = grad_up
 
 
-def row_kernel(place_ref, grads_ref, own_low, own_high, *refs):
-    others = 2 * (SIDE - 1)
-    out_ref = refs[others]
-    ready = fetch(refs[:others], refs[others + 1 : -1], refs[-1])
+def row_kernel(place_ref, grads_ref, own_ups, *refs):
+    count = (len(refs) - 2) // 2
+    out_ref = refs[count]
+    ready = fetch(refs[:count], refs[count + 1 : -1], refs[-1])
     wide, hidden = grads_ref.shape[0], grads_ref.shape[1] // 2
     width = out_ref.shape[2] // 2
+    order = ((0, None), (1, 2), (4, 3), (5, 6))
     values = []
-    for i in range(SIDE):
-        low = own_low if i == 0 else ready(2 * i - 2)
-        total = lax.dot_general(
-            grads_ref[:, :hidden], low[:width], ACROSS, preferred_element_type=jnp.float32
-        )
-        high = own_high if i == 0 else ready(2 * i - 1)
-        total = total + lax.dot_general(
-            grads_ref[:, hidden:], high[:width], ACROSS, preferred_element_type=jnp.float32
-        )
+    for pair in order:
+        total = None
+        for j in (1, 0):
+            value = lax.dot_general(
+                grads_ref[:, j * hidden : (j + 1) * hidden],
+                (own_ups if pair[j] is None else ready(pair[j]))[:width],
+                ACROSS,
+                preferred_element_type=jnp.float32,
+            )
+            total = value if total is None else total + value
         both = total.reshape(-1, 2, CAP // 2, width)
         pair = [both[:, j].reshape(wide // 2, width) for j in (0, 1)]
         values.append(jnp.concatenate(pair, axis=1).astype(jnp.bfloat16))
@@ -247,42 +263,60 @@
         compiler_params=alone,
         name="dispatch",
     )(expert_ids.T, gate_values.T, tokens.T, cotangent.T)
-    send, gate_w, up_w, down_w = lax.optimization_barrier(
+    send, gate, up, down = lax.optimization_barrier(
         (send, gate_weight[0], up_weight[0], down_weight[0].T)
     )
-    half = jax.ShapeDtypeStruct((width + width // 2, hidden), jnp.bfloat16)
-    low, high = pl.pallas_call(
+
+    def on(array):
+        return lax.ppermute(array, AXES, onward)
+
+    def off(array):
+        return lax.ppermute(array, AXES, back)
+
+    gate_1, up_3 = on(gate), off(up)
+    ups = pl.pallas_call(
         pack_kernel,
-        out_shape=(half, half),
+        out_shape=jax.ShapeDtypeStruct((2 * width, hidden), jnp.bfloat16),
         compiler_params=params,
         name="pack",
-    )(gate_w, up_w, down_w)
-    low_1 = lax.ppermute(low, AXES, onward)
-    high_3 = lax.ppermute(high, AXES, back)
-    high_1 = lax.ppermute(high, AXES, onward)
-    low_3 = lax.ppermute(low, AXES, back)
-    low_2 = lax.ppermute(low_1, AXES, onward)
-    high_2 = lax.ppermute(high_3, AXES, back)
-    weights = (low, high, low_1, high_1, low_3, high_3, low_2, high_2)
+    )(up, down)
+    ups_1, gate_3, down_3 = on(ups), off(gate), off(down)
+    gate_2, up_2 = on(gate_1), off(up_3)
+    forward = (gate, gate_1, ups_1, up_3, gate_3, down_3, gate_2, up_2)
+    backward = (gate, gate_1, ups_1, up_3, gate_3, gate_2, up_2)
+
     recv = lax.all_to_all(
         send.reshape(held, CAP, 2 * width), "expert", split_axis=0, concat_axis=0, tiled=True
     ).reshape(slots, 2 * width)
 
-    mine = exchange(recv.reshape(SIDE, wide, 2 * width), first)
     vmem = pl.BlockSpec(memory_space=pltpu.VMEM)
     smem = pl.BlockSpec(memory_space=pltpu.SMEM)
     anywhere = pl.BlockSpec(memory_space=pl.ANY)
-    others = 2 * (SIDE - 1)
+
+    def buffers(shapes):
+        return [pltpu.VMEM(shape, jnp.bfloat16) for shape in shapes] + [
+            pltpu.SemaphoreType.DMA((len(shapes),))
+        ]
+
+    mine = exchange(recv.reshape(SIDE, wide, 2 * width), first)
+    far = pl.pallas_call(
+        far_kernel,
+        in_specs=[smem, vmem, vmem],
+        out_specs=vmem,
+        out_shape=jax.ShapeDtypeStruct((wide, hidden + 128), jnp.int16),
+        compiler_params=params,
+        name="far_products",
+    )(place, recv.reshape(SIDE, wide, 2 * width), ups)
+    far = lax.ppermute(far, AXES, plane_ring(held, 2))
     sums = pl.pallas_call(
         partial_kernel,
-        in_specs=[smem] + [vmem] * 3 + [anywhere] * others,
+        in_specs=[smem] + [vmem] * 3 + [anywhere] * len(forward),
         out_specs=vmem,
         out_shape=jax.ShapeDtypeStruct((wide, coded), jnp.int16),
-        scratch_shapes=[pltpu.VMEM((width + width // 2, hidden), jnp.bfloat16)] * others
-        + [pltpu.SemaphoreType.DMA((others,))],
+        scratch_shapes=buffers([x.shape for x in forward]),
         compiler_params=params,
         name="partials",
-    )(place, mine, *weights)
+    )(place, mine, far[None], ups, *forward)
     sums = exchange(sums.reshape(SIDE, rows, coded), second)
     grads = pl.pallas_call(
         lambda *refs: local_kernel(hidden, *refs),
@@ -293,14 +327,13 @@
     grads = exchange(grads, second).reshape(wide, 2 * hidden)
     row_grads = pl.pallas_call(
         row_kernel,
-        in_specs=[smem] + [vmem] * 3 + [anywhere] * others,
+        in_specs=[smem] + [vmem] * 2 + [anywhere] * len(backward),
         out_specs=vmem,
         out_shape=jax.ShapeDtypeStruct((SIDE, wide // 2, 2 * width), jnp.bfloat16),
-        scratch_shapes=[pltpu.VMEM((width, hidden), jnp.bfloat16)] * others
-        + [pltpu.SemaphoreType.DMA((others,))],
+        scratch_shapes=buffers([(width, hidden)] * len(backward)),
         compiler_params=params,
         name="row_grads",
-    )(place, grads, *weights)
+    )(place, grads, ups, *backward)
     row_grads = exchange(row_grads, first)
     returned = lax.all_to_all(
         row_grads.reshape(held, CAP // 2, 2 * width),

time: 173 us -> 171 us (0.988)
  waiting for transfers between devices: 53.1 us -> 48.4 us
  local copies, waits for them, and re-layouts: 3.53 us -> 0.01 us
  Pallas kernels: 20.8 us -> 24.1 us
  starting transfers between devices: 63.2 us -> 65.2 us
    ppermute x6 -> x8, starting transfers between devices: 18.3 us -> 26.5 us  [the longest x4 15.1 us: off(): return lax.ppermute(array, AXES, back)]
    all_to_all x1, waiting for transfers between devices: 7.99 us -> 0.01 us  [exchange(): lax.all_to_all(blocks, AXES, split_axis=0, concat_axis=0, tiled=True, axi...]
    all_to_all x1, waiting for transfers between devices: 19.3 us -> 26.9 us  [body(): lax.all_to_all(send.reshape(held, CAP, 2 * width), 'expert', split_axis=0...]
    all_to_all x1, starting transfers between devices: 15.4 us -> 9.25 us  [body(): lax.all_to_all(row_grads.reshape(held, CAP // 2, 2 * width), 'expert', sp...]
    ppermute x6 -> x8, waiting for transfers between devices: 10.2 us -> 5.89 us  [the longest x1 5.87 us: body(): far = lax.ppermute(far, AXES, plane_ring(held, 2))]
    unnamed x8 -> x4, local copies, waits for them, and re-layouts: 3.53 us -> 0.01 us
    pallas_call x2 -> x3, Pallas kernels: 4.84 us -> 7.7 us  [the longest x1 4.45 us: body(): pl.pallas_call(row_kernel, in_specs=[smem] + [vmem] * 2 + [anywhere] * le...]
  transfers between devices with their start and end apart: 12 -> 14, of which waited for: 8 -> 6; matrix products, arithmetic and copies ran while one was open for 0% -> 0% of each run, Pallas kernels for 4% -> 6%
where the time goes in v6:
time: 171 us; the launch traced here: 170 us
  starting transfers between devices  65.2 us (38%)
  waiting for transfers between devices  48.4 us (28%)
  blocking collectives  31.1 us (18%)
  Pallas kernels  24.1 us (14%)
    all_to_all x3, blocking collectives, exchange(): lax.all_to_all(blocks, AXES, split_axis=0, concat_axis=0, tiled=True, axi...  31.1 us
    all_to_all x1, waiting for transfers between devices, body(): lax.all_to_all(send.reshape(held, CAP, 2 * width), 'expert', split_axis=0...  26.9 us
    all_to_all x1, starting transfers between devices, body(): lax.all_to_all(send.reshape(held, CAP, 2 * width), 'expert', split_axis=0...  16.8 us
    ppermute x4, starting transfers between devices, off(): return lax.ppermute(array, AXES, back)  15.1 us
    ppermute x3, waiting for transfers between devices, body(): lax.ppermute(grads, AXES, plane_ring(held, k))  9.5 us
    all_to_all x1, starting transfers between devices, body(): lax.all_to_all(row_grads.reshape(held, CAP // 2, 2 * width), 'expert', sp...  9.25 us
    ppermute x3, starting transfers between devices, body(): lax.ppermute(grads, AXES, plane_ring(held, k))  8.42 us
    pallas_call x2, Pallas kernels, weight_grad(): pl.pallas_call(weight_kernel, grid=(per,), in_specs=[pl.BlockSpec(memory_...  6.73 us
  transfers between devices with their start and end apart: 14, of which 6 were waited for; matrix products, arithmetic and copies ran while one was open for 0% of the time, Pallas kernels for 6%

profile of v6, /device:TPU:1, one launch (start us, length us, event | category | flops | bytes accessed | tf_op | source)
XLA Modules:
  0.0 169.6 jit_solution(18276524991515376151)
XLA Ops:
  0.6 0.0 copy-start
  0.6 2.7 %dispatch.1 = (bf16[512,896]{1,0:T(8,128)(2,1)}, bf16[2,256,256]{2,1,0:T(8,128)(2,1)}) custom-call(s32[8,256]{1,0:T(8,128)} %bitcast.35, f32[8,256]{1,0:T(8,128)} %bitcast.36, bf16[448,256]{1,0:T(8,128)(2,1)} %bitcast.32, bf16[448,256]{1,0:T(8,128)(2,1)} %bitcast.33), custom_call_target="tpu_custom_call" | custom-call | tf_op jit(solution)/shard_map/dispatch/pallas_call | solution.py:256
  3.4 16.8 %all-to-all-start = ((bf16[32,16,896]{2,1,0:T(8,128)(2,1)}), bf16[32,16,896]{2,1,0:T(8,128)(2,1)}, u32[]{:S(2)}, u32[]{:S(2)}) async-start(bf16[32,16,896]{2,1,0:T(8,128)(2,1)} %bitcast.31), calls=%async_computation | async-start | bytes 1835008 | tf_op jit(solution)/shard_map/all_to_all | solution.py:288
  20.2 4.6 %collective-permute-start.3 = (bf16[448,1024]{1,0:T(8,128)(2,1)}, bf16[448,1024]{1,0:T(8,128)(2,1)}, u32[]{:S(2)}, u32[]{:S(2)}) collective-permute-start(bf16[448,1024]{1,0:T(8,128)(2,1)} %bitcast.6.up_ref), channel_id=1, source_target_pairs={{0,12},{4,0},{8,4},{12,8},{1,13},{5,1},{9,5},{13,9},{2,14},{6,2},{... | collective-permute-start | bytes 2752520 | tf_op jit(solution)/shard_map/ppermute | solution.py:274
  24.8 0.0 copy-done
  24.8 1.9 %collective-permute-start.1 = (bf16[448,1024]{1,0:T(8,128)(2,1)S(1)}, bf16[448,1024]{1,0:T(8,128)(2,1)}, u32[]{:S(2)}, u32[]{:S(2)}) collective-permute-start(bf16[448,1024]{1,0:T(8,128)(2,1)S(1)} %bitcast.24), channel_id=1, source_target_pairs={{0,4},{4,8},{8,12},{12,0},{1,5},{5,9},{9,13},{13,1},{2,6},{6,10},{... | collective-permute-start | bytes 2752520 | tf_op jit(solution)/shard_map/ppermute | solution.py:271
  26.8 1.6 pack.1.ups_ref.own_ups
  28.3 1.9 %collective-permute-start.2 = (bf16[896,1024]{1,0:T(8,128)(2,1)S(1)}, bf16[896,1024]{1,0:T(8,128)(2,1)}, u32[]{:S(2)}, u32[]{:S(2)}) collective-permute-start(bf16[896,1024]{1,0:T(8,128)(2,1)S(1)} %pack.1.ups_ref.own_ups), channel_id=1, source_target_pairs={{0,4},{4,8},{8,12},{12,0},{1,5},{5,9},{9,13},{13,1},{2,6},{6,10},{... | collective-permute-start | bytes 5505032 | tf_op jit(solution)/shard_map/ppermute | solution.py:271
  30.3 4.6 %collective-permute-start.5 = (bf16[448,1024]{1,0:T(8,128)(2,1)}, bf16[448,1024]{1,0:T(8,128)(2,1)}, u32[]{:S(2)}, u32[]{:S(2)}) collective-permute-start(bf16[448,1024]{1,0:T(8,128)(2,1)} %bitcast.8.down_ref), channel_id=1, source_target_pairs={{0,12},{4,0},{8,4},{12,8},{1,13},{5,1},{9,5},{13,9},{2,14},{6,2},{... | collective-permute-start | bytes 2752520 | tf_op jit(solution)/shard_map/ppermute | solution.py:274
  34.9 3.4 %collective-permute-start.4 = (bf16[448,1024]{1,0:T(8,128)(2,1)S(1)}, bf16[448,1024]{1,0:T(8,128)(2,1)}, u32[]{:S(2)}, u32[]{:S(2)}) collective-permute-start(bf16[448,1024]{1,0:T(8,128)(2,1)S(1)} %bitcast.25), channel_id=1, source_target_pairs={{0,12},{4,0},{8,4},{12,8},{1,13},{5,1},{9,5},{13,9},{2,14},{6,2},{... | collective-permute-start | bytes 2752520 | tf_op jit(solution)/shard_map/ppermute | solution.py:274
  38.2 0.0 collective-permute-done.3.refs_3_
  38.2 2.5 %collective-permute-start.7 = (bf16[448,1024]{1,0:T(8,128)(2,1)}, bf16[448,1024]{1,0:T(8,128)(2,1)}, u32[]{:S(2)}, u32[]{:S(2)}) collective-permute-start(bf16[448,1024]{1,0:T(8,128)(2,1)} %collective-permute-done.3.refs_3_), channel_id=1, source_target_pairs={{0,12},{4,0},{8,4},{12,8},{1,13},{5,1},{9,5},{13,9},{2,14},{6,2},{... | collective-permute-start | bytes 2752520 | tf_op jit(solution)/shard_map/ppermute | solution.py:274
  40.8 0.0 collective-permute-done.1.refs_1_
  40.8 2.8 %collective-permute-start.6 = (bf16[448,1024]{1,0:T(8,128)(2,1)}, bf16[448,1024]{1,0:T(8,128)(2,1)}, u32[]{:S(2)}, u32[]{:S(2)}) collective-permute-start(bf16[448,1024]{1,0:T(8,128)(2,1)} %collective-permute-done.1.refs_1_), channel_id=1, source_target_pairs={{0,4},{4,8},{8,12},{12,0},{1,5},{5,9},{9,13},{13,1},{2,6},{6,10},{... | collective-permute-start | bytes 2752520 | tf_op jit(solution)/shard_map/ppermute | solution.py:271
  43.5 26.9 %all-to-all-done = bf16[32,16,896]{2,1,0:T(8,128)(2,1)} async-done(((bf16[32,16,896]{2,1,0:T(8,128)(2,1)}), bf16[32,16,896]{2,1,0:T(8,128)(2,1)}, u32[]{:S(2)}, u32[]{:S(2)}) %all-to-all-start) | async-done | bytes 917536 | tf_op jit(solution)/shard_map/all_to_all | solution.py:288
  70.4 4.2 %all-to-all-start.1 = ((bf16[4,128,896]{2,1,0:T(8,128)(2,1)}), bf16[4,128,896]{2,1,0:T(8,128)(2,1)}, u32[]{:S(2)}, u32[]{:S(2)}) async-start(bf16[4,128,896]{2,1,0:T(8,128)(2,1)} %bitcast.10.recv_ref.rows_ref), calls=%async_computation.1 | async-start | bytes 1835008 | tf_op jit(solution)/shard_map/all_to_all | solution.py:234
  74.7 1.7 far_products.1
  76.4 0.0 collective-permute-done.5.refs_5_
  76.4 4.8 %collective-permute-start = (s16[128,1152]{1,0:T(8,128)(2,1)S(1)}, s16[128,1152]{1,0:T(8,128)(2,1)S(1)}, u32[]{:S(2)}, u32[]{:S(2)}) collective-permute-start(s16[128,1152]{1,0:T(8,128)(2,1)S(1)} %far_products.1), channel_id=1, source_target_pairs={{0,8},{4,12},{8,0},{12,4},{1,9},{5,13},{9,1},{13,5},{2,10},{6,14},... | collective-permute-start | bytes 884744 | tf_op jit(solution)/shard_map/ppermute | solution.py:310
  81.2 0.0 collective-permute-done.4.refs_4_
  81.2 0.0 collective-permute-done.7.refs_7_.refs_6_
  81.2 0.0 collective-permute-done.6.refs_6_.refs_5_
  81.2 0.0 collective-permute-done.2.refs_2_
  81.2 5.9 %collective-permute-done = s16[128,1152]{1,0:T(8,128)(2,1)S(1)} collective-permute-done((s16[128,1152]{1,0:T(8,128)(2,1)S(1)}, s16[128,1152]{1,0:T(8,128)(2,1)S(1)}, u32[]{:S(2)}, u32[]{:S(2)}) %collective-permute-start) | collective-permute-done | bytes 294944 | tf_op jit(solution)/shard_map/ppermute | solution.py:310
  87.1 0.0 all-to-all-done.1.rows_ref
  87.1 5.5 %partials.1 = s16[128,3200]{1,0:T(8,128)(2,1)S(1)} custom-call(s32[1]{0:T(128)} %bitcast.place_ref, bf16[4,128,896]{2,1,0:T(8,128)(2,1)} %all-to-all-done.1.rows_ref, s16[1,128,1152]{2,1,0:T(8,128)(2,1)S(1)} %bitcast.30, bf16[896,1024]{1,0:T(8,128)(2,1)S(1)} %pack.1.ups_ref.own_ups, bf16[448,1024]{1,0:T(8,128)(2,1)S(1)} %bitcast.26, ...), custom_call_target="tpu_custom_call" | custom-call | tf_op jit(solution)/shard_map/partials/pallas_call | solution.py:311
  92.6 12.1 %all_to_all.30.refs_0_ = s16[4,32,3200]{2,1,0:T(8,128)(2,1)S(1)} all-to-all(s16[4,32,3200]{2,1,0:T(8,128)(2,1)S(1)} %bitcast.28), channel_id=1, replica_groups={{0,1,2,3},{4,5,6,7},{8,9,10,11},{12,13,14,15},{16,20,24,28},{17,21,25,2..., dimensions={0} | all-to-all | bytes 1638400 | tf_op jit(solution)/shard_map/all_to_all | solution.py:234
  104.7 0.3 local_grads.1
  105.0 9.3 %all_to_all.31 = bf16[4,32,2048]{2,1,0:T(8,128)(2,1)S(1)} all-to-all(bf16[4,32,2048]{2,1,0:T(8,128)(2,1)S(1)} %local_grads.1), channel_id=1, replica_groups={{0,1,2,3},{4,5,6,7},{8,9,10,11},{12,13,14,15},{16,20,24,28},{17,21,25,2..., dimensions={0} | all-to-all | bytes 1048576 | tf_op jit(solution)/shard_map/all_to_all | solution.py:234
  114.3 4.4 %row_grads.1 = bf16[4,64,896]{2,1,0:T(8,128)(2,1)S(1)} custom-call(s32[1]{0:T(128)} %bitcast.place_ref, bf16[128,2048]{1,0:T(8,128)(2,1)S(1)} %bitcast.18, bf16[896,1024]{1,0:T(8,128)(2,1)S(1)} %pack.1.ups_ref.own_ups, bf16[448,1024]{1,0:T(8,128)(2,1)S(1)} %bitcast.27, bf16[448,1024]{1,0:T(8,128)(2,1)} %collective-permute-done.1.refs_1_, ...), custom_call_target="tpu_custom_call" | custom-call | tf_op jit(solution)/shard_map/row_grads/pallas_call | solution.py:328
  118.8 9.7 %all_to_all.32 = bf16[4,64,896]{2,1,0:T(8,128)(2,1)} all-to-all(bf16[4,64,896]{2,1,0:T(8,128)(2,1)S(1)} %row_grads.1), channel_id=1, replica_groups={{0,4,8,12},{1,5,9,13},{2,6,10,14},{3,7,11,15},{16,17,18,19},{20,21,22,2..., dimensions={0} | all-to-all | bytes 917504 | tf_op jit(solution)/shard_map/all_to_all | solution.py:234
  128.4 9.2 %all-to-all-start.5 = ((bf16[32,8,896]{2,1,0:T(8,128)(2,1)}), bf16[32,8,896]{2,1,0:T(8,128)(2,1)S(1)}, u32[]{:S(2)}, u32[]{:S(2)}) async-start(bf16[32,8,896]{2,1,0:T(8,128)(2,1)} %bitcast.14), calls=%async_computation.5 | async-start | bytes 917504 | tf_op jit(solution)/shard_map/all_to_all | solution.py:338
  137.7 2.4 %collective-permute-start.10 = (bf16[128,2048]{1,0:T(8,128)(2,1)S(1)}, bf16[128,2048]{1,0:T(8,128)(2,1)S(1)}, u32[]{:S(2)}, u32[]{:S(2)}) collective-permute-start(bf16[128,2048]{1,0:T(8,128)(2,1)S(1)} %bitcast.19), channel_id=1, source_target_pairs={{0,8},{4,12},{8,0},{12,4},{1,9},{5,13},{9,1},{13,5},{2,10},{6,14},... | collective-permute-start | bytes 1572872 | tf_op jit(solution)/shard_map/ppermute | solution.py:346
  140.1 4.1 %collective-permute-start.9 = (bf16[128,2048]{1,0:T(8,128)(2,1)S(1)}, bf16[128,2048]{1,0:T(8,128)(2,1)S(1)}, u32[]{:S(2)}, u32[]{:S(2)}) collective-permute-start(bf16[128,2048]{1,0:T(8,128)(2,1)S(1)} %bitcast.20), channel_id=1, source_target_pairs={{0,12},{4,0},{8,4},{12,8},{1,13},{5,1},{9,5},{13,9},{2,14},{6,2},{... | collective-permute-start | bytes 1572872 | tf_op jit(solution)/shard_map/ppermute | solution.py:346
  144.2 1.9 %collective-permute-start.8 = (bf16[128,2048]{1,0:T(8,128)(2,1)S(1)}, bf16[128,2048]{1,0:T(8,128)(2,1)S(1)}, u32[]{:S(2)}, u32[]{:S(2)}) collective-permute-start(bf16[128,2048]{1,0:T(8,128)(2,1)S(1)} %bitcast.21), channel_id=1, source_target_pairs={{0,4},{4,8},{8,12},{12,0},{1,5},{5,9},{9,13},{13,1},{2,6},{6,10},{... | collective-permute-start | bytes 1572872 | tf_op jit(solution)/shard_map/ppermute | solution.py:346
  146.1 3.3 %collective-permute-done.10.refs_3_ = bf16[128,2048]{1,0:T(8,128)(2,1)S(1)} collective-permute-done((bf16[128,2048]{1,0:T(8,128)(2,1)S(1)}, bf16[128,2048]{1,0:T(8,128)(2,1)S(1)}, u32[]{:S(2)}, u32[]{:S(2)}) %collective-permute-start.10) | collective-permute-done | bytes 524320 | tf_op jit(solution)/shard_map/ppermute | solution.py:346
  149.4 4.2 %collective-permute-done.9.refs_2_ = bf16[128,2048]{1,0:T(8,128)(2,1)S(1)} collective-permute-done((bf16[128,2048]{1,0:T(8,128)(2,1)S(1)}, bf16[128,2048]{1,0:T(8,128)(2,1)S(1)}, u32[]{:S(2)}, u32[]{:S(2)}) %collective-permute-start.9) | collective-permute-done | bytes 524320 | tf_op jit(solution)/shard_map/ppermute | solution.py:346
  153.6 2.1 %collective-permute-done.8.refs_1_ = bf16[128,2048]{1,0:T(8,128)(2,1)S(1)} collective-permute-done((bf16[128,2048]{1,0:T(8,128)(2,1)S(1)}, bf16[128,2048]{1,0:T(8,128)(2,1)S(1)}, u32[]{:S(2)}, u32[]{:S(2)}) %collective-permute-start.8) | collective-permute-done | bytes 524320 | tf_op jit(solution)/shard_map/ppermute | solution.py:346
  155.6 3.4 %weight_grad.3 = bf16[1,448,1024]{2,1,0:T(8,128)(2,1)} custom-call(s32[1]{0:T(128)} %bitcast.place_ref, bf16[4,128,896]{2,1,0:T(8,128)(2,1)} %bitcast.10.recv_ref.rows_ref, bf16[128,2048]{1,0:T(8,128)(2,1)S(1)} %bitcast.22, bf16[128,2048]{1,0:T(8,128)(2,1)S(1)} %collective-permute-done.8.refs_1_, bf16[128,2048]{1,0:T(8,128)(2,1)S(1)} %collective-permute-done.9.refs_2_, ...), custom_call_target="tpu_custom_call" | custom-call | tf_op jit(solution)/shard_map/weight_grad/pallas_call | solution.py:351
  159.0 0.0 copy-start.1
  159.0 3.4 %weight_grad.2 = bf16[1,448,1024]{2,1,0:T(8,128)(2,1)} custom-call(s32[1]{0:T(128)} %bitcast.place_ref, bf16[4,128,896]{2,1,0:T(8,128)(2,1)} %bitcast.10.recv_ref.rows_ref, bf16[128,2048]{1,0:T(8,128)(2,1)S(1)} %bitcast.23, bf16[128,2048]{1,0:T(8,128)(2,1)S(1)} %collective-permute-done.8.refs_1_, bf16[128,2048]{1,0:T(8,128)(2,1)S(1)} %collective-permute-done.9.refs_2_, ...), custom_call_target="tpu_custom_call" | custom-call | tf_op jit(solution)/shard_map/weight_grad/pallas_call | solution.py:351
  162.4 6.1 %all-to-all-done.5 = bf16[32,8,896]{2,1,0:T(8,128)(2,1)S(1)} async-done(((bf16[32,8,896]{2,1,0:T(8,128)(2,1)}), bf16[32,8,896]{2,1,0:T(8,128)(2,1)S(1)}, u32[]{:S(2)}, u32[]{:S(2)}) %all-to-all-start.5) | async-done | bytes 458784 | tf_op jit(solution)/shard_map/all_to_all | solution.py:338
  168.5 0.0 copy-done.1
  168.5 1.1 combine.1
Async XLA Ops:
  0.6 24.2 %copy-start = (bf16[1,448,1024]{2,1,0:T(8,128)(2,1)S(1)}, bf16[1,448,1024]{2,1,0:T(8,128)(2,1)}, u32[]{:S(2)}) copy-start(bf16[1,448,1024]{2,1,0:T(8,128)(2,1)} %param.9) | copy-start | bytes 2752516
  3.4 67.1 %all-to-all-start = ((bf16[32,16,896]{2,1,0:T(8,128)(2,1)}), bf16[32,16,896]{2,1,0:T(8,128)(2,1)}, u32[]{:S(2)}, u32[]{:S(2)}) async-start(bf16[32,16,896]{2,1,0:T(8,128)(2,1)} %bitcast.31), calls=%async_computation | async-start | bytes 1835008 | tf_op jit(solution)/shard_map/all_to_all | solution.py:288
  20.2 18.1 %collective-permute-start.3 = (bf16[448,1024]{1,0:T(8,128)(2,1)}, bf16[448,1024]{1,0:T(8,128)(2,1)}, u32[]{:S(2)}, u32[]{:S(2)}) collective-permute-start(bf16[448,1024]{1,0:T(8,128)(2,1)} %bitcast.6.up_ref), channel_id=1, source_target_pairs={{0,12},{4,0},{8,4},{12,8},{1,13},{5,1},{9,5},{13,9},{2,14},{6,2},{... | collective-permute-start | bytes 2752520 | tf_op jit(solution)/shard_map/ppermute | solution.py:274
  24.8 15.9 %collective-permute-start.1 = (bf16[448,1024]{1,0:T(8,128)(2,1)S(1)}, bf16[448,1024]{1,0:T(8,128)(2,1)}, u32[]{:S(2)}, u32[]{:S(2)}) collective-permute-start(bf16[448,1024]{1,0:T(8,128)(2,1)S(1)} %bitcast.24), channel_id=1, source_target_pairs={{0,4},{4,8},{8,12},{12,0},{1,5},{5,9},{9,13},{13,1},{2,6},{6,10},{... | collective-permute-start | bytes 2752520 | tf_op jit(solution)/shard_map/ppermute | solution.py:271
  28.3 52.9 %collective-permute-start.2 = (bf16[896,1024]{1,0:T(8,128)(2,1)S(1)}, bf16[896,1024]{1,0:T(8,128)(2,1)}, u32[]{:S(2)}, u32[]{:S(2)}) collective-permute-start(bf16[896,1024]{1,0:T(8,128)(2,1)S(1)} %pack.1.ups_ref.own_ups), channel_id=1, source_target_pairs={{0,4},{4,8},{8,12},{12,0},{1,5},{5,9},{9,13},{13,1},{2,6},{6,10},{... | collective-permute-start | bytes 5505032 | tf_op jit(solution)/shard_map/ppermute | solution.py:271
  30.3 46.1 %collective-permute-start.5 = (bf16[448,1024]{1,0:T(8,128)(2,1)}, bf16[448,1024]{1,0:T(8,128)(2,1)}, u32[]{:S(2)}, u32[]{:S(2)}) collective-permute-start(bf16[448,1024]{1,0:T(8,128)(2,1)} %bitcast.8.down_ref), channel_id=1, source_target_pairs={{0,12},{4,0},{8,4},{12,8},{1,13},{5,1},{9,5},{13,9},{2,14},{6,2},{... | collective-permute-start | bytes 2752520 | tf_op jit(solution)/shard_map/ppermute | solution.py:274
  34.9 46.3 %collective-permute-start.4 = (bf16[448,1024]{1,0:T(8,128)(2,1)S(1)}, bf16[448,1024]{1,0:T(8,128)(2,1)}, u32[]{:S(2)}, u32[]{:S(2)}) collective-permute-start(bf16[448,1024]{1,0:T(8,128)(2,1)S(1)} %bitcast.25), channel_id=1, source_target_pairs={{0,12},{4,0},{8,4},{12,8},{1,13},{5,1},{9,5},{13,9},{2,14},{6,2},{... | collective-permute-start | bytes 2752520 | tf_op jit(solution)/shard_map/ppermute | solution.py:274
  38.2 43.0 %collective-permute-start.7 = (bf16[448,1024]{1,0:T(8,128)(2,1)}, bf16[448,1024]{1,0:T(8,128)(2,1)}, u32[]{:S(2)}, u32[]{:S(2)}) collective-permute-start(bf16[448,1024]{1,0:T(8,128)(2,1)} %collective-permute-done.3.refs_3_), channel_id=1, source_target_pairs={{0,12},{4,0},{8,4},{12,8},{1,13},{5,1},{9,5},{13,9},{2,14},{6,2},{... | collective-permute-start | bytes 2752520 | tf_op jit(solution)/shard_map/ppermute | solution.py:274
  40.8 40.4 %collective-permute-start.6 = (bf16[448,1024]{1,0:T(8,128)(2,1)}, bf16[448,1024]{1,0:T(8,128)(2,1)}, u32[]{:S(2)}, u32[]{:S(2)}) collective-permute-start(bf16[448,1024]{1,0:T(8,128)(2,1)} %collective-permute-done.1.refs_1_), channel_id=1, source_target_pairs={{0,4},{4,8},{8,12},{12,0},{1,5},{5,9},{9,13},{13,1},{2,6},{6,10},{... | collective-permute-start | bytes 2752520 | tf_op jit(solution)/shard_map/ppermute | solution.py:271
  70.4 16.7 %all-to-all-start.1 = ((bf16[4,128,896]{2,1,0:T(8,128)(2,1)}), bf16[4,128,896]{2,1,0:T(8,128)(2,1)}, u32[]{:S(2)}, u32[]{:S(2)}) async-start(bf16[4,128,896]{2,1,0:T(8,128)(2,1)} %bitcast.10.recv_ref.rows_ref), calls=%async_computation.1 | async-start | bytes 1835008 | tf_op jit(solution)/shard_map/all_to_all | solution.py:234
  76.4 10.7 %collective-permute-start = (s16[128,1152]{1,0:T(8,128)(2,1)S(1)}, s16[128,1152]{1,0:T(8,128)(2,1)S(1)}, u32[]{:S(2)}, u32[]{:S(2)}) collective-permute-start(s16[128,1152]{1,0:T(8,128)(2,1)S(1)} %far_products.1), channel_id=1, source_target_pairs={{0,8},{4,12},{8,0},{12,4},{1,9},{5,13},{9,1},{13,5},{2,10},{6,14},... | collective-permute-start | bytes 884744 | tf_op jit(solution)/shard_map/ppermute | solution.py:310
  128.4 40.0 %all-to-all-start.5 = ((bf16[32,8,896]{2,1,0:T(8,128)(2,1)}), bf16[32,8,896]{2,1,0:T(8,128)(2,1)S(1)}, u32[]{:S(2)}, u32[]{:S(2)}) async-start(bf16[32,8,896]{2,1,0:T(8,128)(2,1)} %bitcast.14), calls=%async_computation.5 | async-start | bytes 917504 | tf_op jit(solution)/shard_map/all_to_all | solution.py:338
  137.7 11.7 %collective-permute-start.10 = (bf16[128,2048]{1,0:T(8,128)(2,1)S(1)}, bf16[128,2048]{1,0:T(8,128)(2,1)S(1)}, u32[]{:S(2)}, u32[]{:S(2)}) collective-permute-start(bf16[128,2048]{1,0:T(8,128)(2,1)S(1)} %bitcast.19), channel_id=1, source_target_pairs={{0,8},{4,12},{8,0},{12,4},{1,9},{5,13},{9,1},{13,5},{2,10},{6,14},... | collective-permute-start | bytes 1572872 | tf_op jit(solution)/shard_map/ppermute | solution.py:346
  140.1 13.4 %collective-permute-start.9 = (bf16[128,2048]{1,0:T(8,128)(2,1)S(1)}, bf16[128,2048]{1,0:T(8,128)(2,1)S(1)}, u32[]{:S(2)}, u32[]{:S(2)}) collective-permute-start(bf16[128,2048]{1,0:T(8,128)(2,1)S(1)} %bitcast.20), channel_id=1, source_target_pairs={{0,12},{4,0},{8,4},{12,8},{1,13},{5,1},{9,5},{13,9},{2,14},{6,2},{... | collective-permute-start | bytes 1572872 | tf_op jit(solution)/shard_map/ppermute | solution.py:346
  144.2 11.4 %collective-permute-start.8 = (bf16[128,2048]{1,0:T(8,128)(2,1)S(1)}, bf16[128,2048]{1,0:T(8,128)(2,1)S(1)}, u32[]{:S(2)}, u32[]{:S(2)}) collective-permute-start(bf16[128,2048]{1,0:T(8,128)(2,1)S(1)} %bitcast.21), channel_id=1, source_target_pairs={{0,4},{4,8},{8,12},{12,0},{1,5},{5,9},{9,13},{13,1},{2,6},{6,10},{... | collective-permute-start | bytes 1572872 | tf_op jit(solution)/shard_map/ppermute | solution.py:346
  159.0 9.5 %copy-start.1 = (bf16[2,256,256]{2,1,0:T(8,128)(2,1)S(1)}, bf16[2,256,256]{2,1,0:T(8,128)(2,1)}, u32[]{:S(2)}) copy-start(bf16[2,256,256]{2,1,0:T(8,128)(2,1)} %get-tuple-element.18.member_ref) | copy-start | bytes 786436

commit v7 on v6

--- a/solution.py
+++ b/solution.py
@@ -22,10 +22,38 @@
     return block
 
 
-def dispatch_kernel(ids_ref, gates_ref, tokens_ref, cotangent_ref, send_ref, member_ref, both):
+def dispatch_kernel(
+    ids_hbm,
+    gates_hbm,
+    tokens_hbm,
+    cotangent_hbm,
+    send_hbm,
+    member_hbm,
+    ids_ref,
+    gates_ref,
+    both,
+    send_ref,
+    member_ref,
+    sems,
+):
     top_count, tok_rows = ids_ref.shape
-    width = tokens_ref.shape[0]
+    width = tokens_hbm.shape[0]
     slots = send_ref.shape[0]
+    loads = [
+        pltpu.make_async_copy(source, target, sems.at[i])
+        for i, (source, target) in enumerate(
+            (
+                (ids_hbm, ids_ref),
+                (gates_hbm, gates_ref),
+                (tokens_hbm, both.at[:width]),
+                (cotangent_hbm, both.at[width:]),
+            )
+        )
+    ]
+    for load in loads:
+        load.start()
+    loads[0].wait()
+    loads[1].wait()
     held = slots // CAP
     ids = ids_ref[...]
     gates = gates_ref[...]
@@ -57,11 +85,24 @@
     for i in (0, 1):
         member_ref[i] = halves[:, i].reshape(slots // 2, tok_rows).astype(jnp.bfloat16)
     member = member.astype(jnp.bfloat16)
-    both[:width, :] = tokens_ref[...]
-    both[width:, :] = cotangent_ref[...]
-    picked = lax.dot_general(member, both[...], ACROSS, preferred_element_type=jnp.float32)
-    column = lax.broadcasted_iota(jnp.int32, picked.shape, 1)
-    send_ref[...] = jnp.where(column < width, picked, picked * slot_gate).astype(jnp.bfloat16)
+    stores = [pltpu.make_async_copy(member_ref, member_hbm, sems.at[4])]
+    stores[0].start()
+    loads[2].wait()
+    loads[3].wait()
+    column = lax.broadcasted_iota(jnp.int32, (slots // 2, 2 * width), 1)
+    for i in (0, 1):
+        part = slice(i * slots // 2, (i + 1) * slots // 2)
+        picked = lax.dot_general(
+            member[part], both[...], ACROSS, preferred_element_type=jnp.float32
+        )
+        scaled = picked * slot_gate[part]
+        send_ref[part] = jnp.where(column < width, picked, scaled).astype(jnp.bfloat16)
+        stores.append(
+            pltpu.make_async_copy(send_ref.at[part], send_hbm.at[part], sems.at[5 + i])
+        )
+        stores[-1].start()
+    for store in stores:
+        store.wait()
 
 
 def put_coded(out_ref, values):
@@ -259,7 +300,16 @@
             jax.ShapeDtypeStruct((slots, 2 * width), jnp.bfloat16),
             jax.ShapeDtypeStruct((2, slots // 2, tok_rows), jnp.bfloat16),
         ),
-        scratch_shapes=[pltpu.VMEM((2 * width, tok_rows), jnp.bfloat16)],
+        in_specs=[pl.BlockSpec(memory_space=pl.ANY)] * 4,
+        out_specs=[pl.BlockSpec(memory_space=pl.ANY)] * 2,
+        scratch_shapes=[
+            pltpu.VMEM(expert_ids.shape[::-1], jnp.int32),
+            pltpu.VMEM(gate_values.shape[::-1], jnp.float32),
+            pltpu.VMEM((2 * width, tok_rows), jnp.bfloat16),
+            pltpu.VMEM((slots, 2 * width), jnp.bfloat16),
+            pltpu.VMEM((2, slots // 2, tok_rows), jnp.bfloat16),
+            pltpu.SemaphoreType.DMA((7,)),
+        ],
         compiler_params=alone,
         name="dispatch",
     )(expert_ids.T, gate_values.T, tokens.T, cotangent.T)

time: 171 us -> 170 us (level)
  no operation moved by 1% of the time
where the time goes in v7:
time: 170 us; the launch traced here: 169 us
  starting transfers between devices  65.2 us (38%)
  waiting for transfers between devices  48.4 us (28%)
  blocking collectives  31 us (18%)
  Pallas kernels  23.9 us (14%)
    all_to_all x3, blocking collectives, exchange(): lax.all_to_all(blocks, AXES, split_axis=0, concat_axis=0, tiled=True, axi...  31 us
    all_to_all x1, waiting for transfers between devices, body(): lax.all_to_all(send.reshape(held, CAP, 2 * width), 'expert', split_axis=0...  26.9 us
    all_to_all x1, starting transfers between devices, body(): lax.all_to_all(send.reshape(held, CAP, 2 * width), 'expert', split_axis=0...  16.8 us
    ppermute x4, starting transfers between devices, off(): return lax.ppermute(array, AXES, back)  15.1 us
    ppermute x3, waiting for transfers between devices, body(): lax.ppermute(grads, AXES, plane_ring(held, k))  9.5 us
    all_to_all x1, starting transfers between devices, body(): lax.all_to_all(row_grads.reshape(held, CAP // 2, 2 * width), 'expert', sp...  9.26 us
    ppermute x3, starting transfers between devices, body(): lax.ppermute(grads, AXES, plane_ring(held, k))  8.42 us
    pallas_call x2, Pallas kernels, weight_grad(): pl.pallas_call(weight_kernel, grid=(per,), in_specs=[pl.BlockSpec(memory_...  6.73 us
  transfers between devices with their start and end apart: 14, of which 6 were waited for; matrix products, arithmetic and copies ran while one was open for 0% of the time, Pallas kernels for 6%

profile of v7, /device:TPU:1, one launch (start us, length us, event | category | flops | bytes accessed | tf_op | source)
XLA Modules:
  0.0 169.4 jit_solution(12293281813847704070)
XLA Ops:
  0.6 0.0 copy-start
  0.6 2.5 %dispatch.1 = (bf16[512,896]{1,0:T(8,128)(2,1)}, bf16[2,256,256]{2,1,0:T(8,128)(2,1)}) custom-call(s32[8,256]{1,0:T(8,128)} %bitcast.35, f32[8,256]{1,0:T(8,128)} %bitcast.36, bf16[448,256]{1,0:T(8,128)(2,1)} %bitcast.32, bf16[448,256]{1,0:T(8,128)(2,1)} %bitcast.33), custom_call_target="tpu_custom_call" | custom-call | tf_op jit(solution)/shard_map/dispatch/pallas_call | solution.py:297
  3.1 16.8 %all-to-all-start = ((bf16[32,16,896]{2,1,0:T(8,128)(2,1)}), bf16[32,16,896]{2,1,0:T(8,128)(2,1)}, u32[]{:S(2)}, u32[]{:S(2)}) async-start(bf16[32,16,896]{2,1,0:T(8,128)(2,1)} %bitcast.31), calls=%async_computation | async-start | bytes 1835008 | tf_op jit(solution)/shard_map/all_to_all | solution.py:338
  20.0 4.6 %collective-permute-start.3 = (bf16[448,1024]{1,0:T(8,128)(2,1)}, bf16[448,1024]{1,0:T(8,128)(2,1)}, u32[]{:S(2)}, u32[]{:S(2)}) collective-permute-start(bf16[448,1024]{1,0:T(8,128)(2,1)} %bitcast.6.up_ref), channel_id=1, source_target_pairs={{0,12},{4,0},{8,4},{12,8},{1,13},{5,1},{9,5},{13,9},{2,14},{6,2},{... | collective-permute-start | bytes 2752520 | tf_op jit(solution)/shard_map/ppermute | solution.py:324
  24.6 0.0 copy-done
  24.6 1.9 %collective-permute-start.1 = (bf16[448,1024]{1,0:T(8,128)(2,1)S(1)}, bf16[448,1024]{1,0:T(8,128)(2,1)}, u32[]{:S(2)}, u32[]{:S(2)}) collective-permute-start(bf16[448,1024]{1,0:T(8,128)(2,1)S(1)} %bitcast.24), channel_id=1, source_target_pairs={{0,4},{4,8},{8,12},{12,0},{1,5},{5,9},{9,13},{13,1},{2,6},{6,10},{... | collective-permute-start | bytes 2752520 | tf_op jit(solution)/shard_map/ppermute | solution.py:321
  26.6 1.6 pack.1.ups_ref.own_ups
  28.1 1.9 %collective-permute-start.2 = (bf16[896,1024]{1,0:T(8,128)(2,1)S(1)}, bf16[896,1024]{1,0:T(8,128)(2,1)}, u32[]{:S(2)}, u32[]{:S(2)}) collective-permute-start(bf16[896,1024]{1,0:T(8,128)(2,1)S(1)} %pack.1.ups_ref.own_ups), channel_id=1, source_target_pairs={{0,4},{4,8},{8,12},{12,0},{1,5},{5,9},{9,13},{13,1},{2,6},{6,10},{... | collective-permute-start | bytes 5505032 | tf_op jit(solution)/shard_map/ppermute | solution.py:321
  30.1 4.6 %collective-permute-start.5 = (bf16[448,1024]{1,0:T(8,128)(2,1)}, bf16[448,1024]{1,0:T(8,128)(2,1)}, u32[]{:S(2)}, u32[]{:S(2)}) collective-permute-start(bf16[448,1024]{1,0:T(8,128)(2,1)} %bitcast.8.down_ref), channel_id=1, source_target_pairs={{0,12},{4,0},{8,4},{12,8},{1,13},{5,1},{9,5},{13,9},{2,14},{6,2},{... | collective-permute-start | bytes 2752520 | tf_op jit(solution)/shard_map/ppermute | solution.py:324
  34.6 3.4 %collective-permute-start.4 = (bf16[448,1024]{1,0:T(8,128)(2,1)S(1)}, bf16[448,1024]{1,0:T(8,128)(2,1)}, u32[]{:S(2)}, u32[]{:S(2)}) collective-permute-start(bf16[448,1024]{1,0:T(8,128)(2,1)S(1)} %bitcast.25), channel_id=1, source_target_pairs={{0,12},{4,0},{8,4},{12,8},{1,13},{5,1},{9,5},{13,9},{2,14},{6,2},{... | collective-permute-start | bytes 2752520 | tf_op jit(solution)/shard_map/ppermute | solution.py:324
  38.0 0.0 collective-permute-done.3.refs_3_
  38.0 2.5 %collective-permute-start.7 = (bf16[448,1024]{1,0:T(8,128)(2,1)}, bf16[448,1024]{1,0:T(8,128)(2,1)}, u32[]{:S(2)}, u32[]{:S(2)}) collective-permute-start(bf16[448,1024]{1,0:T(8,128)(2,1)} %collective-permute-done.3.refs_3_), channel_id=1, source_target_pairs={{0,12},{4,0},{8,4},{12,8},{1,13},{5,1},{9,5},{13,9},{2,14},{6,2},{... | collective-permute-start | bytes 2752520 | tf_op jit(solution)/shard_map/ppermute | solution.py:324
  40.6 0.0 collective-permute-done.1.refs_1_
  40.6 2.8 %collective-permute-start.6 = (bf16[448,1024]{1,0:T(8,128)(2,1)}, bf16[448,1024]{1,0:T(8,128)(2,1)}, u32[]{:S(2)}, u32[]{:S(2)}) collective-permute-start(bf16[448,1024]{1,0:T(8,128)(2,1)} %collective-permute-done.1.refs_1_), channel_id=1, source_target_pairs={{0,4},{4,8},{8,12},{12,0},{1,5},{5,9},{9,13},{13,1},{2,6},{6,10},{... | collective-permute-start | bytes 2752520 | tf_op jit(solution)/shard_map/ppermute | solution.py:321
  43.3 26.9 %all-to-all-done = bf16[32,16,896]{2,1,0:T(8,128)(2,1)} async-done(((bf16[32,16,896]{2,1,0:T(8,128)(2,1)}), bf16[32,16,896]{2,1,0:T(8,128)(2,1)}, u32[]{:S(2)}, u32[]{:S(2)}) %all-to-all-start) | async-done | bytes 917536 | tf_op jit(solution)/shard_map/all_to_all | solution.py:338
  70.2 4.2 %all-to-all-start.1 = ((bf16[4,128,896]{2,1,0:T(8,128)(2,1)}), bf16[4,128,896]{2,1,0:T(8,128)(2,1)}, u32[]{:S(2)}, u32[]{:S(2)}) async-start(bf16[4,128,896]{2,1,0:T(8,128)(2,1)} %bitcast.10.recv_ref.rows_ref), calls=%async_computation.1 | async-start | bytes 1835008 | tf_op jit(solution)/shard_map/all_to_all | solution.py:275
  74.5 1.7 far_products.1
  76.2 0.0 collective-permute-done.5.refs_5_
  76.2 4.8 %collective-permute-start = (s16[128,1152]{1,0:T(8,128)(2,1)S(1)}, s16[128,1152]{1,0:T(8,128)(2,1)S(1)}, u32[]{:S(2)}, u32[]{:S(2)}) collective-permute-start(s16[128,1152]{1,0:T(8,128)(2,1)S(1)} %far_products.1), channel_id=1, source_target_pairs={{0,8},{4,12},{8,0},{12,4},{1,9},{5,13},{9,1},{13,5},{2,10},{6,14},... | collective-permute-start | bytes 884744 | tf_op jit(solution)/shard_map/ppermute | solution.py:360
  81.0 0.0 collective-permute-done.4.refs_4_
  81.0 0.0 collective-permute-done.7.refs_7_.refs_6_
  81.0 0.0 collective-permute-done.6.refs_6_.refs_5_
  81.0 0.0 collective-permute-done.2.refs_2_
  81.0 5.9 %collective-permute-done = s16[128,1152]{1,0:T(8,128)(2,1)S(1)} collective-permute-done((s16[128,1152]{1,0:T(8,128)(2,1)S(1)}, s16[128,1152]{1,0:T(8,128)(2,1)S(1)}, u32[]{:S(2)}, u32[]{:S(2)}) %collective-permute-start) | collective-permute-done | bytes 294944 | tf_op jit(solution)/shard_map/ppermute | solution.py:360
  86.9 0.0 all-to-all-done.1.rows_ref
  86.9 5.5 %partials.1 = s16[128,3200]{1,0:T(8,128)(2,1)S(1)} custom-call(s32[1]{0:T(128)} %bitcast.place_ref, bf16[4,128,896]{2,1,0:T(8,128)(2,1)} %all-to-all-done.1.rows_ref, s16[1,128,1152]{2,1,0:T(8,128)(2,1)S(1)} %bitcast.30, bf16[896,1024]{1,0:T(8,128)(2,1)S(1)} %pack.1.ups_ref.own_ups, bf16[448,1024]{1,0:T(8,128)(2,1)S(1)} %bitcast.26, ...), custom_call_target="tpu_custom_call" | custom-call | tf_op jit(solution)/shard_map/partials/pallas_call | solution.py:361
  92.5 12.0 %all_to_all.30.refs_0_ = s16[4,32,3200]{2,1,0:T(8,128)(2,1)S(1)} all-to-all(s16[4,32,3200]{2,1,0:T(8,128)(2,1)S(1)} %bitcast.28), channel_id=1, replica_groups={{0,1,2,3},{4,5,6,7},{8,9,10,11},{12,13,14,15},{16,20,24,28},{17,21,25,2..., dimensions={0} | all-to-all | bytes 1638400 | tf_op jit(solution)/shard_map/all_to_all | solution.py:275
  104.5 0.3 local_grads.1
  104.8 9.3 %all_to_all.31 = bf16[4,32,2048]{2,1,0:T(8,128)(2,1)S(1)} all-to-all(bf16[4,32,2048]{2,1,0:T(8,128)(2,1)S(1)} %local_grads.1), channel_id=1, replica_groups={{0,1,2,3},{4,5,6,7},{8,9,10,11},{12,13,14,15},{16,20,24,28},{17,21,25,2..., dimensions={0} | all-to-all | bytes 1048576 | tf_op jit(solution)/shard_map/all_to_all | solution.py:275
  114.1 4.4 %row_grads.1 = bf16[4,64,896]{2,1,0:T(8,128)(2,1)S(1)} custom-call(s32[1]{0:T(128)} %bitcast.place_ref, bf16[128,2048]{1,0:T(8,128)(2,1)S(1)} %bitcast.18, bf16[896,1024]{1,0:T(8,128)(2,1)S(1)} %pack.1.ups_ref.own_ups, bf16[448,1024]{1,0:T(8,128)(2,1)S(1)} %bitcast.27, bf16[448,1024]{1,0:T(8,128)(2,1)} %collective-permute-done.1.refs_1_, ...), custom_call_target="tpu_custom_call" | custom-call | tf_op jit(solution)/shard_map/row_grads/pallas_call | solution.py:378
  118.6 9.7 %all_to_all.32 = bf16[4,64,896]{2,1,0:T(8,128)(2,1)} all-to-all(bf16[4,64,896]{2,1,0:T(8,128)(2,1)S(1)} %row_grads.1), channel_id=1, replica_groups={{0,4,8,12},{1,5,9,13},{2,6,10,14},{3,7,11,15},{16,17,18,19},{20,21,22,2..., dimensions={0} | all-to-all | bytes 917504 | tf_op jit(solution)/shard_map/all_to_all | solution.py:275
  128.2 9.3 %all-to-all-start.5 = ((bf16[32,8,896]{2,1,0:T(8,128)(2,1)}), bf16[32,8,896]{2,1,0:T(8,128)(2,1)S(1)}, u32[]{:S(2)}, u32[]{:S(2)}) async-start(bf16[32,8,896]{2,1,0:T(8,128)(2,1)} %bitcast.14), calls=%async_computation.5 | async-start | bytes 917504 | tf_op jit(solution)/shard_map/all_to_all | solution.py:388
  137.5 2.5 %collective-permute-start.10 = (bf16[128,2048]{1,0:T(8,128)(2,1)S(1)}, bf16[128,2048]{1,0:T(8,128)(2,1)S(1)}, u32[]{:S(2)}, u32[]{:S(2)}) collective-permute-start(bf16[128,2048]{1,0:T(8,128)(2,1)S(1)} %bitcast.19), channel_id=1, source_target_pairs={{0,8},{4,12},{8,0},{12,4},{1,9},{5,13},{9,1},{13,5},{2,10},{6,14},... | collective-permute-start | bytes 1572872 | tf_op jit(solution)/shard_map/ppermute | solution.py:396
  140.0 4.0 %collective-permute-start.9 = (bf16[128,2048]{1,0:T(8,128)(2,1)S(1)}, bf16[128,2048]{1,0:T(8,128)(2,1)S(1)}, u32[]{:S(2)}, u32[]{:S(2)}) collective-permute-start(bf16[128,2048]{1,0:T(8,128)(2,1)S(1)} %bitcast.20), channel_id=1, source_target_pairs={{0,12},{4,0},{8,4},{12,8},{1,13},{5,1},{9,5},{13,9},{2,14},{6,2},{... | collective-permute-start | bytes 1572872 | tf_op jit(solution)/shard_map/ppermute | solution.py:396
  144.0 1.9 %collective-permute-start.8 = (bf16[128,2048]{1,0:T(8,128)(2,1)S(1)}, bf16[128,2048]{1,0:T(8,128)(2,1)S(1)}, u32[]{:S(2)}, u32[]{:S(2)}) collective-permute-start(bf16[128,2048]{1,0:T(8,128)(2,1)S(1)} %bitcast.21), channel_id=1, source_target_pairs={{0,4},{4,8},{8,12},{12,0},{1,5},{5,9},{9,13},{13,1},{2,6},{6,10},{... | collective-permute-start | bytes 1572872 | tf_op jit(solution)/shard_map/ppermute | solution.py:396
  145.9 3.3 %collective-permute-done.10.refs_3_ = bf16[128,2048]{1,0:T(8,128)(2,1)S(1)} collective-permute-done((bf16[128,2048]{1,0:T(8,128)(2,1)S(1)}, bf16[128,2048]{1,0:T(8,128)(2,1)S(1)}, u32[]{:S(2)}, u32[]{:S(2)}) %collective-permute-start.10) | collective-permute-done | bytes 524320 | tf_op jit(solution)/shard_map/ppermute | solution.py:396
  149.2 4.2 %collective-permute-done.9.refs_2_ = bf16[128,2048]{1,0:T(8,128)(2,1)S(1)} collective-permute-done((bf16[128,2048]{1,0:T(8,128)(2,1)S(1)}, bf16[128,2048]{1,0:T(8,128)(2,1)S(1)}, u32[]{:S(2)}, u32[]{:S(2)}) %collective-permute-start.9) | collective-permute-done | bytes 524320 | tf_op jit(solution)/shard_map/ppermute | solution.py:396
  153.4 2.1 %collective-permute-done.8.refs_1_ = bf16[128,2048]{1,0:T(8,128)(2,1)S(1)} collective-permute-done((bf16[128,2048]{1,0:T(8,128)(2,1)S(1)}, bf16[128,2048]{1,0:T(8,128)(2,1)S(1)}, u32[]{:S(2)}, u32[]{:S(2)}) %collective-permute-start.8) | collective-permute-done | bytes 524320 | tf_op jit(solution)/shard_map/ppermute | solution.py:396
  155.4 3.4 %weight_grad.3 = bf16[1,448,1024]{2,1,0:T(8,128)(2,1)} custom-call(s32[1]{0:T(128)} %bitcast.place_ref, bf16[4,128,896]{2,1,0:T(8,128)(2,1)} %bitcast.10.recv_ref.rows_ref, bf16[128,2048]{1,0:T(8,128)(2,1)S(1)} %bitcast.22, bf16[128,2048]{1,0:T(8,128)(2,1)S(1)} %collective-permute-done.8.refs_1_, bf16[128,2048]{1,0:T(8,128)(2,1)S(1)} %collective-permute-done.9.refs_2_, ...), custom_call_target="tpu_custom_call" | custom-call | tf_op jit(solution)/shard_map/weight_grad/pallas_call | solution.py:401
  158.8 0.0 copy-start.1
  158.8 3.4 %weight_grad.2 = bf16[1,448,1024]{2,1,0:T(8,128)(2,1)} custom-call(s32[1]{0:T(128)} %bitcast.place_ref, bf16[4,128,896]{2,1,0:T(8,128)(2,1)} %bitcast.10.recv_ref.rows_ref, bf16[128,2048]{1,0:T(8,128)(2,1)S(1)} %bitcast.23, bf16[128,2048]{1,0:T(8,128)(2,1)S(1)} %collective-permute-done.8.refs_1_, bf16[128,2048]{1,0:T(8,128)(2,1)S(1)} %collective-permute-done.9.refs_2_, ...), custom_call_target="tpu_custom_call" | custom-call | tf_op jit(solution)/shard_map/weight_grad/pallas_call | solution.py:401
  162.2 6.1 %all-to-all-done.5 = bf16[32,8,896]{2,1,0:T(8,128)(2,1)S(1)} async-done(((bf16[32,8,896]{2,1,0:T(8,128)(2,1)}), bf16[32,8,896]{2,1,0:T(8,128)(2,1)S(1)}, u32[]{:S(2)}, u32[]{:S(2)}) %all-to-all-start.5) | async-done | bytes 458784 | tf_op jit(solution)/shard_map/all_to_all | solution.py:388
  168.3 0.0 copy-done.1
  168.3 1.1 combine.1
Async XLA Ops:
  0.6 24.0 %copy-start = (bf16[1,448,1024]{2,1,0:T(8,128)(2,1)S(1)}, bf16[1,448,1024]{2,1,0:T(8,128)(2,1)}, u32[]{:S(2)}) copy-start(bf16[1,448,1024]{2,1,0:T(8,128)(2,1)} %param.9) | copy-start | bytes 2752516
  3.1 67.1 %all-to-all-start = ((bf16[32,16,896]{2,1,0:T(8,128)(2,1)}), bf16[32,16,896]{2,1,0:T(8,128)(2,1)}, u32[]{:S(2)}, u32[]{:S(2)}) async-start(bf16[32,16,896]{2,1,0:T(8,128)(2,1)} %bitcast.31), calls=%async_computation | async-start | bytes 1835008 | tf_op jit(solution)/shard_map/all_to_all | solution.py:338
  20.0 18.1 %collective-permute-start.3 = (bf16[448,1024]{1,0:T(8,128)(2,1)}, bf16[448,1024]{1,0:T(8,128)(2,1)}, u32[]{:S(2)}, u32[]{:S(2)}) collective-permute-start(bf16[448,1024]{1,0:T(8,128)(2,1)} %bitcast.6.up_ref), channel_id=1, source_target_pairs={{0,12},{4,0},{8,4},{12,8},{1,13},{5,1},{9,5},{13,9},{2,14},{6,2},{... | collective-permute-start | bytes 2752520 | tf_op jit(solution)/shard_map/ppermute | solution.py:324
  24.6 15.9 %collective-permute-start.1 = (bf16[448,1024]{1,0:T(8,128)(2,1)S(1)}, bf16[448,1024]{1,0:T(8,128)(2,1)}, u32[]{:S(2)}, u32[]{:S(2)}) collective-permute-start(bf16[448,1024]{1,0:T(8,128)(2,1)S(1)} %bitcast.24), channel_id=1, source_target_pairs={{0,4},{4,8},{8,12},{12,0},{1,5},{5,9},{9,13},{13,1},{2,6},{6,10},{... | collective-permute-start | bytes 2752520 | tf_op jit(solution)/shard_map/ppermute | solution.py:321
  28.1 52.9 %collective-permute-start.2 = (bf16[896,1024]{1,0:T(8,128)(2,1)S(1)}, bf16[896,1024]{1,0:T(8,128)(2,1)}, u32[]{:S(2)}, u32[]{:S(2)}) collective-permute-start(bf16[896,1024]{1,0:T(8,128)(2,1)S(1)} %pack.1.ups_ref.own_ups), channel_id=1, source_target_pairs={{0,4},{4,8},{8,12},{12,0},{1,5},{5,9},{9,13},{13,1},{2,6},{6,10},{... | collective-permute-start | bytes 5505032 | tf_op jit(solution)/shard_map/ppermute | solution.py:321
  30.1 46.1 %collective-permute-start.5 = (bf16[448,1024]{1,0:T(8,128)(2,1)}, bf16[448,1024]{1,0:T(8,128)(2,1)}, u32[]{:S(2)}, u32[]{:S(2)}) collective-permute-start(bf16[448,1024]{1,0:T(8,128)(2,1)} %bitcast.8.down_ref), channel_id=1, source_target_pairs={{0,12},{4,0},{8,4},{12,8},{1,13},{5,1},{9,5},{13,9},{2,14},{6,2},{... | collective-permute-start | bytes 2752520 | tf_op jit(solution)/shard_map/ppermute | solution.py:324
  34.6 46.4 %collective-permute-start.4 = (bf16[448,1024]{1,0:T(8,128)(2,1)S(1)}, bf16[448,1024]{1,0:T(8,128)(2,1)}, u32[]{:S(2)}, u32[]{:S(2)}) collective-permute-start(bf16[448,1024]{1,0:T(8,128)(2,1)S(1)} %bitcast.25), channel_id=1, source_target_pairs={{0,12},{4,0},{8,4},{12,8},{1,13},{5,1},{9,5},{13,9},{2,14},{6,2},{... | collective-permute-start | bytes 2752520 | tf_op jit(solution)/shard_map/ppermute | solution.py:324
  38.0 43.0 %collective-permute-start.7 = (bf16[448,1024]{1,0:T(8,128)(2,1)}, bf16[448,1024]{1,0:T(8,128)(2,1)}, u32[]{:S(2)}, u32[]{:S(2)}) collective-permute-start(bf16[448,1024]{1,0:T(8,128)(2,1)} %collective-permute-done.3.refs_3_), channel_id=1, source_target_pairs={{0,12},{4,0},{8,4},{12,8},{1,13},{5,1},{9,5},{13,9},{2,14},{6,2},{... | collective-permute-start | bytes 2752520 | tf_op jit(solution)/shard_map/ppermute | solution.py:324
  40.6 40.5 %collective-permute-start.6 = (bf16[448,1024]{1,0:T(8,128)(2,1)}, bf16[448,1024]{1,0:T(8,128)(2,1)}, u32[]{:S(2)}, u32[]{:S(2)}) collective-permute-start(bf16[448,1024]{1,0:T(8,128)(2,1)} %collective-permute-done.1.refs_1_), channel_id=1, source_target_pairs={{0,4},{4,8},{8,12},{12,0},{1,5},{5,9},{9,13},{13,1},{2,6},{6,10},{... | collective-permute-start | bytes 2752520 | tf_op jit(solution)/shard_map/ppermute | solution.py:321
  70.2 16.7 %all-to-all-start.1 = ((bf16[4,128,896]{2,1,0:T(8,128)(2,1)}), bf16[4,128,896]{2,1,0:T(8,128)(2,1)}, u32[]{:S(2)}, u32[]{:S(2)}) async-start(bf16[4,128,896]{2,1,0:T(8,128)(2,1)} %bitcast.10.recv_ref.rows_ref), calls=%async_computation.1 | async-start | bytes 1835008 | tf_op jit(solution)/shard_map/all_to_all | solution.py:275
  76.2 10.7 %collective-permute-start = (s16[128,1152]{1,0:T(8,128)(2,1)S(1)}, s16[128,1152]{1,0:T(8,128)(2,1)S(1)}, u32[]{:S(2)}, u32[]{:S(2)}) collective-permute-start(s16[128,1152]{1,0:T(8,128)(2,1)S(1)} %far_products.1), channel_id=1, source_target_pairs={{0,8},{4,12},{8,0},{12,4},{1,9},{5,13},{9,1},{13,5},{2,10},{6,14},... | collective-permute-start | bytes 884744 | tf_op jit(solution)/shard_map/ppermute | solution.py:360
  128.2 40.1 %all-to-all-start.5 = ((bf16[32,8,896]{2,1,0:T(8,128)(2,1)}), bf16[32,8,896]{2,1,0:T(8,128)(2,1)S(1)}, u32[]{:S(2)}, u32[]{:S(2)}) async-start(bf16[32,8,896]{2,1,0:T(8,128)(2,1)} %bitcast.14), calls=%async_computation.5 | async-start | bytes 917504 | tf_op jit(solution)/shard_map/all_to_all | solution.py:388
  137.5 11.7 %collective-permute-start.10 = (bf16[128,2048]{1,0:T(8,128)(2,1)S(1)}, bf16[128,2048]{1,0:T(8,128)(2,1)S(1)}, u32[]{:S(2)}, u32[]{:S(2)}) collective-permute-start(bf16[128,2048]{1,0:T(8,128)(2,1)S(1)} %bitcast.19), channel_id=1, source_target_pairs={{0,8},{4,12},{8,0},{12,4},{1,9},{5,13},{9,1},{13,5},{2,10},{6,14},... | collective-permute-start | bytes 1572872 | tf_op jit(solution)/shard_map/ppermute | solution.py:396
  140.0 13.4 %collective-permute-start.9 = (bf16[128,2048]{1,0:T(8,128)(2,1)S(1)}, bf16[128,2048]{1,0:T(8,128)(2,1)S(1)}, u32[]{:S(2)}, u32[]{:S(2)}) collective-permute-start(bf16[128,2048]{1,0:T(8,128)(2,1)S(1)} %bitcast.20), channel_id=1, source_target_pairs={{0,12},{4,0},{8,4},{12,8},{1,13},{5,1},{9,5},{13,9},{2,14},{6,2},{... | collective-permute-start | bytes 1572872 | tf_op jit(solution)/shard_map/ppermute | solution.py:396
  144.0 11.4 %collective-permute-start.8 = (bf16[128,2048]{1,0:T(8,128)(2,1)S(1)}, bf16[128,2048]{1,0:T(8,128)(2,1)S(1)}, u32[]{:S(2)}, u32[]{:S(2)}) collective-permute-start(bf16[128,2048]{1,0:T(8,128)(2,1)S(1)} %bitcast.21), channel_id=1, source_target_pairs={{0,4},{4,8},{8,12},{12,0},{1,5},{5,9},{9,13},{13,1},{2,6},{6,10},{... | collective-permute-start | bytes 1572872 | tf_op jit(solution)/shard_map/ppermute | solution.py:396
  158.8 9.5 %copy-start.1 = (bf16[2,256,256]{2,1,0:T(8,128)(2,1)S(1)}, bf16[2,256,256]{2,1,0:T(8,128)(2,1)}, u32[]{:S(2)}) copy-start(bf16[2,256,256]{2,1,0:T(8,128)(2,1)} %get-tuple-element.18.member_ref) | copy-start | bytes 786436
